TPU v7x, 32 devices: a whole 2x2x4 slice. The times are simulated.
32 devices in a mesh: ctx: 8 (over z, x), fft: 4 (over y, core).
Axes of the slice: x: 2, y: 2, z: 4, core: 2. Of those that a mesh axis runs over, the one named last changes fastest.
Arguments:
- tokens: bfloat16 [4096, 2048], P('ctx'), may hold values from -6 to 6
- w_in: bfloat16 [2048, 3, 2048], P(None, None, 'fft'), may hold values from -0.125 to 0.125
- short_taps: float32 [7, 384], replicated, may hold values from -2 to 2
- long_filter: float32 [4096, 128], P('ctx'), may hold values from -0.09375 to 0.09375
- skip_gain: float32 [2048], replicated, may hold values from -4 to 4
- w_out: bfloat16 [2048, 2048], P('fft'), may hold values from -0.125 to 0.125
Outputs:
- mixed: bfloat16 [4096, 2048], P(('ctx', 'fft'))
All inputs are finite; a program needn't handle non-finite values.
Results may differ from a plain program's by a relative error of at most 0.014.
Values may be sent and summed in bfloat16 or wider, within the bound.
No kernel may reach another device: no remote copies, remote signals or barrier semaphores. Data moves between devices by JAX's collectives and lax.ppermute only.
A program may use at most 128 MiB of HBM per device.

v0:
```python
import functools

import jax
import jax.numpy as jnp
from jax import lax
from jax.experimental import pallas as pl
from jax.experimental.pallas import tpu as pltpu
from jax.sharding import PartitionSpec as P

MIB = 1 << 20
LANES = 128
RIM = 16
LAG = 256


def passed_along(block, axis, distance):
    devices = range(lax.axis_size(axis))
    route = [(i - distance, i) for i in devices if i - distance in devices]
    return lax.ppermute(block, axis, route)


def swapped(block, mask):
    return lax.ppermute(block, "fft", [(i, i ^ mask) for i in range(lax.axis_size("fft"))])


def project_kernel(streams, group_size, parts, rim, tokens, taps, weights, out, ext, wbuf, proj, coefs, sems):
    n_tok = tokens.shape[0]
    width = wbuf.shape[3]
    n_blocks = wbuf.shape[1]
    n_taps = taps.shape[1]
    first = pltpu.make_async_copy(rim, ext.at[pl.ds(0, RIM)], sems.at[0])
    main = pltpu.make_async_copy(tokens, ext.at[pl.ds(RIM, n_tok)], sems.at[1])
    first.start()
    main.start()
    loads = {}
    for blk in range(n_blocks):
        for k, stream in enumerate(streams):
            copy = pltpu.make_async_copy(
                weights.at[stream, :, pl.ds(blk * width, width)], wbuf.at[k, blk], sems.at[2 + blk * len(streams) + k]
            )
            copy.start()
            loads[blk, k] = copy
    n_groups = taps.shape[2]
    n_chan = n_groups * group_size
    spread = (
        lax.broadcasted_iota(jnp.int32, (n_groups, n_chan), 0)
        == lax.broadcasted_iota(jnp.int32, (n_groups, n_chan), 1) // group_size
    ).astype(jnp.float32)
    for k, stream in enumerate(streams):
        coefs[k] = jnp.dot(
            taps[stream], spread, precision=lax.Precision.HIGHEST, preferred_element_type=jnp.float32
        )
    first.wait()
    main.wait()
    chunk = min(128, n_tok)
    for blk in range(n_blocks):
        for k in range(len(streams)):
            loads[blk, k].wait()
            full = jnp.dot(ext[...], wbuf[k, blk], preferred_element_type=jnp.float32)
            full = full.astype(jnp.bfloat16).astype(jnp.float32)
            for tile in range(width // LANES):
                proj[k, tile] = full[:, tile * LANES : (tile + 1) * LANES]
        for tile in range(width // LANES):
            chan = blk * width + tile * LANES
            for row in range(0, n_tok, chunk):
                made = None
                for k in range(len(streams)):
                    feat = None
                    for j in range(n_taps):
                        term = coefs[k, j : j + 1, chan : chan + LANES] * proj[k, tile, pl.ds(RIM + row - j, chunk), :]
                        feat = term if feat is None else feat + term
                    feat = feat.astype(jnp.bfloat16).astype(jnp.float32)
                    made = feat if made is None else made * feat
                turned = made.T.astype(jnp.bfloat16)
                if parts == 1:
                    out[chan : chan + LANES, row : row + chunk] = turned
                else:
                    span = n_tok // parts
                    for at in range(0, chunk, span):
                        out[(row + at) // span, chan : chan + LANES, :] = turned[:, at : at + span]


def project(streams, group_size, parts, rim, tokens, taps, weights):
    n_tok, depth = tokens.shape
    block = weights.shape[2]
    width = min(256, block)
    n_streams = len(streams)
    shape = (block, n_tok) if parts == 1 else (parts, block, n_tok // parts)
    any_spec = pl.BlockSpec(memory_space=pl.ANY)
    vmem = pl.BlockSpec(memory_space=pltpu.VMEM)
    flops = 2 * n_tok * depth * block * n_streams
    return pl.pallas_call(
        functools.partial(project_kernel, streams, group_size, parts),
        out_shape=jax.ShapeDtypeStruct(shape, jnp.bfloat16),
        in_specs=[any_spec, any_spec, vmem, any_spec],
        out_specs=vmem,
        scratch_shapes=[
            pltpu.VMEM((RIM + n_tok, depth), jnp.bfloat16),
            pltpu.VMEM((n_streams, block // width, depth, width), jnp.bfloat16),
            pltpu.VMEM((n_streams, width // LANES, RIM + n_tok, LANES), jnp.float32),
            pltpu.VMEM((n_streams, taps.shape[1], block), jnp.float32),
            pltpu.SemaphoreType.DMA((2 + n_streams * (block // width),)),
        ],
        compiler_params=pltpu.CompilerParams(vmem_limit_bytes=24 * MIB),
        cost_estimate=pl.CostEstimate(
            flops=flops, bytes_accessed=2 * (n_tok * depth + depth * block * n_streams), transcendentals=0
        ),
    )(rim, tokens, taps, weights)


def lags_kernel(filt, out):
    n_src, n_groups, cols = filt.shape
    length = n_src * cols
    zeros = jnp.zeros((1, LANES), jnp.float32)
    for g in range(n_groups):
        row = [zeros] + [filt[s, g : g + 1, :].astype(jnp.float32) for s in range(n_src)] + [zeros]
        row = jnp.concatenate(row, axis=1)
        wide = jnp.broadcast_to(row, (LANES, length + 2 * LANES))
        turned = pltpu.roll(wide, 0, 1, stride=1, stride_axis=0)
        out[g] = turned[:, : length + LANES].astype(jnp.bfloat16)


def lag_table(filt):
    n_src, n_groups, cols = filt.shape
    length = n_src * cols
    return pl.pallas_call(
        lags_kernel,
        out_shape=jax.ShapeDtypeStruct((n_groups, LANES, length + LANES), jnp.bfloat16),
        in_specs=[pl.BlockSpec(memory_space=pltpu.VMEM)],
        out_specs=pl.BlockSpec(memory_space=pltpu.VMEM),
        compiler_params=pltpu.CompilerParams(vmem_limit_bytes=40 * MIB),
        cost_estimate=pl.CostEstimate(
            flops=4 * n_groups * LANES * length, bytes_accessed=2 * n_groups * LANES * length, transcendentals=0
        ),
    )(filt)


def convolve_kernel(span, rows, mixed, lags, gain, out, held, total):
    n_src, n_chan, cols = mixed.shape
    n_blocks = n_src * cols // LAG
    per_src = cols // LAG
    n_fft, n_ctx, _, piece = out.shape
    pieces = LAG // piece
    size = n_blocks * rows
    static = n_blocks <= 16
    lead = 0 if static else size

    def lag_block(g, d):
        if static:
            at = d * LAG
            return jnp.concatenate([lags[g, :, at + LANES : at + LANES + LAG], lags[g, :, at : at + LAG]], axis=0)
        at = pl.multiple_of(d * LAG, LAG)
        near = lags[g, :, pl.ds(pl.multiple_of(at + LANES, LANES), LAG)]
        return jnp.concatenate([near, lags[g, :, pl.ds(at, LAG)]], axis=0)

    for g in range(n_chan // span):
        chans = slice(g * span, (g + 1) * span)
        if rows != span or lead:
            held[...] = jnp.zeros_like(held)
        for i in range(n_blocks):
            block = mixed[i // per_src, chans, (i % per_src) * LAG : (i % per_src + 1) * LAG]
            held[lead + i * rows : lead + i * rows + span, :] = block
        if static:
            total[...] = jnp.dot(held[...], lag_block(g, 0), preferred_element_type=jnp.float32)
            for d in range(1, n_blocks):
                part = jnp.dot(held[: size - d * rows, :], lag_block(g, d), preferred_element_type=jnp.float32)
                total[d * rows :, :] += part
        else:
            total[...] = jnp.zeros_like(total)

            @pl.loop(0, n_blocks)
            def _(d):
                shifted = held[pl.ds(pl.multiple_of(size - d * rows, rows), size), :]
                total[...] += jnp.dot(shifted, lag_block(g, d), preferred_element_type=jnp.float32)

        for i in range(n_blocks):
            direct = gain[chans, :] * held[lead + i * rows : lead + i * rows + span, :].astype(jnp.float32)
            both = (total[i * rows : i * rows + span, :] + direct).astype(jnp.bfloat16)
            for h in range(pieces):
                at = i * pieces + h
                out[at % n_fft, at // n_fft, chans, :] = both[:, h * piece : (h + 1) * piece]


def convolve(span, mixed, lags, gain, n_fft):
    n_src, n_chan, cols = mixed.shape
    n_blocks = n_src * cols // LAG
    rows = max(span, 16)
    size = n_blocks * rows
    held = size if n_blocks <= 16 else 2 * size
    vmem = pl.BlockSpec(memory_space=pltpu.VMEM)
    return pl.pallas_call(
        functools.partial(convolve_kernel, span, rows),
        out_shape=jax.ShapeDtypeStruct((n_fft, n_src, n_chan, cols // n_fft), jnp.bfloat16),
        in_specs=[vmem, vmem, vmem],
        out_specs=vmem,
        scratch_shapes=[pltpu.VMEM((held, LAG), jnp.bfloat16), pltpu.VMEM((size, LAG), jnp.float32)],
        compiler_params=pltpu.CompilerParams(vmem_limit_bytes=40 * MIB),
        cost_estimate=pl.CostEstimate(
            flops=n_chan * (n_src * cols) ** 2, bytes_accessed=2 * lags.size + 4 * mixed.size, transcendentals=0
        ),
    )(mixed, lags, gain)


def finish_kernel(place, query, conv, w0, w1, w2, w3, out, gated):
    n_fft, block, n_tok = query.shape
    for j in range(n_fft):
        product = query[j].astype(jnp.float32) * conv[j].astype(jnp.float32)
        gated[j] = product.T.astype(jnp.bfloat16)
    mine = place[0]
    width = out.shape[1]
    step = min(512, width)
    for col in range(0, width, step):
        acc = None
        for mask, w in enumerate((w0, w1, w2, w3)):
            part = jnp.dot(gated[mine ^ mask], w[:, col : col + step], preferred_element_type=jnp.float32)
            acc = part if acc is None else acc + part
        out[:, col : col + step] = acc.astype(jnp.bfloat16)


def finish(place, query, conv, weights):
    n_fft, block, n_tok = query.shape
    width = weights[0].shape[1]
    vmem = pl.BlockSpec(memory_space=pltpu.VMEM)
    return pl.pallas_call(
        finish_kernel,
        out_shape=jax.ShapeDtypeStruct((n_tok, width), jnp.bfloat16),
        in_specs=[pl.BlockSpec(memory_space=pltpu.SMEM)] + [vmem] * 6,
        out_specs=vmem,
        scratch_shapes=[pltpu.VMEM((n_fft, n_tok, block), jnp.bfloat16)],
        compiler_params=pltpu.CompilerParams(vmem_limit_bytes=24 * MIB),
        cost_estimate=pl.CostEstimate(
            flops=2 * n_fft * block * n_tok * width, bytes_accessed=2 * n_fft * block * width, transcendentals=0
        ),
    )(place, query, conv, *weights)


def body(tokens, w_in, short_taps, long_filter, skip_gain, w_out):
    n_ctx = lax.axis_size("ctx")
    n_fft = lax.axis_size("fft")
    tok_len, width = tokens.shape
    block = w_in.shape[2]
    n_groups = long_filter.shape[1]
    group_size = width // n_groups
    n_taps = short_taps.shape[0]
    ctx_index = lax.axis_index("ctx")
    fft_index = lax.axis_index("fft")
    stretch = block // n_ctx
    span = min(stretch, group_size)
    spans = stretch // span

    rim = passed_along(tokens[tok_len - RIM :], "ctx", 1)
    local_groups = block // group_size
    taps = lax.dynamic_slice_in_dim(
        short_taps.reshape(n_taps, 3, n_groups), fft_index * local_groups, local_groups, 2
    ).transpose(1, 0, 2)
    weights = w_in.transpose(1, 0, 2)
    mixed = project((1, 2), group_size, 1, rim, tokens, taps, weights)
    mixed = lax.all_to_all(mixed.reshape(n_ctx, stretch, tok_len), "ctx", 0, 0, tiled=True)

    local = lax.dynamic_slice_in_dim(long_filter, fft_index * local_groups, local_groups, 1).T
    local = jnp.repeat(local.astype(jnp.bfloat16), group_size // span, axis=0)
    filt = lax.all_to_all(local.reshape(n_ctx, spans, tok_len), "ctx", 0, 0, tiled=True)
    lags = lag_table(filt)

    query = project((0,), group_size, n_fft, rim, tokens, taps, weights)
    query = lax.all_to_all(query, "fft", 0, 0, tiled=True)

    gain = lax.dynamic_slice_in_dim(skip_gain, fft_index * block + ctx_index * stretch, stretch, 0)
    conv = convolve(span, mixed, lags, gain[:, None], n_fft)
    conv = lax.all_to_all(
        conv.reshape(n_fft * n_ctx, stretch, tok_len // n_fft), ("fft", "ctx"), 0, 0, tiled=True
    ).reshape(n_fft, block, tok_len // n_fft)

    beside = swapped(w_out, 1)
    across = swapped(w_out, 2)
    corner = swapped(across, 1)
    return finish(fft_index[None], query, conv, (w_out, beside, across, corner))


def solution(mesh):
    return jax.shard_map(
        body,
        mesh=mesh,
        in_specs=(P("ctx", None), P(None, None, "fft"), P(), P("ctx", None), P(), P("fft", None)),
        out_specs=P(("ctx", "fft"), None),
        check_vma=False,
    )
```

profile of v0, /device:TPU:0, one launch (start us, length us, event | category | flops | bytes accessed | tf_op | source)
XLA Modules:
  0.0 94.9 jit_solution(7384684834416853568)
XLA Ops:
  0.0 0.0 copy-start
  0.0 3.0 %collective-permute-start.2 = (bf16[512,2048]{1,0:T(8,128)(2,1)}, bf16[512,2048]{1,0:T(8,128)(2,1)}, u32[]{:S(2)}, u32[]{:S(2)}) collective-permute-start(bf16[512,2048]{1,0:T(8,128)(2,1)} %w0.1), channel_id=1, source_target_pairs={{0,2},{1,3},{2,0},{3,1},{4,6},{5,7},{6,4},{7,5},{8,10},{9,11},{10,... | collective-permute-start | bytes 6291464 | tf_op jit(solution)/shard_map/ppermute | solution.py:23
  3.0 0.8 slice.3
  3.8 3.4 %collective-permute-start = (bf16[16,2048]{1,0:T(8,128)(2,1)S(1)}, bf16[16,2048]{1,0:T(8,128)(2,1)S(1)}, u32[]{:S(2)}, u32[]{:S(2)}) collective-permute-start(bf16[16,2048]{1,0:T(8,128)(2,1)S(1)} %slice.3), channel_id=1, source_target_pairs={{0,4},{4,8},{8,12},{12,16},{16,20},{20,24},{24,28},{1,5},{5,9},{9,... | collective-permute-start | bytes 196616 | tf_op jit(solution)/shard_map/ppermute | solution.py:19
  7.2 0.0 copy-done
  7.2 0.1 fusion
  7.3 0.1 copy.7
  7.4 0.6 reshape_reshape_broadcast_in_dim.3
  8.1 4.9 %all-to-all-start.2 = ((bf16[8,4,512]{2,1,0:T(4,128)(2,1)}), bf16[8,4,512]{2,1,0:T(4,128)(2,1)S(1)}, u32[]{:S(2)}, u32[]{:S(2)}) async-start(bf16[8,4,512]{2,1,0:T(4,128)(2,1)} %reshape_reshape_broadcast_in_dim.3), calls=%async_computation.2 | async-start | bytes 65536 | tf_op jit(solution)/shard_map/all_to_all | solution.py:262
  12.9 0.8 dynamic-slice_bitcast_fusion.taps
  13.7 0.0 collective-permute-done.rim
  13.7 0.0 copy-start.1
  13.7 2.8 %copy-done.1 = bf16[2048,3,512]{2,0,1:T(8,128)(2,1)S(1)} copy-done((bf16[2048,3,512]{2,0,1:T(8,128)(2,1)S(1)}, bf16[2048,3,512]{2,0,1:T(8,128)(2,1)}, u32[]{:S(2)}) %copy-start.1) | copy-done | bytes 6291480
  16.5 0.0 copy-start.3
  16.5 1.6 %copy-done.3 = bf16[512,2048]{1,0:T(8,128)(2,1)S(1)} copy-done((bf16[512,2048]{1,0:T(8,128)(2,1)S(1)}, bf16[512,2048]{1,0:T(8,128)(2,1)}, u32[]{:S(2)}) %copy-start.3) | copy-done | bytes 2097176
  18.1 0.0 copy-start.4
  18.1 7.5 %shard_map.65 = bf16[512,512]{1,0:T(8,128)(2,1)} custom-call(bf16[16,2048]{1,0:T(8,128)(2,1)S(1)} %collective-permute-done.rim, bf16[512,2048]{1,0:T(8,128)(2,1)S(1)} %copy-done.3, f32[3,7,32]{2,1,0:T(8,128)S(1)} %dynamic-slice_bitcast_fusion.taps, bf16[3,2048,512]{2,1,0:T(8,128)(2,1)S(1)} %bitcast.12), custom_call_target="tpu_custom_call" | custom-call | flops 2147483648 | bytes 6291456 | tf_op jit(solution)/shard_map/pallas_call | solution.py:92
  25.6 0.0 all-to-all-done.2.filt
  25.7 6.0 %all-to-all-start.1 = ((bf16[8,64,512]{2,1,0:T(8,128)(2,1)}), bf16[8,64,512]{2,1,0:T(8,128)(2,1)S(1)}, u32[]{:S(2)}, u32[]{:S(2)}) async-start(bf16[8,64,512]{2,1,0:T(8,128)(2,1)} %bitcast.4), calls=%async_computation.1 | async-start | bytes 1048576 | tf_op jit(solution)/shard_map/all_to_all | solution.py:258
  31.7 0.0 collective-permute-start.1
  31.7 17.2 %collective-permute-done.2.w2 = bf16[512,2048]{1,0:T(8,128)(2,1)} collective-permute-done((bf16[512,2048]{1,0:T(8,128)(2,1)}, bf16[512,2048]{1,0:T(8,128)(2,1)}, u32[]{:S(2)}, u32[]{:S(2)}) %collective-permute-start.2) | collective-permute-done | bytes 2097184 | tf_op jit(solution)/shard_map/ppermute | solution.py:23
  48.9 0.0 collective-permute-start.3
  48.9 0.0 copy-done.4
  48.9 0.0 copy-start.2
  48.9 2.8 %copy-done.2 = bf16[2048,3,512]{2,0,1:T(8,128)(2,1)S(1)} copy-done((bf16[2048,3,512]{2,0,1:T(8,128)(2,1)S(1)}, bf16[2048,3,512]{2,0,1:T(8,128)(2,1)}, u32[]{:S(2)}) %copy-start.2) | copy-done | bytes 6291480
  51.7 4.3 %shard_map.64 = bf16[4,512,128]{2,1,0:T(8,128)(2,1)} custom-call(bf16[16,2048]{1,0:T(8,128)(2,1)S(1)} %collective-permute-done.rim, bf16[512,2048]{1,0:T(8,128)(2,1)S(1)} %copy-done.4, f32[3,7,32]{2,1,0:T(8,128)S(1)} %dynamic-slice_bitcast_fusion.taps, bf16[3,2048,512]{2,1,0:T(8,128)(2,1)S(1)} %bitcast.13), custom_call_target="tpu_custom_call" | custom-call | flops 1073741824 | bytes 4194304 | tf_op jit(solution)/shard_map/pallas_call | solution.py:92
  56.0 0.0 all-to-all-done.1.mixed
  56.0 3.5 %all-to-all-start = ((bf16[4,512,128]{2,1,0:T(8,128)(2,1)}), bf16[4,512,128]{2,1,0:T(8,128)(2,1)S(1)}, u32[]{:S(2)}, u32[]{:S(2)}) async-start(bf16[4,512,128]{2,1,0:T(8,128)(2,1)} %shard_map.64), calls=%async_computation | async-start | bytes 1048576 | tf_op jit(solution)/shard_map/all_to_all | solution.py:266
  59.5 0.8 dynamic-slice_bitcast_fusion.1
  60.3 0.1 copy.8.gain
  60.4 1.2 %shard_map.66.lags = bf16[4,128,4224]{2,1,0:T(8,128)(2,1)S(1)} custom-call(bf16[8,4,512]{2,1,0:T(4,128)(2,1)S(1)} %all-to-all-done.2.filt), custom_call_target="tpu_custom_call" | custom-call | flops 8388608 | bytes 4194304 | tf_op jit(solution)/shard_map/pallas_call | solution.py:126
  61.6 0.0 copy-start.5
  61.6 1.6 %shard_map.67 = bf16[4,8,64,128]{3,2,1,0:T(8,128)(2,1)S(1)} custom-call(bf16[8,64,512]{2,1,0:T(8,128)(2,1)S(1)} %all-to-all-done.1.mixed, bf16[4,128,4224]{2,1,0:T(8,128)(2,1)S(1)} %shard_map.66.lags, f32[64,1]{1,0:T(8,128)S(1)} %copy.8.gain), custom_call_target="tpu_custom_call" | custom-call | flops 1073741824 | bytes 5373952 | tf_op jit(solution)/shard_map/pallas_call | solution.py:191
  63.2 0.0 copy-start.6
  63.2 0.8 copy-done.6
  64.0 4.4 %all-to-all-done.query = bf16[4,512,128]{2,1,0:T(8,128)(2,1)S(1)} async-done(((bf16[4,512,128]{2,1,0:T(8,128)(2,1)}), bf16[4,512,128]{2,1,0:T(8,128)(2,1)S(1)}, u32[]{:S(2)}, u32[]{:S(2)}) %all-to-all-start) | async-done | bytes 524320 | tf_op jit(solution)/shard_map/all_to_all | solution.py:266
  68.4 21.4 %all_to_all.20 = bf16[32,64,128]{2,1,0:T(8,128)(2,1)S(1)} all-to-all(bf16[32,64,128]{2,1,0:T(8,128)(2,1)} %bitcast.15), channel_id=1, replica_groups=mesh['ctx'=8,'fft'=4] {'fft','ctx'}, dimensions={0} | all-to-all | bytes 1048576 | tf_op jit(solution)/shard_map/all_to_all | solution.py:270
  89.8 0.0 collective-permute-done.1.w1
  89.8 0.0 collective-permute-done.3.w3
  89.8 0.0 copy-done.5
  89.8 5.1 %shard_map.68 = bf16[128,2048]{1,0:T(8,128)(2,1)} custom-call(s32[1]{0:T(128)} %bitcast.place, bf16[4,512,128]{2,1,0:T(8,128)(2,1)S(1)} %all-to-all-done.query, bf16[4,512,128]{2,1,0:T(8,128)(2,1)S(1)} %bitcast.14, bf16[512,2048]{1,0:T(8,128)(2,1)S(1)} %copy-done.5, bf16[512,2048]{1,0:T(8,128)(2,1)} %collective-permute-done.1.w1, ...), custom_call_target="tpu_custom_call" | custom-call | flops 1073741824 | bytes 8388608 | tf_op jit(solution)/shard_map/pallas_call | solution.py:224
Async XLA Ops:
  0.0 7.2 %copy-start = (f32[512,128]{1,0:T(8,128)S(1)}, f32[512,128]{1,0:T(8,128)}, u32[]{:S(2)}) copy-start(f32[512,128]{1,0:T(8,128)} %param.9) | copy-start | bytes 786436
  0.0 48.9 %collective-permute-start.2 = (bf16[512,2048]{1,0:T(8,128)(2,1)}, bf16[512,2048]{1,0:T(8,128)(2,1)}, u32[]{:S(2)}, u32[]{:S(2)}) collective-permute-start(bf16[512,2048]{1,0:T(8,128)(2,1)} %w0.1), channel_id=1, source_target_pairs={{0,2},{1,3},{2,0},{3,1},{4,6},{5,7},{6,4},{7,5},{8,10},{9,11},{10,... | collective-permute-start | bytes 6291464 | tf_op jit(solution)/shard_map/ppermute | solution.py:23
  3.8 9.9 %collective-permute-start = (bf16[16,2048]{1,0:T(8,128)(2,1)S(1)}, bf16[16,2048]{1,0:T(8,128)(2,1)S(1)}, u32[]{:S(2)}, u32[]{:S(2)}) collective-permute-start(bf16[16,2048]{1,0:T(8,128)(2,1)S(1)} %slice.3), channel_id=1, source_target_pairs={{0,4},{4,8},{8,12},{12,16},{16,20},{20,24},{24,28},{1,5},{5,9},{9,... | collective-permute-start | bytes 196616 | tf_op jit(solution)/shard_map/ppermute | solution.py:19
  8.1 17.6 %all-to-all-start.2 = ((bf16[8,4,512]{2,1,0:T(4,128)(2,1)}), bf16[8,4,512]{2,1,0:T(4,128)(2,1)S(1)}, u32[]{:S(2)}, u32[]{:S(2)}) async-start(bf16[8,4,512]{2,1,0:T(4,128)(2,1)} %reshape_reshape_broadcast_in_dim.3), calls=%async_computation.2 | async-start | bytes 65536 | tf_op jit(solution)/shard_map/all_to_all | solution.py:262
  13.7 2.8 %copy-start.1 = (bf16[2048,3,512]{2,0,1:T(8,128)(2,1)S(1)}, bf16[2048,3,512]{2,0,1:T(8,128)(2,1)}, u32[]{:S(2)}) copy-start(bf16[2048,3,512]{2,0,1:T(8,128)(2,1)} %param.7) | copy-start | bytes 18874372
  16.5 1.6 %copy-start.3 = (bf16[512,2048]{1,0:T(8,128)(2,1)S(1)}, bf16[512,2048]{1,0:T(8,128)(2,1)}, u32[]{:S(2)}) copy-start(bf16[512,2048]{1,0:T(8,128)(2,1)} %tokens.3) | copy-start | bytes 6291460
  18.1 30.8 %copy-start.4 = (bf16[512,2048]{1,0:T(8,128)(2,1)S(1)}, bf16[512,2048]{1,0:T(8,128)(2,1)}, u32[]{:S(2)}) copy-start(bf16[512,2048]{1,0:T(8,128)(2,1)} %tokens.3) | copy-start | bytes 6291460
  25.7 30.4 %all-to-all-start.1 = ((bf16[8,64,512]{2,1,0:T(8,128)(2,1)}), bf16[8,64,512]{2,1,0:T(8,128)(2,1)S(1)}, u32[]{:S(2)}, u32[]{:S(2)}) async-start(bf16[8,64,512]{2,1,0:T(8,128)(2,1)} %bitcast.4), calls=%async_computation.1 | async-start | bytes 1048576 | tf_op jit(solution)/shard_map/all_to_all | solution.py:258
  31.7 58.2 %collective-permute-start.1 = (bf16[512,2048]{1,0:T(8,128)(2,1)}, bf16[512,2048]{1,0:T(8,128)(2,1)}, u32[]{:S(2)}, u32[]{:S(2)}) collective-permute-start(bf16[512,2048]{1,0:T(8,128)(2,1)} %w0.1), channel_id=1, source_target_pairs={{0,1},{1,0},{2,3},{3,2},{4,5},{5,4},{6,7},{7,6},{8,9},{9,8},{10,11... | collective-permute-start | bytes 6291464 | tf_op jit(solution)/shard_map/ppermute | solution.py:23
  48.9 40.9 %collective-permute-start.3 = (bf16[512,2048]{1,0:T(8,128)(2,1)}, bf16[512,2048]{1,0:T(8,128)(2,1)}, u32[]{:S(2)}, u32[]{:S(2)}) collective-permute-start(bf16[512,2048]{1,0:T(8,128)(2,1)} %collective-permute-done.2.w2), channel_id=1, source_target_pairs={{0,1},{1,0},{2,3},{3,2},{4,5},{5,4},{6,7},{7,6},{8,9},{9,8},{10,11... | collective-permute-start | bytes 6291464 | tf_op jit(solution)/shard_map/ppermute | solution.py:23
  48.9 2.8 %copy-start.2 = (bf16[2048,3,512]{2,0,1:T(8,128)(2,1)S(1)}, bf16[2048,3,512]{2,0,1:T(8,128)(2,1)}, u32[]{:S(2)}) copy-start(bf16[2048,3,512]{2,0,1:T(8,128)(2,1)} %param.7) | copy-start | bytes 18874372
  56.0 12.4 %all-to-all-start = ((bf16[4,512,128]{2,1,0:T(8,128)(2,1)}), bf16[4,512,128]{2,1,0:T(8,128)(2,1)S(1)}, u32[]{:S(2)}, u32[]{:S(2)}) async-start(bf16[4,512,128]{2,1,0:T(8,128)(2,1)} %shard_map.64), calls=%async_computation | async-start | bytes 1048576 | tf_op jit(solution)/shard_map/all_to_all | solution.py:266
  61.6 28.3 %copy-start.5 = (bf16[512,2048]{1,0:T(8,128)(2,1)S(1)}, bf16[512,2048]{1,0:T(8,128)(2,1)}, u32[]{:S(2)}) copy-start(bf16[512,2048]{1,0:T(8,128)(2,1)} %w0.1) | copy-start | bytes 6291460
  63.2 0.8 copy-start.6
where the time goes:
time: 95.6 us; the launch traced here: 94.9 us
  waiting for transfers between devices  21.6 us (23%)
  blocking collectives  21.4 us (22%)
  starting transfers between devices  20.7 us (22%)
  Pallas kernels  19.8 us (21%)
  local copies, waits for them, and re-layouts  11.3 us (12%)
    all_to_all x1, blocking collectives, body(): lax.all_to_all(conv.reshape(n_fft * n_ctx, stretch, tok_len // n_fft), ('...  21.4 us
    ppermute x3, waiting for transfers between devices, swapped(): lax.ppermute(block, 'fft', [(i, i ^ mask) for i in range(lax.axis_size('f...  17.2 us
    pallas_call x2, Pallas kernels, project(): pl.pallas_call(functools.partial(project_kernel, streams, group_size, par...  11.9 us
    unnamed x14, local copies, waits for them, and re-layouts  7.99 us
    all_to_all x1, starting transfers between devices, body(): lax.all_to_all(mixed.reshape(n_ctx, stretch, tok_len), 'ctx', 0, 0, tiled...  6.01 us
    pallas_call x1, Pallas kernels, finish(): pl.pallas_call(finish_kernel, out_shape=jax.ShapeDtypeStruct((n_tok, widt...  5.11 us
    all_to_all x1, starting transfers between devices, body(): lax.all_to_all(local.reshape(n_ctx, spans, tok_len), 'ctx', 0, 0, tiled=T...  4.88 us
    all_to_all x1, waiting for transfers between devices, body(): query = lax.all_to_all(query, 'fft', 0, 0, tiled=True)  4.38 us
  transfers between devices with their start and end apart: 7, of which 2 were waited for; matrix products, arithmetic and copies ran while one was open for 3% of the time, Pallas kernels for 15%

commit v1 on v0

v1 whole, which is shorter than its diff:
```python
import functools

import jax
import jax.numpy as jnp
from jax import lax
from jax.experimental import pallas as pl
from jax.experimental.pallas import tpu as pltpu
from jax.sharding import PartitionSpec as P

MIB = 1 << 20
LANES = 128
RIM = 16
LAG = 256


def fft_index():
    return lax.axis_index("chip") * lax.axis_size("core") + lax.axis_index("core")


def passed_along(block, axis, distance):
    devices = range(lax.axis_size(axis))
    route = [(i - distance, i) for i in devices if i - distance in devices]
    return lax.ppermute(block, axis, route)


def swapped(block, axis):
    return lax.ppermute(block, axis, [(i, i ^ 1) for i in range(lax.axis_size(axis))])


def spread_taps(taps, group0, group_size):
    n_taps, n_groups = taps.shape
    rows = jnp.concatenate([taps, jnp.zeros((8 - n_taps, n_groups), jnp.float32)], axis=0)
    index = group0 + lax.broadcasted_iota(jnp.int32, (8, LANES), 1) // group_size
    return jnp.take_along_axis(rows, index, axis=1, mode="promise_in_bounds")


def filtered(coef, rows_of, n_taps):
    feat = None
    for j in range(n_taps):
        term = coef[j : j + 1, :] * rows_of(j)
        feat = term if feat is None else feat + term
    return feat.astype(jnp.bfloat16).astype(jnp.float32)


def mix_kernel(group_size, sizes, tokens, taps, weights, filt, out, ext, wbuf, proj, lag, turned_lag, sems):
    stretch, chan_rows = sizes
    n_tok = tokens.shape[0]
    n_ctx = out.shape[0]
    _, n_blocks, _, width = wbuf.shape
    n_taps, n_groups = taps.shape[0], taps.shape[1] // 3
    block = n_blocks * width
    group0 = fft_index() * (block // group_size)
    main = pltpu.make_async_copy(tokens, ext, sems.at[0])
    main.start()
    loads = {}
    for blk in range(n_blocks):
        for k in range(2):
            loads[blk, k] = pltpu.make_async_copy(
                weights.at[k + 1, :, pl.ds(blk * width, width)], wbuf.at[k, blk], sems.at[2 + blk * 2 + k]
            )
            loads[blk, k].start()
    lag_load = pltpu.make_async_copy(filt, lag, sems.at[1])
    lag_load.start()
    tiles = block // LANES
    for k in range(2):
        for tile in range(tiles):
            proj[k, tile, 0:RIM, :] = jnp.zeros((RIM, LANES), jnp.float32)
    main.wait()
    chunk = min(128, n_tok)
    for blk in range(n_blocks):
        for k in range(2):
            loads[blk, k].wait()
            full = jnp.dot(ext[...], wbuf[k, blk], preferred_element_type=jnp.float32)
            full = full.astype(jnp.bfloat16).astype(jnp.float32)
            for t in range(width // LANES):
                proj[k, blk * (width // LANES) + t, RIM:, :] = full[:, t * LANES : (t + 1) * LANES]
        for t in range(width // LANES):
            tile = blk * (width // LANES) + t
            coefs = [
                spread_taps(taps[:, s * n_groups : (s + 1) * n_groups], group0 + tile * (LANES // group_size), group_size)
                for s in (1, 2)
            ]
            for row in range(0, n_tok, chunk):
                key, value = [
                    filtered(coefs[k], lambda j: proj[k, tile, RIM + row - j : RIM + row - j + chunk, :], n_taps)
                    for k in range(2)
                ]
                flipped = (key * value).T.astype(jnp.bfloat16)
                for c in range(0, LANES, stretch):
                    out[(tile * LANES + c) // stretch, 0:stretch, row : row + chunk] = flipped[c : c + stretch, :]
    lag_load.wait()
    for at in range(0, n_tok, LANES):
        turned_lag[:, at : at + LANES] = lag[at : at + LANES, :].T
    for dest in range(n_ctx):
        tile = dest * stretch // LANES
        group8 = dest * stretch // group_size // 8 * 8
        lags = turned_lag[pl.ds(pl.multiple_of(group0 + group8, 8), 8), :]
        ends = []
        for k in range(2):
            ends += [proj[k, tile, RIM : RIM + 8, :], proj[k, tile, RIM + n_tok - 8 :, :]]
        if n_tok > 4 * LANES:
            ends.append(jnp.zeros((8, n_tok - 4 * LANES), jnp.float32))
        extra = jnp.concatenate([lags, jnp.concatenate(ends, axis=1)], axis=0)
        out[dest, chan_rows:, :] = extra.astype(jnp.bfloat16)


def mix(group_size, tokens, taps, weights, filt, n_ctx):
    n_tok, depth = tokens.shape
    block = weights.shape[2]
    width = min(256, block)
    stretch = block // n_ctx
    chan_rows = -(-stretch // 16) * 16
    hbm = pl.BlockSpec(memory_space=pltpu.HBM)
    vmem = pl.BlockSpec(memory_space=pltpu.VMEM)
    return pl.pallas_call(
        functools.partial(mix_kernel, group_size, (stretch, chan_rows)),
        out_shape=jax.ShapeDtypeStruct((n_ctx, chan_rows + 16, n_tok), jnp.bfloat16),
        in_specs=[hbm, vmem, hbm, hbm],
        out_specs=vmem,
        scratch_shapes=[
            pltpu.VMEM((n_tok, depth), jnp.bfloat16),
            pltpu.VMEM((2, block // width, depth, width), jnp.bfloat16),
            pltpu.VMEM((2, block // LANES, RIM + n_tok, LANES), jnp.float32),
            pltpu.VMEM(filt.shape, jnp.float32),
            pltpu.VMEM(filt.shape[::-1], jnp.float32),
            pltpu.SemaphoreType.DMA((2 + 2 * (block // width),)),
        ],
        compiler_params=pltpu.CompilerParams(vmem_limit_bytes=56 * MIB),
        cost_estimate=pl.CostEstimate(
            flops=4 * n_tok * depth * block, bytes_accessed=2 * (n_tok * depth + 2 * depth * block), transcendentals=0
        ),
        name="mix",
    )(tokens, taps, weights, filt)


def query_kernel(group_size, rim, tokens, taps, weights, mine, other, pieces, ext, wbuf, proj, sems):
    n_tok = tokens.shape[0]
    n_blocks, _, width = wbuf.shape
    n_taps, n_groups = taps.shape[0], taps.shape[1] // 3
    piece = pieces.shape[2]
    group0 = fft_index() * (n_blocks * width // group_size)
    first = pltpu.make_async_copy(rim, ext.at[pl.ds(0, RIM)], sems.at[0])
    main = pltpu.make_async_copy(tokens, ext.at[pl.ds(RIM, n_tok)], sems.at[1])
    first.start()
    main.start()
    loads = []
    for blk in range(n_blocks):
        loads.append(
            pltpu.make_async_copy(weights.at[0, :, pl.ds(blk * width, width)], wbuf.at[blk], sems.at[2 + blk])
        )
        loads[blk].start()
    first.wait()
    main.wait()
    for blk in range(n_blocks):
        loads[blk].wait()
        full = jnp.dot(ext[...], wbuf[blk], preferred_element_type=jnp.float32)
        full = full.astype(jnp.bfloat16).astype(jnp.float32)
        for t in range(width // LANES):
            tile = blk * (width // LANES) + t
            proj[tile] = full[:, t * LANES : (t + 1) * LANES]
            coef = spread_taps(taps[:, :n_groups], group0 + tile * (LANES // group_size), group_size)
            for row in range(0, n_tok, LANES):
                feat = filtered(coef, lambda j: proj[tile, RIM + row - j : RIM + row - j + LANES, :], n_taps)
                at = row % piece
                pieces[row // piece, tile * LANES : (tile + 1) * LANES, at : at + LANES] = feat.T.astype(jnp.bfloat16)
    chip = lax.axis_index("chip")
    mine[...] = pieces[chip]
    other[...] = pieces[chip ^ 1]


def make_query(group_size, rim, tokens, taps, weights, n_chips):
    n_tok, depth = tokens.shape
    block = weights.shape[2]
    width = min(256, block)
    hbm = pl.BlockSpec(memory_space=pltpu.HBM)
    vmem = pl.BlockSpec(memory_space=pltpu.VMEM)
    return pl.pallas_call(
        functools.partial(query_kernel, group_size),
        out_shape=[jax.ShapeDtypeStruct((block, n_tok // n_chips), jnp.bfloat16)] * 2,
        in_specs=[hbm, hbm, vmem, hbm],
        out_specs=[vmem, vmem],
        scratch_shapes=[
            pltpu.VMEM((n_chips, block, n_tok // n_chips), jnp.bfloat16),
            pltpu.VMEM((RIM + n_tok, depth), jnp.bfloat16),
            pltpu.VMEM((block // width, depth, width), jnp.bfloat16),
            pltpu.VMEM((block // LANES, RIM + n_tok, LANES), jnp.float32),
            pltpu.SemaphoreType.DMA((2 + block // width,)),
        ],
        compiler_params=pltpu.CompilerParams(vmem_limit_bytes=56 * MIB),
        cost_estimate=pl.CostEstimate(
            flops=2 * n_tok * depth * block, bytes_accessed=2 * (n_tok * depth + depth * block), transcendentals=0
        ),
        name="query",
    )(rim, tokens, taps, weights)


def convolve_kernel(group_size, sizes, payload, taps, gain, out, lags, fixed, lagrow, held, total):
    stretch, chan_rows, span, rows = sizes
    n_src, _, cols = payload.shape
    n_chips, n_ctx, _, piece = out.shape
    n_taps, n_groups = taps.shape[0], taps.shape[1] // 3
    n_blocks = n_src * cols // LAG
    per_src = cols // LAG
    pieces = LAG // piece
    size = n_blocks * rows
    length = n_src * cols
    static = n_blocks <= 16
    lead = 0 if static else size
    local = lax.axis_index("ctx") * stretch
    block = stretch * n_ctx

    group0 = (fft_index() * block + local // LANES * LANES) // group_size
    coefs = [
        spread_taps(taps[:, s * n_groups : (s + 1) * n_groups], group0, group_size) for s in (1, 2)
    ]
    first = []
    for s in range(n_src):
        made = None
        for k in range(2):
            head = payload[s, chan_rows + 8 : chan_rows + 16, 2 * k * LANES : (2 * k + 1) * LANES]
            if s == 0:
                tail = jnp.zeros((8, LANES), jnp.float32)
            else:
                tail = payload[s - 1, chan_rows + 8 : chan_rows + 16, (2 * k + 1) * LANES : (2 * k + 2) * LANES]
                tail = tail.astype(jnp.float32)
            both = jnp.concatenate([tail, head.astype(jnp.float32)], axis=0)
            feat = filtered(coefs[k], lambda j: both[8 - j : 16 - j, :], n_taps)
            made = feat if made is None else made * feat
        first.append(made)
    for s in range(0, n_src, 16):
        some = first[s : s + 16]
        if len(some) < 16:
            some = some + [jnp.zeros(((16 - len(some)) * 8, LANES), jnp.float32)]
        fixed[:, s * 8 : s * 8 + LANES] = jnp.concatenate(some, axis=0).T
    chan0 = local % LANES
    lane = lax.broadcasted_iota(jnp.int32, (span, LANES), 1)

    for s in range(n_src):
        lagrow[:, s * cols : (s + 1) * cols] = payload[s, chan_rows : chan_rows + 8, :].astype(jnp.float32)
    group_in = local // group_size % 8
    zeros = jnp.zeros((1, LANES), jnp.float32)

    def lag_block(d):
        if static:
            at = d * LAG
            return jnp.concatenate([lags[:, at + LANES : at + LANES + LAG], lags[:, at : at + LAG]], axis=0)
        at = pl.multiple_of(d * LAG, LAG)
        near = lags[:, pl.ds(pl.multiple_of(at + LANES, LANES), LAG)]
        return jnp.concatenate([near, lags[:, pl.ds(at, LAG)]], axis=0)

    for g in range(stretch // span):
        row = jnp.concatenate([zeros, lagrow[pl.ds(group_in + g, 1), :], zeros], axis=1)
        wide = jnp.broadcast_to(row, (LANES, length + 2 * LANES))
        turned = pltpu.roll(wide, 0, 1, stride=1, stride_axis=0)
        lags[...] = turned[:, : length + LANES].astype(jnp.bfloat16)
        chans = slice(g * span, (g + 1) * span)
        if rows != span or lead:
            held[...] = jnp.zeros_like(held)
        for i in range(n_blocks):
            s = i // per_src
            part = payload[s, chans, (i % per_src) * LAG : (i % per_src + 1) * LAG]
            at = lead + i * rows
            held[at : at + span, :] = part
            if i % per_src == 0:
                patch = fixed[pl.ds(pl.multiple_of(chan0 + g * span, 8), span), s // 16 * LANES : (s // 16 + 1) * LANES]
                if s % 16:
                    patch = pltpu.roll(patch, LANES - s % 16 * 8, 1)
                patched = jnp.where(lane < 8, patch, part[:, :LANES].astype(jnp.float32))
                held[at : at + span, :LANES] = patched.astype(jnp.bfloat16)
        if static:
            total[...] = jnp.dot(held[...], lag_block(0), preferred_element_type=jnp.float32)
            for d in range(1, n_blocks):
                part = jnp.dot(held[: size - d * rows, :], lag_block(d), preferred_element_type=jnp.float32)
                total[d * rows :, :] += part
        else:
            total[...] = jnp.zeros_like(total)

            @pl.loop(0, n_blocks)
            def _(d):
                shifted = held[pl.ds(pl.multiple_of(size - d * rows, rows), size), :]
                total[...] += jnp.dot(shifted, lag_block(d), preferred_element_type=jnp.float32)

        for i in range(n_blocks):
            at = lead + i * rows
            direct = gain[chans, :] * held[at : at + span, :].astype(jnp.float32)
            both = (total[i * rows : i * rows + span, :] + direct).astype(jnp.bfloat16)
            for h in range(pieces):
                at = i * pieces + h
                out[at % n_chips, at // n_chips, chans, :] = both[:, h * piece : (h + 1) * piece]


def convolve(group_size, span, stretch, payload, taps, gain, n_chips):
    n_src, all_rows, cols = payload.shape
    n_blocks = n_src * cols // LAG
    rows = max(span, 16)
    size = n_blocks * rows
    length = n_src * cols
    held = size if n_blocks <= 16 else 2 * size
    vmem = pl.BlockSpec(memory_space=pltpu.VMEM)
    return pl.pallas_call(
        functools.partial(convolve_kernel, group_size, (stretch, all_rows - 16, span, rows)),
        out_shape=jax.ShapeDtypeStruct((n_chips, n_src, stretch, cols // n_chips), jnp.bfloat16),
        in_specs=[vmem, vmem, vmem],
        out_specs=vmem,
        scratch_shapes=[
            pltpu.VMEM((LANES, length + LANES), jnp.bfloat16),
            pltpu.VMEM((LANES, -(-n_src // 16) * LANES), jnp.float32),
            pltpu.VMEM((8, length), jnp.float32),
            pltpu.VMEM((held, LAG), jnp.bfloat16),
            pltpu.VMEM((size, LAG), jnp.float32),
        ],
        compiler_params=pltpu.CompilerParams(vmem_limit_bytes=48 * MIB),
        cost_estimate=pl.CostEstimate(
            flops=stretch * length**2, bytes_accessed=4 * payload.size, transcendentals=0
        ),
        name="convolve",
    )(payload, taps, gain)


def output_kernel(other_core, q_near, q_far, conv, w_near, w_far, out, gated):
    n_tok = out.shape[0]

    @pl.when(pl.program_id(0) == 0)
    def _():
        chip = lax.axis_index("chip")
        core = lax.axis_index("core") ^ other_core
        for k, query in enumerate((q_near, q_far)):
            for c in range(0, query.shape[0], LANES):
                for t in range(0, n_tok, LANES):
                    at = pl.ds(pl.multiple_of(core * n_tok + t, LANES), LANES)
                    rows = pl.ds(c, LANES)
                    product = query[rows, at].astype(jnp.float32) * conv[chip ^ k, rows, at].astype(jnp.float32)
                    gated[k, t : t + LANES, c : c + LANES] = product.T.astype(jnp.bfloat16)

    acc = jnp.dot(gated[0], w_near[...], preferred_element_type=jnp.float32)
    acc += jnp.dot(gated[1], w_far[...], preferred_element_type=jnp.float32)
    out[...] = acc.astype(out.dtype)


def output_part(other_core, dtype, query, conv, weights):
    _, block, n_tok = conv.shape
    n_tok //= 2
    width = weights[0].shape[1]
    step = min(512, width)
    vmem = pl.BlockSpec(memory_space=pltpu.VMEM)
    columns = pl.BlockSpec((block, step), lambda n: (0, n))
    return pl.pallas_call(
        functools.partial(output_kernel, other_core),
        grid=(width // step,),
        out_shape=jax.ShapeDtypeStruct((n_tok, width), dtype),
        in_specs=[vmem] * 3 + [columns] * 2,
        out_specs=pl.BlockSpec((n_tok, step), lambda n: (0, n)),
        scratch_shapes=[pltpu.VMEM((2, n_tok, block), jnp.bfloat16)],
        compiler_params=pltpu.CompilerParams(vmem_limit_bytes=24 * MIB),
        cost_estimate=pl.CostEstimate(
            flops=4 * block * n_tok * width, bytes_accessed=4 * block * width, transcendentals=0
        ),
        name="output_part",
    )(*query, conv, *weights)


def body(tokens, w_in, short_taps, long_filter, skip_gain, w_out):
    n_ctx, n_chips, n_cores = (lax.axis_size(axis) for axis in ("ctx", "chip", "core"))
    tok_len, width = tokens.shape
    block = w_in.shape[2]
    group_size = width // long_filter.shape[1]
    stretch = block // n_ctx
    span = min(stretch, group_size)
    piece = tok_len // n_chips

    weights = w_in.transpose(1, 0, 2)
    across = swapped(w_out, "chip")
    sent = mix(group_size, tokens, short_taps, weights, long_filter, n_ctx)
    payload = lax.all_to_all(sent, "ctx", 0, 0, tiled=True)

    ends, _ = lax.optimization_barrier((tokens[tok_len - RIM :], sent))
    rim = passed_along(ends, "ctx", 1)
    near, far = make_query(group_size, rim, tokens, short_taps, weights, n_chips)
    near, far, conv_taps = lax.optimization_barrier((near, far, short_taps))

    gain = lax.dynamic_slice_in_dim(skip_gain, fft_index() * block + lax.axis_index("ctx") * stretch, stretch, 0)
    conv = convolve(group_size, span, stretch, payload, conv_taps, gain[:, None], n_chips)
    far, _ = lax.optimization_barrier((far, conv))
    query = (near, swapped(far, "chip"))
    conv = lax.all_to_all(conv.reshape(n_chips * n_ctx, stretch, piece), ("chip", "ctx"), 0, 0, tiled=True)
    conv = conv.reshape(n_chips, block, piece)

    beside = swapped(output_part(1, jnp.bfloat16, query, conv, (w_out, across)), "core")
    total = output_part(0, jnp.float32, query, conv, (w_out, across))
    return (total + beside.astype(jnp.float32)).astype(jnp.bfloat16)


def solution(mesh):
    n_ctx, n_fft = (mesh.shape[axis] for axis in ("ctx", "fft"))
    split = jax.sharding.Mesh(mesh.devices.reshape(n_ctx, n_fft // 2, 2), ("ctx", "chip", "core"))
    fft = ("chip", "core")
    return jax.shard_map(
        body,
        mesh=split,
        in_specs=(P("ctx", None), P(None, None, fft), P(), P("ctx", None), P(), P(fft, None)),
        out_specs=P(("ctx",) + fft, None),
        check_vma=False,
    )
```

time: 95.6 us -> 83.6 us (0.87)
  blocking collectives: 21.4 us -> 0 us
  local copies, waits for them, and re-layouts: 11.3 us -> 1.67 us
  starting transfers between devices: 20.7 us -> 27.1 us
  Pallas kernels: 19.8 us -> 26.2 us
  waiting for transfers between devices: 21.6 us -> 27 us
    all_to_all x1 -> x0, blocking collectives: 21.4 us -> none  [body(): lax.all_to_all(conv.reshape(n_fft * n_ctx, stretch, tok_len // n_fft), ('...]
    unnamed x14 -> x12, local copies, waits for them, and re-layouts: 7.99 us -> 0.65 us
    pallas_call x5, Pallas kernels: 19.8 us -> 26.2 us  [the longest x1 9.6 us: mix(): pl.pallas_call(functools.partial(mix_kernel, group_size, (stretch, chan_r...]
    ppermute x3, waiting for transfers between devices: 17.2 us -> 23.3 us  [swapped(): lax.ppermute(block, axis, [(i, i ^ 1) for i in range(lax.axis_size(axis))])]
    all_to_all x3 -> x2, starting transfers between devices: 14.4 us -> 19.6 us  [the longest x1 12.4 us: body(): lax.all_to_all(conv.reshape(n_chips * n_ctx, stretch, piece), ('chip', 'c...]
    all_to_all x3 -> x2, waiting for transfers between devices: 4.38 us -> 1.65 us  [the longest x1 1.64 us: body(): payload = lax.all_to_all(sent, 'ctx', 0, 0, tiled=True)]
    ppermute x1, waiting for transfers between devices: 0.01 us -> 2.05 us  [passed_along(): return lax.ppermute(block, axis, route)]
  transfers between devices with their start and end apart: 7 -> 6, of which waited for: 2 -> 3; matrix products, arithmetic and copies ran while one was open for 3% -> 1% of each run, Pallas kernels for 15% -> 16%
where the time goes in v1:
time: 83.6 us; the launch traced here: 83.1 us
  starting transfers between devices  27.1 us (32%)
  waiting for transfers between devices  27 us (32%)
  Pallas kernels  26.2 us (31%)
  local copies, waits for them, and re-layouts  1.67 us (2%)
  other arithmetic  0.9 us (1%)
    ppermute x3, waiting for transfers between devices, swapped(): lax.ppermute(block, axis, [(i, i ^ 1) for i in range(lax.axis_size(axis))])  23.3 us
    all_to_all x1, starting transfers between devices, body(): lax.all_to_all(conv.reshape(n_chips * n_ctx, stretch, piece), ('chip', 'c...  12.4 us
    pallas_call x1, Pallas kernels, mix(): pl.pallas_call(functools.partial(mix_kernel, group_size, (stretch, chan_r...  9.6 us
    all_to_all x1, starting transfers between devices, body(): payload = lax.all_to_all(sent, 'ctx', 0, 0, tiled=True)  7.27 us
    pallas_call x2, Pallas kernels, output_part(): pl.pallas_call(functools.partial(output_kernel, other_core), grid=(width...  6.79 us
    pallas_call x1, Pallas kernels, make_query(): pl.pallas_call(functools.partial(query_kernel, group_size), out_shape=[ja...  6.46 us
    ppermute x1, starting transfers between devices, passed_along(): return lax.ppermute(block, axis, route)  3.85 us
    ppermute x3, starting transfers between devices, swapped(): lax.ppermute(block, axis, [(i, i ^ 1) for i in range(lax.axis_size(axis))])  3.65 us
  transfers between devices with their start and end apart: 6, of which 3 were waited for; matrix products, arithmetic and copies ran while one was open for 1% of the time, Pallas kernels for 16%

profile of v1, /device:TPU:0, one launch (start us, length us, event | category | flops | bytes accessed | tf_op | source)
XLA Modules:
  0.0 83.1 jit_solution(344378142011945742)
XLA Ops:
  0.0 0.0 copy-start
  0.0 0.0 copy-start.1
  0.0 9.6 %mix.1 = bf16[8,80,512]{2,1,0:T(8,128)(2,1)} custom-call(bf16[512,2048]{1,0:T(8,128)(2,1)} %tokens.3, f32[7,384]{1,0:T(8,128)} %taps.4, bf16[3,2048,512]{2,1,0:T(8,128)(2,1)} %bitcast.7, f32[512,128]{1,0:T(8,128)} %filt.1), custom_call_target="tpu_custom_call" | custom-call | flops 2147483648 | bytes 6291456 | tf_op jit(solution)/shard_map/mix/pallas_call | solution.py:115
  9.6 7.3 %all-to-all-start = ((bf16[8,80,512]{2,1,0:T(8,128)(2,1)}), bf16[8,80,512]{2,1,0:T(8,128)(2,1)S(1)}, u32[]{:S(2)}, u32[]{:S(2)}) async-start(bf16[8,80,512]{2,1,0:T(8,128)(2,1)} %mix.1), calls=%async_computation | async-start | bytes 1310720 | tf_op jit(solution)/shard_map/all_to_all | solution.py:374
  16.9 0.0 copy-done.1
  16.9 1.6 %collective-permute-start.2 = (bf16[512,2048]{1,0:T(8,128)(2,1)S(1)}, bf16[512,2048]{1,0:T(8,128)(2,1)}, u32[]{:S(2)}, u32[]{:S(2)}) collective-permute-start(bf16[512,2048]{1,0:T(8,128)(2,1)S(1)} %copy-done.1), channel_id=1, source_target_pairs={{0,2},{2,0},{1,3},{3,1},{4,6},{6,4},{5,7},{7,5},{8,10},{10,8},{9,1... | collective-permute-start | bytes 6291464 | tf_op jit(solution)/shard_map/ppermute | solution.py:27
  18.5 0.8 %slice.3 = bf16[16,2048]{1,0:T(8,128)(2,1)S(1)} slice(bf16[512,2048]{1,0:T(8,128)(2,1)} %tokens.3), slice={[496:512], [0:2048]} | slice | bytes 131072 | tf_op jit(solution)/shard_map/slice | solution.py:376
  19.3 3.8 %collective-permute-start = (bf16[16,2048]{1,0:T(8,128)(2,1)S(1)}, bf16[16,2048]{1,0:T(8,128)(2,1)S(1)}, u32[]{:S(2)}, u32[]{:S(2)}) collective-permute-start(bf16[16,2048]{1,0:T(8,128)(2,1)S(1)} %slice.3), channel_id=1, source_target_pairs={{0,4},{4,8},{8,12},{12,16},{16,20},{20,24},{24,28},{1,5},{5,9},{9,... | collective-permute-start | bytes 196616 | tf_op jit(solution)/shard_map/ppermute | solution.py:23
  23.2 0.0 copy-done
  23.2 0.1 dynamic-slice_bitcast_fusion
  23.3 0.1 copy.7.gain
  23.4 0.0 copy-start.3
  23.4 2.0 %collective-permute-done.rim = bf16[16,2048]{1,0:T(8,128)(2,1)S(1)} collective-permute-done((bf16[16,2048]{1,0:T(8,128)(2,1)S(1)}, bf16[16,2048]{1,0:T(8,128)(2,1)S(1)}, u32[]{:S(2)}, u32[]{:S(2)}) %collective-permute-start) | collective-permute-done | bytes 65568 | tf_op jit(solution)/shard_map/ppermute | solution.py:23
  25.4 0.0 copy-start.4
  25.4 0.6 copy-done.4
  26.0 6.5 %query.1 = (bf16[512,256]{1,0:T(8,128)(2,1)}, bf16[512,256]{1,0:T(8,128)(2,1)}) custom-call(bf16[16,2048]{1,0:T(8,128)(2,1)} %copy-done.4, bf16[512,2048]{1,0:T(8,128)(2,1)} %tokens.3, f32[7,384]{1,0:T(8,128)} %taps.4, bf16[3,2048,512]{2,1,0:T(8,128)(2,1)} %bitcast.8), custom_call_target="tpu_custom_call" | custom-call | flops 1073741824 | bytes 4194304 | tf_op jit(solution)/shard_map/query/pallas_call | solution.py:177
  32.5 0.0 copy-start.5
  32.5 0.0 copy-start.2
  32.5 1.6 %all-to-all-done.payload = bf16[8,80,512]{2,1,0:T(8,128)(2,1)S(1)} async-done(((bf16[8,80,512]{2,1,0:T(8,128)(2,1)}), bf16[8,80,512]{2,1,0:T(8,128)(2,1)S(1)}, u32[]{:S(2)}, u32[]{:S(2)}) %all-to-all-start) | async-done | bytes 655392 | tf_op jit(solution)/shard_map/all_to_all | solution.py:374
  34.2 0.0 copy-done.3
  34.2 3.4 %convolve.1 = bf16[2,8,64,256]{3,2,1,0:T(8,128)(2,1)} custom-call(bf16[8,80,512]{2,1,0:T(8,128)(2,1)S(1)} %all-to-all-done.payload, f32[7,384]{1,0:T(8,128)S(1)} %copy-done.3, f32[64,1]{1,0:T(8,128)S(1)} %copy.7.gain), custom_call_target="tpu_custom_call" | custom-call | flops 1073741824 | bytes 1310720 | tf_op jit(solution)/shard_map/convolve/pallas_call | solution.py:300
  37.6 12.4 %all-to-all-start.1 = ((bf16[16,64,256]{2,1,0:T(8,128)(2,1)}), bf16[16,64,256]{2,1,0:T(8,128)(2,1)S(1)}, u32[]{:S(2)}, u32[]{:S(2)}) async-start(bf16[16,64,256]{2,1,0:T(8,128)(2,1)} %bitcast.2), calls=%async_computation.1 | async-start | bytes 1048576 | tf_op jit(solution)/shard_map/all_to_all | solution.py:385
  49.9 0.0 copy-done.5
  49.9 2.0 %collective-permute-start.1 = (bf16[512,256]{1,0:T(8,128)(2,1)S(1)}, bf16[512,256]{1,0:T(8,128)(2,1)S(1)}, u32[]{:S(2)}, u32[]{:S(2)}) collective-permute-start(bf16[512,256]{1,0:T(8,128)(2,1)S(1)} %copy-done.5), channel_id=1, source_target_pairs={{0,2},{2,0},{1,3},{3,1},{4,6},{6,4},{5,7},{7,5},{8,10},{10,8},{9,1... | collective-permute-start | bytes 786440 | tf_op jit(solution)/shard_map/ppermute | solution.py:27
  51.9 23.3 %collective-permute-done.1.q_far = bf16[512,256]{1,0:T(8,128)(2,1)S(1)} collective-permute-done((bf16[512,256]{1,0:T(8,128)(2,1)S(1)}, bf16[512,256]{1,0:T(8,128)(2,1)S(1)}, u32[]{:S(2)}, u32[]{:S(2)}) %collective-permute-start.1) | collective-permute-done | bytes 262176 | tf_op jit(solution)/shard_map/ppermute | solution.py:27
  75.3 0.0 collective-permute-done.2.w_far
  75.3 0.0 all-to-all-done.1
  75.3 0.0 copy-done.2
  75.3 3.4 %output_part.3 = bf16[128,2048]{1,0:T(8,128)(2,1)S(1)} custom-call(bf16[512,256]{1,0:T(8,128)(2,1)S(1)} %copy-done.2, bf16[512,256]{1,0:T(8,128)(2,1)S(1)} %collective-permute-done.1.q_far, bf16[2,512,256]{2,1,0:T(8,128)(2,1)S(1)} %bitcast.5, bf16[512,2048]{1,0:T(8,128)(2,1)S(1)} %copy-done.1, bf16[512,2048]{1,0:T(8,128)(2,1)} %collective-permute-done.2.w_far), custom_call_target="tpu_custom_call" | custom-call | flops 536870912 | bytes 4194304 | tf_op jit(solution)/shard_map/output_part/pallas_call | solution.py:347
  78.7 0.1 collective-permute-start.3
  78.8 3.4 %output_part.2 = f32[128,2048]{1,0:T(8,128)S(1)} custom-call(bf16[512,256]{1,0:T(8,128)(2,1)S(1)} %copy-done.2, bf16[512,256]{1,0:T(8,128)(2,1)S(1)} %collective-permute-done.1.q_far, bf16[2,512,256]{2,1,0:T(8,128)(2,1)S(1)} %bitcast.6, bf16[512,2048]{1,0:T(8,128)(2,1)S(1)} %copy-done.1, bf16[512,2048]{1,0:T(8,128)(2,1)} %collective-permute-done.2.w_far), custom_call_target="tpu_custom_call" | custom-call | flops 536870912 | bytes 4194304 | tf_op jit(solution)/shard_map/output_part/pallas_call | solution.py:347
  82.2 0.0 collective-permute-done.3
  82.2 0.9 %add_convert_fusion = bf16[128,2048]{1,0:T(8,128)(2,1)} fusion(f32[128,2048]{1,0:T(8,128)S(1)} %output_part.2, bf16[128,2048]{1,0:T(8,128)(2,1)S(1)} %collective-permute-done.3), kind=kLoop, calls=%fused_computation | loop fusion | flops 786432 | bytes 2097152 | tf_op jit(solution)/shard_map/convert_element_type | solution.py:390
Async XLA Ops:
  0.0 23.2 %copy-start = (f32[2048]{0:T(1024)S(1)}, f32[2048]{0:T(1024)}, u32[]{:S(2)}) copy-start(f32[2048]{0:T(1024)} %param.10) | copy-start | bytes 24580
  0.0 16.9 %copy-start.1 = (bf16[512,2048]{1,0:T(8,128)(2,1)S(1)}, bf16[512,2048]{1,0:T(8,128)(2,1)}, u32[]{:S(2)}) copy-start(bf16[512,2048]{1,0:T(8,128)(2,1)} %w_near.3) | copy-start | bytes 6291460
  9.6 24.6 %all-to-all-start = ((bf16[8,80,512]{2,1,0:T(8,128)(2,1)}), bf16[8,80,512]{2,1,0:T(8,128)(2,1)S(1)}, u32[]{:S(2)}, u32[]{:S(2)}) async-start(bf16[8,80,512]{2,1,0:T(8,128)(2,1)} %mix.1), calls=%async_computation | async-start | bytes 1310720 | tf_op jit(solution)/shard_map/all_to_all | solution.py:374
  16.9 58.4 %collective-permute-start.2 = (bf16[512,2048]{1,0:T(8,128)(2,1)S(1)}, bf16[512,2048]{1,0:T(8,128)(2,1)}, u32[]{:S(2)}, u32[]{:S(2)}) collective-permute-start(bf16[512,2048]{1,0:T(8,128)(2,1)S(1)} %copy-done.1), channel_id=1, source_target_pairs={{0,2},{2,0},{1,3},{3,1},{4,6},{6,4},{5,7},{7,5},{8,10},{10,8},{9,1... | collective-permute-start | bytes 6291464 | tf_op jit(solution)/shard_map/ppermute | solution.py:27
  19.3 6.1 %collective-permute-start = (bf16[16,2048]{1,0:T(8,128)(2,1)S(1)}, bf16[16,2048]{1,0:T(8,128)(2,1)S(1)}, u32[]{:S(2)}, u32[]{:S(2)}) collective-permute-start(bf16[16,2048]{1,0:T(8,128)(2,1)S(1)} %slice.3), channel_id=1, source_target_pairs={{0,4},{4,8},{8,12},{12,16},{16,20},{20,24},{24,28},{1,5},{5,9},{9,... | collective-permute-start | bytes 196616 | tf_op jit(solution)/shard_map/ppermute | solution.py:23
  23.4 10.8 %copy-start.3 = (f32[7,384]{1,0:T(8,128)S(1)}, f32[7,384]{1,0:T(8,128)}, u32[]{:S(2)}) copy-start(f32[7,384]{1,0:T(8,128)} %taps.4) | copy-start | bytes 32260
  25.4 0.6 copy-start.4
  32.5 17.4 %copy-start.5 = (bf16[512,256]{1,0:T(8,128)(2,1)S(1)}, bf16[512,256]{1,0:T(8,128)(2,1)}, u32[]{:S(2)}) copy-start(bf16[512,256]{1,0:T(8,128)(2,1)} %get-tuple-element.18) | copy-start | bytes 786436
  32.5 42.8 %copy-start.2 = (bf16[512,256]{1,0:T(8,128)(2,1)S(1)}, bf16[512,256]{1,0:T(8,128)(2,1)}, u32[]{:S(2)}) copy-start(bf16[512,256]{1,0:T(8,128)(2,1)} %get-tuple-element.15.q_near) | copy-start | bytes 786436
  37.6 37.7 %all-to-all-start.1 = ((bf16[16,64,256]{2,1,0:T(8,128)(2,1)}), bf16[16,64,256]{2,1,0:T(8,128)(2,1)S(1)}, u32[]{:S(2)}, u32[]{:S(2)}) async-start(bf16[16,64,256]{2,1,0:T(8,128)(2,1)} %bitcast.2), calls=%async_computation.1 | async-start | bytes 1048576 | tf_op jit(solution)/shard_map/all_to_all | solution.py:385
  49.9 25.3 %collective-permute-start.1 = (bf16[512,256]{1,0:T(8,128)(2,1)S(1)}, bf16[512,256]{1,0:T(8,128)(2,1)S(1)}, u32[]{:S(2)}, u32[]{:S(2)}) collective-permute-start(bf16[512,256]{1,0:T(8,128)(2,1)S(1)} %copy-done.5), channel_id=1, source_target_pairs={{0,2},{2,0},{1,3},{3,1},{4,6},{6,4},{5,7},{7,5},{8,10},{10,8},{9,1... | collective-permute-start | bytes 786440 | tf_op jit(solution)/shard_map/ppermute | solution.py:27
  78.7 3.5 %collective-permute-start.3 = (bf16[128,2048]{1,0:T(8,128)(2,1)S(1)}, bf16[128,2048]{1,0:T(8,128)(2,1)S(1)}, u32[]{:S(2)}, u32[]{:S(2)}) collective-permute-start(bf16[128,2048]{1,0:T(8,128)(2,1)S(1)} %output_part.3), channel_id=1, source_target_pairs={{0,1},{1,0},{2,3},{3,2},{4,5},{5,4},{6,7},{7,6},{8,9},{9,8},{10,11... | collective-permute-start | bytes 1572872 | tf_op jit(solution)/shard_map/ppermute | solution.py:27

commit v2 on v1

--- a/solution.py
+++ b/solution.py
@@ -11,6 +11,7 @@
 LANES = 128
 RIM = 16
 LAG = 256
+STAGE_FLOPS = 10**11
 
 
 def fft_index():
@@ -42,66 +43,89 @@
     return feat.astype(jnp.bfloat16).astype(jnp.float32)
 
 
-def mix_kernel(group_size, sizes, tokens, taps, weights, filt, out, ext, wbuf, proj, lag, turned_lag, sems):
-    stretch, chan_rows = sizes
+def mix_kernel(group_size, tokens, taps, weights, filt, out, ext, wbuf, proj, lag, turned_lag, sems):
     n_tok = tokens.shape[0]
     n_ctx = out.shape[0]
+    stretch = out.shape[1] - 8
     _, n_blocks, _, width = wbuf.shape
     n_taps, n_groups = taps.shape[0], taps.shape[1] // 3
     block = n_blocks * width
     group0 = fft_index() * (block // group_size)
     main = pltpu.make_async_copy(tokens, ext, sems.at[0])
+    lag_load = pltpu.make_async_copy(filt, lag, sems.at[1])
+    loads = [
+        pltpu.make_async_copy(weights.at[k + 1, :, pl.ds(blk * width, width)], wbuf.at[k, blk], sems.at[2 + blk * 2 + k])
+        for blk in range(n_blocks)
+        for k in range(2)
+    ]
+    lag_load.start()
     main.start()
-    loads = {}
-    for blk in range(n_blocks):
-        for k in range(2):
-            loads[blk, k] = pltpu.make_async_copy(
-                weights.at[k + 1, :, pl.ds(blk * width, width)], wbuf.at[k, blk], sems.at[2 + blk * 2 + k]
-            )
-            loads[blk, k].start()
-    lag_load = pltpu.make_async_copy(filt, lag, sems.at[1])
-    lag_load.start()
+    for load in loads:
+        load.start()
     tiles = block // LANES
     for k in range(2):
         for tile in range(tiles):
             proj[k, tile, 0:RIM, :] = jnp.zeros((RIM, LANES), jnp.float32)
-    main.wait()
+    coefs = [
+        [
+            spread_taps(taps[:, s * n_groups : (s + 1) * n_groups], group0 + tile * (LANES // group_size), group_size)
+            for tile in range(tiles)
+        ]
+        for s in (1, 2)
+    ]
+    lag_load.wait()
+    for at in range(0, n_tok, LANES):
+        turned_lag[:, at : at + LANES] = lag[at : at + LANES, :].T
+    per_lag = n_tok // (2 * LANES)
+    spans = max(1, stretch // group_size)
+    for dest in range(n_ctx):
+        rows = []
+        for g in range(spans):
+            row = turned_lag[pl.ds(group0 + dest * stretch // group_size + g, 1), :]
+            rows += [row[:, h * 2 * LANES : (h + 1) * 2 * LANES] for h in range(per_lag)]
+        if len(rows) < 8:
+            rows.append(jnp.zeros((8 - len(rows), 2 * LANES), jnp.float32))
+        out[dest, stretch:, 2 * LANES :] = jnp.concatenate(rows, axis=0).astype(jnp.bfloat16)
     chunk = min(128, n_tok)
-    for blk in range(n_blocks):
+    per_block = width // LANES
+
+    def multiply(blk):
         for k in range(2):
-            loads[blk, k].wait()
             full = jnp.dot(ext[...], wbuf[k, blk], preferred_element_type=jnp.float32)
             full = full.astype(jnp.bfloat16).astype(jnp.float32)
-            for t in range(width // LANES):
-                proj[k, blk * (width // LANES) + t, RIM:, :] = full[:, t * LANES : (t + 1) * LANES]
-        for t in range(width // LANES):
-            tile = blk * (width // LANES) + t
-            coefs = [
-                spread_taps(taps[:, s * n_groups : (s + 1) * n_groups], group0 + tile * (LANES // group_size), group_size)
-                for s in (1, 2)
-            ]
+            for t in range(per_block):
+                proj[k, blk * per_block + t, RIM:, :] = full[:, t * LANES : (t + 1) * LANES]
+
+    def finish(blk):
+        for tile in range(blk * per_block, (blk + 1) * per_block):
             for row in range(0, n_tok, chunk):
                 key, value = [
-                    filtered(coefs[k], lambda j: proj[k, tile, RIM + row - j : RIM + row - j + chunk, :], n_taps)
+                    filtered(coefs[k][tile], lambda j: proj[k, tile, RIM + row - j : RIM + row - j + chunk, :], n_taps)
                     for k in range(2)
                 ]
                 flipped = (key * value).T.astype(jnp.bfloat16)
                 for c in range(0, LANES, stretch):
                     out[(tile * LANES + c) // stretch, 0:stretch, row : row + chunk] = flipped[c : c + stretch, :]
-    lag_load.wait()
-    for at in range(0, n_tok, LANES):
-        turned_lag[:, at : at + LANES] = lag[at : at + LANES, :].T
+
+    main.wait()
+    for blk in range(n_blocks):
+        for load in loads[2 * blk : 2 * blk + 2]:
+            load.wait()
+        multiply(blk)
+        if blk:
+            finish(blk - 1)
+    finish(n_blocks - 1)
+    low = lax.broadcasted_iota(jnp.int32, (8, LANES), 1) < LANES // 2
     for dest in range(n_ctx):
-        tile = dest * stretch // LANES
-        group8 = dest * stretch // group_size // 8 * 8
-        lags = turned_lag[pl.ds(pl.multiple_of(group0 + group8, 8), 8), :]
-        ends = []
+        tile, lane = divmod(dest * stretch, LANES)
         for k in range(2):
-            ends += [proj[k, tile, RIM : RIM + 8, :], proj[k, tile, RIM + n_tok - 8 :, :]]
-        if n_tok > 4 * LANES:
-            ends.append(jnp.zeros((8, n_tok - 4 * LANES), jnp.float32))
-        extra = jnp.concatenate([lags, jnp.concatenate(ends, axis=1)], axis=0)
-        out[dest, chan_rows:, :] = extra.astype(jnp.bfloat16)
+            head = proj[k, tile, RIM : RIM + 8, :]
+            tail = proj[k, tile, RIM + n_tok - 8 :, :]
+            if lane:
+                head = pltpu.roll(head, LANES - lane, 1)
+            if lane != LANES // 2:
+                tail = pltpu.roll(tail, (LANES // 2 - lane) % LANES, 1)
+            out[dest, stretch:, k * LANES : (k + 1) * LANES] = jnp.where(low, head, tail).astype(jnp.bfloat16)
 
 
 def mix(group_size, tokens, taps, weights, filt, n_ctx):
@@ -109,12 +133,11 @@
     block = weights.shape[2]
     width = min(256, block)
     stretch = block // n_ctx
-    chan_rows = -(-stretch // 16) * 16
     hbm = pl.BlockSpec(memory_space=pltpu.HBM)
     vmem = pl.BlockSpec(memory_space=pltpu.VMEM)
     return pl.pallas_call(
-        functools.partial(mix_kernel, group_size, (stretch, chan_rows)),
-        out_shape=jax.ShapeDtypeStruct((n_ctx, chan_rows + 16, n_tok), jnp.bfloat16),
+        functools.partial(mix_kernel, group_size),
+        out_shape=jax.ShapeDtypeStruct((n_ctx, stretch + 8, n_tok), jnp.bfloat16),
         in_specs=[hbm, vmem, hbm, hbm],
         out_specs=vmem,
         scratch_shapes=[
@@ -195,7 +218,7 @@
 
 
 def convolve_kernel(group_size, sizes, payload, taps, gain, out, lags, fixed, lagrow, held, total):
-    stretch, chan_rows, span, rows = sizes
+    stretch, span, rows = sizes
     n_src, _, cols = payload.shape
     n_chips, n_ctx, _, piece = out.shape
     n_taps, n_groups = taps.shape[0], taps.shape[1] // 3
@@ -206,24 +229,18 @@
     length = n_src * cols
     static = n_blocks <= 16
     lead = 0 if static else size
-    local = lax.axis_index("ctx") * stretch
-    block = stretch * n_ctx
-
-    group0 = (fft_index() * block + local // LANES * LANES) // group_size
+
+    group0 = (fft_index() * stretch * n_ctx + lax.axis_index("ctx") * stretch) // group_size
     coefs = [
         spread_taps(taps[:, s * n_groups : (s + 1) * n_groups], group0, group_size) for s in (1, 2)
     ]
+    ends = [[payload[s, stretch:, k * LANES : (k + 1) * LANES].astype(jnp.float32) for k in range(2)] for s in range(n_src)]
     first = []
     for s in range(n_src):
         made = None
         for k in range(2):
-            head = payload[s, chan_rows + 8 : chan_rows + 16, 2 * k * LANES : (2 * k + 1) * LANES]
-            if s == 0:
-                tail = jnp.zeros((8, LANES), jnp.float32)
-            else:
-                tail = payload[s - 1, chan_rows + 8 : chan_rows + 16, (2 * k + 1) * LANES : (2 * k + 2) * LANES]
-                tail = tail.astype(jnp.float32)
-            both = jnp.concatenate([tail, head.astype(jnp.float32)], axis=0)
+            before = pltpu.roll(ends[s - 1][k], LANES // 2, 1) if s else jnp.zeros((8, LANES), jnp.float32)
+            both = jnp.concatenate([before, ends[s][k]], axis=0)
             feat = filtered(coefs[k], lambda j: both[8 - j : 16 - j, :], n_taps)
             made = feat if made is None else made * feat
         first.append(made)
@@ -232,12 +249,15 @@
         if len(some) < 16:
             some = some + [jnp.zeros(((16 - len(some)) * 8, LANES), jnp.float32)]
         fixed[:, s * 8 : s * 8 + LANES] = jnp.concatenate(some, axis=0).T
-    chan0 = local % LANES
     lane = lax.broadcasted_iota(jnp.int32, (span, LANES), 1)
 
+    per_lag = cols // (2 * LANES)
     for s in range(n_src):
-        lagrow[:, s * cols : (s + 1) * cols] = payload[s, chan_rows : chan_rows + 8, :].astype(jnp.float32)
-    group_in = local // group_size % 8
+        piece_rows = payload[s, stretch:, 2 * LANES :].astype(jnp.float32)
+        for g in range(stretch // span):
+            for h in range(per_lag):
+                at = s * cols + h * 2 * LANES
+                lagrow[g : g + 1, at : at + 2 * LANES] = piece_rows[g * per_lag + h : g * per_lag + h + 1, :]
     zeros = jnp.zeros((1, LANES), jnp.float32)
 
     def lag_block(d):
@@ -249,7 +269,7 @@
         return jnp.concatenate([near, lags[:, pl.ds(at, LAG)]], axis=0)
 
     for g in range(stretch // span):
-        row = jnp.concatenate([zeros, lagrow[pl.ds(group_in + g, 1), :], zeros], axis=1)
+        row = jnp.concatenate([zeros, lagrow[g : g + 1, :], zeros], axis=1)
         wide = jnp.broadcast_to(row, (LANES, length + 2 * LANES))
         turned = pltpu.roll(wide, 0, 1, stride=1, stride_axis=0)
         lags[...] = turned[:, : length + LANES].astype(jnp.bfloat16)
@@ -262,7 +282,7 @@
             at = lead + i * rows
             held[at : at + span, :] = part
             if i % per_src == 0:
-                patch = fixed[pl.ds(pl.multiple_of(chan0 + g * span, 8), span), s // 16 * LANES : (s // 16 + 1) * LANES]
+                patch = fixed[chans, s // 16 * LANES : (s // 16 + 1) * LANES]
                 if s % 16:
                     patch = pltpu.roll(patch, LANES - s % 16 * 8, 1)
                 patched = jnp.where(lane < 8, patch, part[:, :LANES].astype(jnp.float32))
@@ -290,7 +310,7 @@
 
 
 def convolve(group_size, span, stretch, payload, taps, gain, n_chips):
-    n_src, all_rows, cols = payload.shape
+    n_src, _, cols = payload.shape
     n_blocks = n_src * cols // LAG
     rows = max(span, 16)
     size = n_blocks * rows
@@ -298,7 +318,7 @@
     held = size if n_blocks <= 16 else 2 * size
     vmem = pl.BlockSpec(memory_space=pltpu.VMEM)
     return pl.pallas_call(
-        functools.partial(convolve_kernel, group_size, (stretch, all_rows - 16, span, rows)),
+        functools.partial(convolve_kernel, group_size, (stretch, span, rows)),
         out_shape=jax.ShapeDtypeStruct((n_chips, n_src, stretch, cols // n_chips), jnp.bfloat16),
         in_specs=[vmem, vmem, vmem],
         out_specs=vmem,
@@ -317,46 +337,61 @@
     )(payload, taps, gain)
 
 
-def output_kernel(other_core, q_near, q_far, conv, w_near, w_far, out, gated):
+def stage_kernel(w_near, w_far, out, sems):
+    copies = [pltpu.make_async_copy(w, out.at[k], sems.at[k]) for k, w in enumerate((w_near, w_far))]
+    for copy in copies:
+        copy.start()
+    for copy in copies:
+        copy.wait()
+
+
+def stage(w_near, w_far):
+    hbm = pl.BlockSpec(memory_space=pltpu.HBM)
+    return pl.pallas_call(
+        stage_kernel,
+        out_shape=pltpu.VMEM((2,) + w_near.shape, w_near.dtype),
+        in_specs=[hbm, hbm],
+        out_specs=pl.BlockSpec(memory_space=pltpu.VMEM),
+        scratch_shapes=[pltpu.SemaphoreType.DMA((2,))],
+        compiler_params=pltpu.CompilerParams(vmem_limit_bytes=16 * MIB),
+        cost_estimate=pl.CostEstimate(flops=STAGE_FLOPS, bytes_accessed=8 * w_near.size, transcendentals=0),
+        name="stage",
+    )(w_near, w_far)
+
+
+def output_kernel(other_core, q_near, q_far, conv, weights, out):
     n_tok = out.shape[0]
-
-    @pl.when(pl.program_id(0) == 0)
-    def _():
-        chip = lax.axis_index("chip")
-        core = lax.axis_index("core") ^ other_core
-        for k, query in enumerate((q_near, q_far)):
-            for c in range(0, query.shape[0], LANES):
-                for t in range(0, n_tok, LANES):
-                    at = pl.ds(pl.multiple_of(core * n_tok + t, LANES), LANES)
-                    rows = pl.ds(c, LANES)
-                    product = query[rows, at].astype(jnp.float32) * conv[chip ^ k, rows, at].astype(jnp.float32)
-                    gated[k, t : t + LANES, c : c + LANES] = product.T.astype(jnp.bfloat16)
-
-    acc = jnp.dot(gated[0], w_near[...], preferred_element_type=jnp.float32)
-    acc += jnp.dot(gated[1], w_far[...], preferred_element_type=jnp.float32)
-    out[...] = acc.astype(out.dtype)
+    chip = lax.axis_index("chip")
+    core = lax.axis_index("core") ^ other_core
+    at = pl.ds(pl.multiple_of(core * n_tok, LANES), n_tok)
+    gated = []
+    for k, query in enumerate((q_near, q_far)):
+        product = query[:, at].astype(jnp.float32) * conv[chip ^ k, :, at].astype(jnp.float32)
+        gated.append(product.T.astype(jnp.bfloat16))
+    width = out.shape[1]
+    step = min(512, width)
+    for col in range(0, width, step):
+        acc = jnp.dot(gated[0], weights[0, :, col : col + step], preferred_element_type=jnp.float32)
+        acc += jnp.dot(gated[1], weights[1, :, col : col + step], preferred_element_type=jnp.float32)
+        out[:, col : col + step] = acc.astype(out.dtype)
 
 
 def output_part(other_core, dtype, query, conv, weights):
     _, block, n_tok = conv.shape
     n_tok //= 2
-    width = weights[0].shape[1]
-    step = min(512, width)
+    width = weights.shape[2]
     vmem = pl.BlockSpec(memory_space=pltpu.VMEM)
-    columns = pl.BlockSpec((block, step), lambda n: (0, n))
     return pl.pallas_call(
         functools.partial(output_kernel, other_core),
-        grid=(width // step,),
         out_shape=jax.ShapeDtypeStruct((n_tok, width), dtype),
-        in_specs=[vmem] * 3 + [columns] * 2,
-        out_specs=pl.BlockSpec((n_tok, step), lambda n: (0, n)),
-        scratch_shapes=[pltpu.VMEM((2, n_tok, block), jnp.bfloat16)],
+        in_specs=[vmem] * 4,
+        out_specs=vmem,
         compiler_params=pltpu.CompilerParams(vmem_limit_bytes=24 * MIB),
         cost_estimate=pl.CostEstimate(
             flops=4 * block * n_tok * width, bytes_accessed=4 * block * width, transcendentals=0
         ),
         name="output_part",
-    )(*query, conv, *weights)
+    )(*query, conv, weights)
 
 
 def body(tokens, w_in, short_taps, long_filter, skip_gain, w_out):
@@ -375,18 +410,20 @@
 
     ends, _ = lax.optimization_barrier((tokens[tok_len - RIM :], sent))
     rim = passed_along(ends, "ctx", 1)
-    near, far = make_query(group_size, rim, tokens, short_taps, weights, n_chips)
-    near, far, conv_taps = lax.optimization_barrier((near, far, short_taps))
+    rim, conv_taps = lax.optimization_barrier((rim, short_taps))
 
     gain = lax.dynamic_slice_in_dim(skip_gain, fft_index() * block + lax.axis_index("ctx") * stretch, stretch, 0)
     conv = convolve(group_size, span, stretch, payload, conv_taps, gain[:, None], n_chips)
-    far, _ = lax.optimization_barrier((far, conv))
+
+    rim, query_taps, _ = lax.optimization_barrier((rim, short_taps, conv))
+    near, far = make_query(group_size, rim, tokens, query_taps, weights, n_chips)
     query = (near, swapped(far, "chip"))
     conv = lax.all_to_all(conv.reshape(n_chips * n_ctx, stretch, piece), ("chip", "ctx"), 0, 0, tiled=True)
     conv = conv.reshape(n_chips, block, piece)
 
-    beside = swapped(output_part(1, jnp.bfloat16, query, conv, (w_out, across)), "core")
-    total = output_part(0, jnp.float32, query, conv, (w_out, across))
+    out_weights = stage(w_out, across)
+    beside = swapped(output_part(1, jnp.bfloat16, query, conv, out_weights), "core")
+    total = output_part(0, jnp.float32, query, conv, out_weights)
     return (total + beside.astype(jnp.float32)).astype(jnp.bfloat16)
 
 

time: 83.6 us -> 66.4 us (0.79)
  starting transfers between devices: 27.1 us -> 19 us
  Pallas kernels: 26.2 us -> 19.2 us
  waiting for transfers between devices: 27 us -> 21.5 us
  local copies, waits for them, and re-layouts: 1.67 us -> 5.18 us
    ppermute x3, waiting for transfers between devices: 23.3 us -> 10.8 us  [swapped(): lax.ppermute(block, axis, [(i, i ^ 1) for i in range(lax.axis_size(axis))])]
    all_to_all x1, starting transfers between devices: 12.4 us -> 4.23 us  [body(): lax.all_to_all(conv.reshape(n_chips * n_ctx, stretch, piece), ('chip', 'c...]
    all_to_all x1, waiting for transfers between devices: 1.64 us -> 8.83 us  [body(): payload = lax.all_to_all(sent, 'ctx', 0, 0, tiled=True)]
    pallas_call x4 -> x5, Pallas kernels: 19.8 us -> 12.6 us  [the longest x1 7.4 us: mix(): pl.pallas_call(functools.partial(mix_kernel, group_size), out_shape=jax.S...]
    unnamed x12 -> x14, local copies, waits for them, and re-layouts: 0.65 us -> 4.16 us
    all_to_all x1, starting transfers between devices: 7.27 us -> 5.82 us  [body(): payload = lax.all_to_all(sent, 'ctx', 0, 0, tiled=True)]
    ppermute x3, starting transfers between devices: 3.65 us -> 5.05 us  [swapped(): lax.ppermute(block, axis, [(i, i ^ 1) for i in range(lax.axis_size(axis))])]
  transfers between devices with their start and end apart: 6 -> 6, of which waited for: 3 -> 5; matrix products, arithmetic and copies ran while one was open for 1% -> 2% of each run, Pallas kernels for 16% -> 28%
where the time goes in v2:
time: 66.4 us; the launch traced here: 65.9 us
  waiting for transfers between devices  21.5 us (32%)
  Pallas kernels  19.2 us (29%)
  starting transfers between devices  19 us (29%)
  local copies, waits for them, and re-layouts  5.18 us (8%)
  other arithmetic  0.9 us (1%)
    ppermute x3, waiting for transfers between devices, swapped(): lax.ppermute(block, axis, [(i, i ^ 1) for i in range(lax.axis_size(axis))])  10.8 us
    all_to_all x1, waiting for transfers between devices, body(): payload = lax.all_to_all(sent, 'ctx', 0, 0, tiled=True)  8.83 us
    pallas_call x1, Pallas kernels, mix(): pl.pallas_call(functools.partial(mix_kernel, group_size), out_shape=jax.S...  7.4 us
    pallas_call x1, Pallas kernels, make_query(): pl.pallas_call(functools.partial(query_kernel, group_size), out_shape=[ja...  6.6 us
    all_to_all x1, starting transfers between devices, body(): payload = lax.all_to_all(sent, 'ctx', 0, 0, tiled=True)  5.82 us
    ppermute x3, starting transfers between devices, swapped(): lax.ppermute(block, axis, [(i, i ^ 1) for i in range(lax.axis_size(axis))])  5.05 us
    all_to_all x1, starting transfers between devices, body(): lax.all_to_all(conv.reshape(n_chips * n_ctx, stretch, piece), ('chip', 'c...  4.23 us
    unnamed x14, local copies, waits for them, and re-layouts  4.16 us
  transfers between devices with their start and end apart: 6, of which 5 were waited for; matrix products, arithmetic and copies ran while one was open for 2% of the time, Pallas kernels for 28%

profile of v2, /device:TPU:0, one launch (start us, length us, event | category | flops | bytes accessed | tf_op | source)
XLA Modules:
  0.0 65.9 jit_solution(11246403381069708839)
XLA Ops:
  0.0 0.0 copy-start
  0.0 3.0 %collective-permute-start.2 = (bf16[512,2048]{1,0:T(8,128)(2,1)}, bf16[512,2048]{1,0:T(8,128)(2,1)S(1)}, u32[]{:S(2)}, u32[]{:S(2)}) collective-permute-start(bf16[512,2048]{1,0:T(8,128)(2,1)} %w_near.1), channel_id=1, source_target_pairs={{0,2},{2,0},{1,3},{3,1},{4,6},{6,4},{5,7},{7,5},{8,10},{10,8},{9,1... | collective-permute-start | bytes 6291464 | tf_op jit(solution)/shard_map/ppermute | solution.py:28
  3.0 0.0 copy-start.4
  3.0 7.4 %mix.1 = bf16[8,72,512]{2,1,0:T(8,128)(2,1)} custom-call(bf16[512,2048]{1,0:T(8,128)(2,1)} %tokens.3, f32[7,384]{1,0:T(8,128)} %taps.3, bf16[3,2048,512]{2,1,0:T(8,128)(2,1)} %bitcast.7, f32[512,128]{1,0:T(8,128)} %filt.1), custom_call_target="tpu_custom_call" | custom-call | flops 2147483648 | bytes 6291456 | tf_op jit(solution)/shard_map/mix/pallas_call | solution.py:138
  10.4 5.8 %all-to-all-start = ((bf16[8,72,512]{2,1,0:T(8,128)(2,1)}), bf16[8,72,512]{2,1,0:T(8,128)(2,1)S(1)}, u32[]{:S(2)}, u32[]{:S(2)}) async-start(bf16[8,72,512]{2,1,0:T(8,128)(2,1)} %mix.1), calls=%async_computation | async-start | bytes 1179648 | tf_op jit(solution)/shard_map/all_to_all | solution.py:409
  16.2 0.8 %slice.3 = bf16[16,2048]{1,0:T(8,128)(2,1)S(1)} slice(bf16[512,2048]{1,0:T(8,128)(2,1)} %tokens.3), slice={[496:512], [0:2048]} | slice | bytes 131072 | tf_op jit(solution)/shard_map/slice | solution.py:411
  17.0 3.9 %collective-permute-start = (bf16[16,2048]{1,0:T(8,128)(2,1)S(1)}, bf16[16,2048]{1,0:T(8,128)(2,1)S(1)}, u32[]{:S(2)}, u32[]{:S(2)}) collective-permute-start(bf16[16,2048]{1,0:T(8,128)(2,1)S(1)} %slice.3), channel_id=1, source_target_pairs={{0,4},{4,8},{8,12},{12,16},{16,20},{20,24},{24,28},{1,5},{5,9},{9,... | collective-permute-start | bytes 196616 | tf_op jit(solution)/shard_map/ppermute | solution.py:24
  21.0 0.0 copy-done
  21.0 0.1 dynamic-slice_bitcast_fusion
  21.1 0.1 copy.7.gain
  21.2 1.8 %collective-permute-done.rim = bf16[16,2048]{1,0:T(8,128)(2,1)S(1)} collective-permute-done((bf16[16,2048]{1,0:T(8,128)(2,1)S(1)}, bf16[16,2048]{1,0:T(8,128)(2,1)S(1)}, u32[]{:S(2)}, u32[]{:S(2)}) %collective-permute-start) | collective-permute-done | bytes 65568 | tf_op jit(solution)/shard_map/ppermute | solution.py:24
  23.0 0.0 copy-start.6
  23.0 8.8 %all-to-all-done.payload = bf16[8,72,512]{2,1,0:T(8,128)(2,1)S(1)} async-done(((bf16[8,72,512]{2,1,0:T(8,128)(2,1)}), bf16[8,72,512]{2,1,0:T(8,128)(2,1)S(1)}, u32[]{:S(2)}, u32[]{:S(2)}) %all-to-all-start) | async-done | bytes 589856 | tf_op jit(solution)/shard_map/all_to_all | solution.py:409
  31.8 0.0 copy-done.4
  31.8 3.4 %convolve.1 = bf16[2,8,64,256]{3,2,1,0:T(8,128)(2,1)} custom-call(bf16[8,72,512]{2,1,0:T(8,128)(2,1)S(1)} %all-to-all-done.payload, f32[7,384]{1,0:T(8,128)S(1)} %copy-done.4, f32[64,1]{1,0:T(8,128)S(1)} %copy.7.gain), custom_call_target="tpu_custom_call" | custom-call | flops 1073741824 | bytes 1179648 | tf_op jit(solution)/shard_map/convolve/pallas_call | solution.py:320
  35.2 0.0 copy-done.6
  35.2 4.2 %all-to-all-start.1 = ((bf16[16,64,256]{2,1,0:T(8,128)(2,1)}), bf16[16,64,256]{2,1,0:T(8,128)(2,1)S(1)}, u32[]{:S(2)}, u32[]{:S(2)}) async-start(bf16[16,64,256]{2,1,0:T(8,128)(2,1)} %bitcast.2), calls=%async_computation.1 | async-start | bytes 1048576 | tf_op jit(solution)/shard_map/all_to_all | solution.py:421
  39.4 0.0 copy-start.5
  39.4 6.6 %query.1 = (bf16[512,256]{1,0:T(8,128)(2,1)}, bf16[512,256]{1,0:T(8,128)(2,1)}) custom-call(bf16[16,2048]{1,0:T(8,128)(2,1)} %copy-done.6, bf16[512,2048]{1,0:T(8,128)(2,1)} %tokens.3, f32[7,384]{1,0:T(8,128)} %taps.3, bf16[3,2048,512]{2,1,0:T(8,128)(2,1)} %bitcast.8), custom_call_target="tpu_custom_call" | custom-call | flops 1073741824 | bytes 4194304 | tf_op jit(solution)/shard_map/query/pallas_call | solution.py:200
  46.1 0.0 copy-start.3
  46.1 2.0 %collective-permute-start.1 = (bf16[512,256]{1,0:T(8,128)(2,1)}, bf16[512,256]{1,0:T(8,128)(2,1)S(1)}, u32[]{:S(2)}, u32[]{:S(2)}) collective-permute-start(bf16[512,256]{1,0:T(8,128)(2,1)} %get-tuple-element.18), channel_id=1, source_target_pairs={{0,2},{2,0},{1,3},{3,1},{4,6},{6,4},{5,7},{7,5},{8,10},{10,8},{9,1... | collective-permute-start | bytes 786440 | tf_op jit(solution)/shard_map/ppermute | solution.py:28
  48.1 6.3 %collective-permute-done.2.w_far = bf16[512,2048]{1,0:T(8,128)(2,1)S(1)} collective-permute-done((bf16[512,2048]{1,0:T(8,128)(2,1)}, bf16[512,2048]{1,0:T(8,128)(2,1)S(1)}, u32[]{:S(2)}, u32[]{:S(2)}) %collective-permute-start.2) | collective-permute-done | bytes 2097184 | tf_op jit(solution)/shard_map/ppermute | solution.py:28
  54.4 0.0 copy-done.5
  54.4 0.3 stage.1.weights
  54.7 0.0 copy-start.1
  54.7 1.9 %copy-done.1 = bf16[2,512,2048]{2,1,0:T(8,128)(2,1)} copy-done((bf16[2,512,2048]{2,1,0:T(8,128)(2,1)}, bf16[2,512,2048]{2,1,0:T(8,128)(2,1)S(1)}, u32[]{:S(2)}) %copy-start.1) | copy-done | bytes 4194328
  56.6 3.4 %collective-permute-done.1.q_far = bf16[512,256]{1,0:T(8,128)(2,1)S(1)} collective-permute-done((bf16[512,256]{1,0:T(8,128)(2,1)}, bf16[512,256]{1,0:T(8,128)(2,1)S(1)}, u32[]{:S(2)}, u32[]{:S(2)}) %collective-permute-start.1) | collective-permute-done | bytes 262176 | tf_op jit(solution)/shard_map/ppermute | solution.py:28
  60.0 0.0 all-to-all-done.1
  60.0 0.0 copy-done.3
  60.0 0.0 copy-start.2
  60.1 2.2 %copy-done.2 = bf16[2,512,2048]{2,1,0:T(8,128)(2,1)S(1)} copy-done((bf16[2,512,2048]{2,1,0:T(8,128)(2,1)S(1)}, bf16[2,512,2048]{2,1,0:T(8,128)(2,1)}, u32[]{:S(2)}) %copy-start.2) | copy-done | bytes 4194328
  62.2 0.8 %output_part.3 = bf16[128,2048]{1,0:T(8,128)(2,1)S(1)} custom-call(bf16[512,256]{1,0:T(8,128)(2,1)S(1)} %copy-done.3, bf16[512,256]{1,0:T(8,128)(2,1)S(1)} %collective-permute-done.1.q_far, bf16[2,512,256]{2,1,0:T(8,128)(2,1)S(1)} %bitcast.5, bf16[2,512,2048]{2,1,0:T(8,128)(2,1)S(1)} %copy-done.2), custom_call_target="tpu_custom_call" | custom-call | flops 536870912 | bytes 4194304 | tf_op jit(solution)/shard_map/output_part/pallas_call | solution.py:384
  63.0 0.1 collective-permute-start.3
  63.1 0.8 %output_part.2 = f32[128,2048]{1,0:T(8,128)S(1)} custom-call(bf16[512,256]{1,0:T(8,128)(2,1)S(1)} %copy-done.3, bf16[512,256]{1,0:T(8,128)(2,1)S(1)} %collective-permute-done.1.q_far, bf16[2,512,256]{2,1,0:T(8,128)(2,1)S(1)} %bitcast.6, bf16[2,512,2048]{2,1,0:T(8,128)(2,1)S(1)} %copy-done.2), custom_call_target="tpu_custom_call" | custom-call | flops 536870912 | bytes 4194304 | tf_op jit(solution)/shard_map/output_part/pallas_call | solution.py:384
  63.9 1.1 %collective-permute-done.3 = bf16[128,2048]{1,0:T(8,128)(2,1)S(1)} collective-permute-done((bf16[128,2048]{1,0:T(8,128)(2,1)S(1)}, bf16[128,2048]{1,0:T(8,128)(2,1)S(1)}, u32[]{:S(2)}, u32[]{:S(2)}) %collective-permute-start.3) | collective-permute-done | bytes 524320 | tf_op jit(solution)/shard_map/ppermute | solution.py:28
  65.0 0.9 %add_convert_fusion = bf16[128,2048]{1,0:T(8,128)(2,1)} fusion(f32[128,2048]{1,0:T(8,128)S(1)} %output_part.2, bf16[128,2048]{1,0:T(8,128)(2,1)S(1)} %collective-permute-done.3), kind=kLoop, calls=%fused_computation | loop fusion | flops 786432 | bytes 2097152 | tf_op jit(solution)/shard_map/convert_element_type | solution.py:427
Async XLA Ops:
  0.0 21.0 %copy-start = (f32[2048]{0:T(1024)S(1)}, f32[2048]{0:T(1024)}, u32[]{:S(2)}) copy-start(f32[2048]{0:T(1024)} %param.10) | copy-start | bytes 24580
  0.0 54.4 %collective-permute-start.2 = (bf16[512,2048]{1,0:T(8,128)(2,1)}, bf16[512,2048]{1,0:T(8,128)(2,1)S(1)}, u32[]{:S(2)}, u32[]{:S(2)}) collective-permute-start(bf16[512,2048]{1,0:T(8,128)(2,1)} %w_near.1), channel_id=1, source_target_pairs={{0,2},{2,0},{1,3},{3,1},{4,6},{6,4},{5,7},{7,5},{8,10},{10,8},{9,1... | collective-permute-start | bytes 6291464 | tf_op jit(solution)/shard_map/ppermute | solution.py:28
  3.0 28.9 %copy-start.4 = (f32[7,384]{1,0:T(8,128)S(1)}, f32[7,384]{1,0:T(8,128)}, u32[]{:S(2)}) copy-start(f32[7,384]{1,0:T(8,128)} %taps.3) | copy-start | bytes 32260
  10.4 21.5 %all-to-all-start = ((bf16[8,72,512]{2,1,0:T(8,128)(2,1)}), bf16[8,72,512]{2,1,0:T(8,128)(2,1)S(1)}, u32[]{:S(2)}, u32[]{:S(2)}) async-start(bf16[8,72,512]{2,1,0:T(8,128)(2,1)} %mix.1), calls=%async_computation | async-start | bytes 1179648 | tf_op jit(solution)/shard_map/all_to_all | solution.py:409
  17.0 6.0 %collective-permute-start = (bf16[16,2048]{1,0:T(8,128)(2,1)S(1)}, bf16[16,2048]{1,0:T(8,128)(2,1)S(1)}, u32[]{:S(2)}, u32[]{:S(2)}) collective-permute-start(bf16[16,2048]{1,0:T(8,128)(2,1)S(1)} %slice.3), channel_id=1, source_target_pairs={{0,4},{4,8},{8,12},{12,16},{16,20},{20,24},{24,28},{1,5},{5,9},{9,... | collective-permute-start | bytes 196616 | tf_op jit(solution)/shard_map/ppermute | solution.py:24
  23.0 12.2 %copy-start.6 = (bf16[16,2048]{1,0:T(8,128)(2,1)}, bf16[16,2048]{1,0:T(8,128)(2,1)S(1)}, u32[]{:S(2)}) copy-start(bf16[16,2048]{1,0:T(8,128)(2,1)S(1)} %collective-permute-done.rim) | copy-start | bytes 196612
  35.2 24.9 %all-to-all-start.1 = ((bf16[16,64,256]{2,1,0:T(8,128)(2,1)}), bf16[16,64,256]{2,1,0:T(8,128)(2,1)S(1)}, u32[]{:S(2)}, u32[]{:S(2)}) async-start(bf16[16,64,256]{2,1,0:T(8,128)(2,1)} %bitcast.2), calls=%async_computation.1 | async-start | bytes 1048576 | tf_op jit(solution)/shard_map/all_to_all | solution.py:421
  39.4 14.9 %copy-start.5 = (bf16[512,2048]{1,0:T(8,128)(2,1)S(1)}, bf16[512,2048]{1,0:T(8,128)(2,1)}, u32[]{:S(2)}) copy-start(bf16[512,2048]{1,0:T(8,128)(2,1)} %w_near.1) | copy-start | bytes 6291460
  46.1 14.0 %copy-start.3 = (bf16[512,256]{1,0:T(8,128)(2,1)S(1)}, bf16[512,256]{1,0:T(8,128)(2,1)}, u32[]{:S(2)}) copy-start(bf16[512,256]{1,0:T(8,128)(2,1)} %get-tuple-element.17.q_near) | copy-start | bytes 786436
  46.1 14.0 %collective-permute-start.1 = (bf16[512,256]{1,0:T(8,128)(2,1)}, bf16[512,256]{1,0:T(8,128)(2,1)S(1)}, u32[]{:S(2)}, u32[]{:S(2)}) collective-permute-start(bf16[512,256]{1,0:T(8,128)(2,1)} %get-tuple-element.18), channel_id=1, source_target_pairs={{0,2},{2,0},{1,3},{3,1},{4,6},{6,4},{5,7},{7,5},{8,10},{10,8},{9,1... | collective-permute-start | bytes 786440 | tf_op jit(solution)/shard_map/ppermute | solution.py:28
  54.7 2.0 %copy-start.1 = (bf16[2,512,2048]{2,1,0:T(8,128)(2,1)}, bf16[2,512,2048]{2,1,0:T(8,128)(2,1)S(1)}, u32[]{:S(2)}) copy-start(bf16[2,512,2048]{2,1,0:T(8,128)(2,1)S(1)} %stage.1.weights) | copy-start | bytes 12582916
  60.0 2.2 %copy-start.2 = (bf16[2,512,2048]{2,1,0:T(8,128)(2,1)S(1)}, bf16[2,512,2048]{2,1,0:T(8,128)(2,1)}, u32[]{:S(2)}) copy-start(bf16[2,512,2048]{2,1,0:T(8,128)(2,1)} %copy-done.1) | copy-start | bytes 12582916
  63.0 2.0 %collective-permute-start.3 = (bf16[128,2048]{1,0:T(8,128)(2,1)S(1)}, bf16[128,2048]{1,0:T(8,128)(2,1)S(1)}, u32[]{:S(2)}, u32[]{:S(2)}) collective-permute-start(bf16[128,2048]{1,0:T(8,128)(2,1)S(1)} %output_part.3), channel_id=1, source_target_pairs={{0,1},{1,0},{2,3},{3,2},{4,5},{5,4},{6,7},{7,6},{8,9},{9,8},{10,11... | collective-permute-start | bytes 1572872 | tf_op jit(solution)/shard_map/ppermute | solution.py:28

commit v3 on v2

--- a/solution.py
+++ b/solution.py
@@ -11,7 +11,10 @@
 LANES = 128
 RIM = 16
 LAG = 256
-STAGE_FLOPS = 10**11
+ARRIVED_FLOPS = 10**11
+ARRIVED_VMEM = 2 * MIB
+OUTPUT_VMEM = 32 * MIB
+CONVOLVE_FLOPS = 10**10
 
 
 def fft_index():
@@ -43,7 +46,7 @@
     return feat.astype(jnp.bfloat16).astype(jnp.float32)
 
 
-def mix_kernel(group_size, tokens, taps, weights, filt, out, ext, wbuf, proj, lag, turned_lag, sems):
+def mix_kernel(group_size, tokens, taps, weights, filt, w_out, out, direct, ext, wbuf, proj, lag, turned_lag, cut, sems):
     n_tok = tokens.shape[0]
     n_ctx = out.shape[0]
     stretch = out.shape[1] - 8
@@ -107,13 +110,19 @@
                 for c in range(0, LANES, stretch):
                     out[(tile * LANES + c) // stretch, 0:stretch, row : row + chunk] = flipped[c : c + stretch, :]
 
+    fetch = pltpu.make_async_copy(w_out.at[pl.ds(w_out.shape[0] - cut.shape[0], cut.shape[0])], cut, sems.at[2 + 2 * n_blocks])
+    store = pltpu.make_async_copy(cut, direct, sems.at[3 + 2 * n_blocks])
     main.wait()
     for blk in range(n_blocks):
         for load in loads[2 * blk : 2 * blk + 2]:
             load.wait()
+        if blk == n_blocks - 1:
+            fetch.start()
         multiply(blk)
         if blk:
             finish(blk - 1)
+    fetch.wait()
+    store.start()
     finish(n_blocks - 1)
     low = lax.broadcasted_iota(jnp.int32, (8, LANES), 1) < LANES // 2
     for dest in range(n_ctx):
@@ -126,95 +135,124 @@
             if lane != LANES // 2:
                 tail = pltpu.roll(tail, (LANES // 2 - lane) % LANES, 1)
             out[dest, stretch:, k * LANES : (k + 1) * LANES] = jnp.where(low, head, tail).astype(jnp.bfloat16)
-
-
-def mix(group_size, tokens, taps, weights, filt, n_ctx):
+    store.wait()
+
+
+def mix(group_size, tokens, taps, weights, filt, w_out, rest, n_ctx):
     n_tok, depth = tokens.shape
     block = weights.shape[2]
     width = min(256, block)
     stretch = block // n_ctx
+    direct = (rest, w_out.shape[1])
     hbm = pl.BlockSpec(memory_space=pltpu.HBM)
     vmem = pl.BlockSpec(memory_space=pltpu.VMEM)
     return pl.pallas_call(
         functools.partial(mix_kernel, group_size),
-        out_shape=jax.ShapeDtypeStruct((n_ctx, stretch + 8, n_tok), jnp.bfloat16),
-        in_specs=[hbm, vmem, hbm, hbm],
-        out_specs=vmem,
+        out_shape=[jax.ShapeDtypeStruct(shape, jnp.bfloat16) for shape in ((n_ctx, stretch + 8, n_tok), direct)],
+        in_specs=[hbm, vmem, hbm, hbm, hbm],
+        out_specs=[vmem, hbm],
         scratch_shapes=[
             pltpu.VMEM((n_tok, depth), jnp.bfloat16),
             pltpu.VMEM((2, block // width, depth, width), jnp.bfloat16),
             pltpu.VMEM((2, block // LANES, RIM + n_tok, LANES), jnp.float32),
             pltpu.VMEM(filt.shape, jnp.float32),
             pltpu.VMEM(filt.shape[::-1], jnp.float32),
-            pltpu.SemaphoreType.DMA((2 + 2 * (block // width),)),
+            pltpu.VMEM(direct, jnp.bfloat16),
+            pltpu.SemaphoreType.DMA((4 + 2 * (block // width),)),
         ],
         compiler_params=pltpu.CompilerParams(vmem_limit_bytes=56 * MIB),
         cost_estimate=pl.CostEstimate(
             flops=4 * n_tok * depth * block, bytes_accessed=2 * (n_tok * depth + 2 * depth * block), transcendentals=0
         ),
         name="mix",
-    )(tokens, taps, weights, filt)
-
-
-def query_kernel(group_size, rim, tokens, taps, weights, mine, other, pieces, ext, wbuf, proj, sems):
+    )(tokens, taps, weights, filt, w_out)
+
+
+def query_kernel(group_size, tokens, taps, weights, after, mine, other, ends, pieces, ext, wbuf, proj, sems):
     n_tok = tokens.shape[0]
-    n_blocks, _, width = wbuf.shape
+    block = wbuf.shape[1]
     n_taps, n_groups = taps.shape[0], taps.shape[1] // 3
     piece = pieces.shape[2]
-    group0 = fft_index() * (n_blocks * width // group_size)
-    first = pltpu.make_async_copy(rim, ext.at[pl.ds(0, RIM)], sems.at[0])
-    main = pltpu.make_async_copy(tokens, ext.at[pl.ds(RIM, n_tok)], sems.at[1])
-    first.start()
+    group0 = fft_index() * (block // group_size)
+    main = pltpu.make_async_copy(tokens, ext, sems.at[0])
+    load = pltpu.make_async_copy(weights.at[0], wbuf, sems.at[1])
     main.start()
-    loads = []
-    for blk in range(n_blocks):
-        loads.append(
-            pltpu.make_async_copy(weights.at[0, :, pl.ds(blk * width, width)], wbuf.at[blk], sems.at[2 + blk])
-        )
-        loads[blk].start()
-    first.wait()
+    load.start()
+    tiles = block // LANES
+    for tile in range(tiles):
+        proj[tile, 0:RIM, :] = jnp.zeros((RIM, LANES), jnp.float32)
     main.wait()
-    for blk in range(n_blocks):
-        loads[blk].wait()
-        full = jnp.dot(ext[...], wbuf[blk], preferred_element_type=jnp.float32)
-        full = full.astype(jnp.bfloat16).astype(jnp.float32)
-        for t in range(width // LANES):
-            tile = blk * (width // LANES) + t
-            proj[tile] = full[:, t * LANES : (t + 1) * LANES]
-            coef = spread_taps(taps[:, :n_groups], group0 + tile * (LANES // group_size), group_size)
-            for row in range(0, n_tok, LANES):
-                feat = filtered(coef, lambda j: proj[tile, RIM + row - j : RIM + row - j + LANES, :], n_taps)
-                at = row % piece
-                pieces[row // piece, tile * LANES : (tile + 1) * LANES, at : at + LANES] = feat.T.astype(jnp.bfloat16)
+    load.wait()
+    full = jnp.dot(ext[...], wbuf[...], preferred_element_type=jnp.float32)
+    full = full.astype(jnp.bfloat16).astype(jnp.float32)
+    for tile in range(tiles):
+        proj[tile, RIM:, :] = full[:, tile * LANES : (tile + 1) * LANES]
+    for tile in range(tiles):
+        lanes = slice(tile * LANES, (tile + 1) * LANES)
+        coef = spread_taps(taps[:, :n_groups], group0 + tile * (LANES // group_size), group_size)
+        both = jnp.concatenate([proj[tile, RIM + n_tok - 8 :, :], proj[tile, RIM : RIM + 8, :]], axis=0)
+        ends[:, lanes] = both.astype(jnp.bfloat16)
+        for row in range(0, n_tok, LANES):
+            feat = filtered(coef, lambda j: proj[tile, RIM + row - j : RIM + row - j + LANES, :], n_taps)
+            at = row % piece
+            pieces[row // piece, lanes, at : at + LANES] = feat.T.astype(jnp.bfloat16)
     chip = lax.axis_index("chip")
     mine[...] = pieces[chip]
     other[...] = pieces[chip ^ 1]
 
 
-def make_query(group_size, rim, tokens, taps, weights, n_chips):
+def make_query(group_size, tokens, taps, weights, after, n_chips):
     n_tok, depth = tokens.shape
     block = weights.shape[2]
-    width = min(256, block)
     hbm = pl.BlockSpec(memory_space=pltpu.HBM)
     vmem = pl.BlockSpec(memory_space=pltpu.VMEM)
+    piece = (block, n_tok // n_chips)
     return pl.pallas_call(
         functools.partial(query_kernel, group_size),
-        out_shape=[jax.ShapeDtypeStruct((block, n_tok // n_chips), jnp.bfloat16)] * 2,
-        in_specs=[hbm, hbm, vmem, hbm],
-        out_specs=[vmem, vmem],
+        out_shape=[jax.ShapeDtypeStruct(shape, jnp.bfloat16) for shape in (piece, piece, (16, block))],
+        in_specs=[hbm, vmem, hbm, hbm],
+        out_specs=[vmem] * 3,
         scratch_shapes=[
-            pltpu.VMEM((n_chips, block, n_tok // n_chips), jnp.bfloat16),
-            pltpu.VMEM((RIM + n_tok, depth), jnp.bfloat16),
-            pltpu.VMEM((block // width, depth, width), jnp.bfloat16),
+            pltpu.VMEM((n_chips,) + piece, jnp.bfloat16),
+            pltpu.VMEM((n_tok, depth), jnp.bfloat16),
+            pltpu.VMEM((depth, block), jnp.bfloat16),
             pltpu.VMEM((block // LANES, RIM + n_tok, LANES), jnp.float32),
-            pltpu.SemaphoreType.DMA((2 + block // width,)),
+            pltpu.SemaphoreType.DMA((2,)),
         ],
         compiler_params=pltpu.CompilerParams(vmem_limit_bytes=56 * MIB),
         cost_estimate=pl.CostEstimate(
             flops=2 * n_tok * depth * block, bytes_accessed=2 * (n_tok * depth + depth * block), transcendentals=0
         ),
         name="query",
-    )(rim, tokens, taps, weights)
+    )(tokens, taps, weights, after)
+
+
+def fix_kernel(group_size, before, ends, taps, out):
+    n_taps, n_groups = taps.shape[0], taps.shape[1] // 3
+    block = out.shape[0]
+    group0 = fft_index() * (block // group_size)
+    for tile in range(block // LANES):
+        lanes = slice(tile * LANES, (tile + 1) * LANES)
+        coef = spread_taps(taps[:, :n_groups], group0 + tile * (LANES // group_size), group_size)
+        both = jnp.concatenate(
+            [before[:, lanes].astype(jnp.float32)[:8], ends[:, lanes].astype(jnp.float32)[8:]], axis=0
+        )
+        feat = filtered(coef, lambda j: both[8 - j : 16 - j, :], n_taps)
+        feat = jnp.concatenate([feat, jnp.zeros((LANES - 8, LANES), jnp.float32)], axis=0)
+        out[lanes, :] = feat.T.astype(jnp.bfloat16)
+
+
+def make_fix(group_size, before, ends, taps):
+    vmem = pl.BlockSpec(memory_space=pltpu.VMEM)
+    return pl.pallas_call(
+        functools.partial(fix_kernel, group_size),
+        out_shape=jax.ShapeDtypeStruct((ends.shape[1], LANES), jnp.bfloat16),
+        in_specs=[vmem] * 3,
+        out_specs=vmem,
+        compiler_params=pltpu.CompilerParams(vmem_limit_bytes=16 * MIB),
+        cost_estimate=pl.CostEstimate(flops=10**6, bytes_accessed=10**5, transcendentals=0),
+        name="fix",
+    )(before, ends, taps)
 
 
 def convolve_kernel(group_size, sizes, payload, taps, gain, out, lags, fixed, lagrow, held, total):
@@ -331,67 +369,119 @@
         ],
         compiler_params=pltpu.CompilerParams(vmem_limit_bytes=48 * MIB),
         cost_estimate=pl.CostEstimate(
-            flops=stretch * length**2, bytes_accessed=4 * payload.size, transcendentals=0
+            flops=CONVOLVE_FLOPS, bytes_accessed=4 * payload.size, transcendentals=0
         ),
         name="convolve",
     )(payload, taps, gain)
 
 
-def stage_kernel(w_near, w_far, out, sems):
-    copies = [pltpu.make_async_copy(w, out.at[k], sems.at[k]) for k, w in enumerate((w_near, w_far))]
-    for copy in copies:
-        copy.start()
-    for copy in copies:
-        copy.wait()
-
-
-def stage(w_near, w_far):
-    hbm = pl.BlockSpec(memory_space=pltpu.HBM)
-    return pl.pallas_call(
-        stage_kernel,
-        out_shape=pltpu.VMEM((2,) + w_near.shape, w_near.dtype),
-        in_specs=[hbm, hbm],
-        out_specs=pl.BlockSpec(memory_space=pltpu.VMEM),
-        scratch_shapes=[pltpu.SemaphoreType.DMA((2,))],
-        compiler_params=pltpu.CompilerParams(vmem_limit_bytes=16 * MIB),
-        cost_estimate=pl.CostEstimate(flops=STAGE_FLOPS, bytes_accessed=8 * w_near.size, transcendentals=0),
-        name="stage",
-    )(w_near, w_far)
-
-
-def output_kernel(other_core, q_near, q_far, conv, weights, out):
-    n_tok = out.shape[0]
-    chip = lax.axis_index("chip")
-    core = lax.axis_index("core") ^ other_core
-    at = pl.ds(pl.multiple_of(core * n_tok, LANES), n_tok)
-    gated = []
-    for k, query in enumerate((q_near, q_far)):
-        product = query[:, at].astype(jnp.float32) * conv[chip ^ k, :, at].astype(jnp.float32)
-        gated.append(product.T.astype(jnp.bfloat16))
-    width = out.shape[1]
-    step = min(512, width)
-    for col in range(0, width, step):
-        acc = jnp.dot(gated[0], weights[0, :, col : col + step], preferred_element_type=jnp.float32)
-        acc += jnp.dot(gated[1], weights[1, :, col : col + step], preferred_element_type=jnp.float32)
-        out[:, col : col + step] = acc.astype(out.dtype)
-
-
-def output_part(other_core, dtype, query, conv, weights):
+def arrived_kernel(kept, *refs):
+    refs[-1][...] = kept[...]
+
+
+def arrived(kept, *blocks):
+    vmem = pl.BlockSpec(memory_space=pltpu.VMEM)
+    return pl.pallas_call(
+        arrived_kernel,
+        out_shape=jax.ShapeDtypeStruct(kept.shape, kept.dtype),
+        in_specs=[vmem] + [pl.BlockSpec(memory_space=pltpu.HBM)] * len(blocks),
+        out_specs=vmem,
+        compiler_params=pltpu.CompilerParams(vmem_limit_bytes=ARRIVED_VMEM),
+        cost_estimate=pl.CostEstimate(flops=ARRIVED_FLOPS, bytes_accessed=0, transcendentals=0),
+        name="arrived",
+    )(kept, *blocks)
+
+
+def other_kernel(q_near, q_far, fix_near, fix_far, conv, w_near, mine, theirs, direct, other, wbuf, gated, sems):
+    n_tok, width = other.shape
+    block = w_near.shape[0]
+    part = mine.shape[0]
+    chip, core = lax.axis_index("chip"), lax.axis_index("core")
+    parity = lax.axis_index("ctx") % 2
+    loads = []
+    for n in range(wbuf.shape[0]):
+        columns = pl.ds(n * wbuf.shape[3], wbuf.shape[3])
+        pairs = [(w_near, wbuf.at[n, 0])]
+        for k, w in enumerate((mine, theirs)):
+            pairs.append((w, wbuf.at[n, 1, pl.ds(pl.multiple_of((parity ^ k) * part, part), part)]))
+        pairs.append((direct, wbuf.at[n, 1, pl.ds(2 * part, block - 2 * part)]))
+        loads.append(
+            [pltpu.make_async_copy(w.at[:, columns], to, sems.at[4 * n + i]) for i, (w, to) in enumerate(pairs)]
+        )
+    for step in loads:
+        for load in step:
+            load.start()
+    early = lax.broadcasted_iota(jnp.int32, (block, LANES), 1) < 8
+
+    def gate(k, half):
+        query, fix = ((q_near, fix_near), (q_far, fix_far))[k]
+        pieces = []
+        for t in range(0, n_tok, LANES):
+            at = pl.ds(pl.multiple_of((core ^ half) * n_tok + t, LANES), LANES)
+            values = query[:, at].astype(jnp.float32)
+            if t == 0:
+                first = jnp.logical_and(early, jnp.logical_and(chip == 0, core == half))
+                values = jnp.where(first, fix[...].astype(jnp.float32), values)
+            product = values * conv[chip ^ k, :, at].astype(jnp.float32)
+            pieces.append(product.T.astype(jnp.bfloat16))
+        return pieces[0] if len(pieces) == 1 else jnp.concatenate(pieces, axis=0)
+
+    theirs_gated = [gate(k, 1) for k in range(2)]
+    for k in range(2):
+        gated[k] = gate(k, 0)
+    for n, step in enumerate(loads):
+        for load in step:
+            load.wait()
+        acc = jnp.dot(theirs_gated[0], wbuf[n, 0], preferred_element_type=jnp.float32)
+        acc += jnp.dot(theirs_gated[1], wbuf[n, 1], preferred_element_type=jnp.float32)
+        other[:, n * wbuf.shape[3] : (n + 1) * wbuf.shape[3]] = acc.astype(other.dtype)
+
+
+def other_part(query, fixes, conv, weights):
     _, block, n_tok = conv.shape
     n_tok //= 2
-    width = weights.shape[2]
-    vmem = pl.BlockSpec(memory_space=pltpu.VMEM)
-    return pl.pallas_call(
-        functools.partial(output_kernel, other_core),
-        out_shape=jax.ShapeDtypeStruct((n_tok, width), dtype),
-        in_specs=[vmem] * 4,
+    width = weights[0].shape[1]
+    step = width // 2
+    vmem = pl.BlockSpec(memory_space=pltpu.VMEM)
+    hbm = pl.BlockSpec(memory_space=pltpu.HBM)
+    shapes = (n_tok, width), (width // step, 2, block, step), (2, n_tok, block)
+    return pl.pallas_call(
+        other_kernel,
+        out_shape=[jax.ShapeDtypeStruct(shape, jnp.bfloat16) for shape in shapes],
+        in_specs=[vmem] * 5 + [hbm] * 4,
+        out_specs=[vmem] * 3,
+        scratch_shapes=[pltpu.SemaphoreType.DMA((4 * (width // step),))],
+        compiler_params=pltpu.CompilerParams(vmem_limit_bytes=OUTPUT_VMEM),
+        cost_estimate=pl.CostEstimate(
+            flops=4 * block * n_tok * width, bytes_accessed=4 * block * width, transcendentals=0
+        ),
+        name="other_part",
+    )(*query, *fixes, conv, *weights)
+
+
+def own_kernel(gated, weights, out):
+    step = weights.shape[3]
+    for n in range(weights.shape[0]):
+        acc = jnp.dot(gated[0], weights[n, 0], preferred_element_type=jnp.float32)
+        acc += jnp.dot(gated[1], weights[n, 1], preferred_element_type=jnp.float32)
+        out[:, n * step : (n + 1) * step] = acc
+
+
+def own_part(gated, weights):
+    n_steps, _, block, step = weights.shape
+    n_tok = gated.shape[1]
+    vmem = pl.BlockSpec(memory_space=pltpu.VMEM)
+    return pl.pallas_call(
+        own_kernel,
+        out_shape=jax.ShapeDtypeStruct((n_tok, n_steps * step), jnp.float32),
+        in_specs=[vmem] * 2,
         out_specs=vmem,
         compiler_params=pltpu.CompilerParams(vmem_limit_bytes=24 * MIB),
         cost_estimate=pl.CostEstimate(
-            flops=4 * block * n_tok * width, bytes_accessed=4 * block * width, transcendentals=0
+            flops=4 * block * n_tok * n_steps * step, bytes_accessed=2 * weights.size, transcendentals=0
         ),
-        name="output_part",
-    )(*query, conv, weights)
+        name="own_part",
+    )(gated, weights)
 
 
 def body(tokens, w_in, short_taps, long_filter, skip_gain, w_out):
@@ -404,27 +494,28 @@
     piece = tok_len // n_chips
 
     weights = w_in.transpose(1, 0, 2)
-    across = swapped(w_out, "chip")
-    sent = mix(group_size, tokens, short_taps, weights, long_filter, n_ctx)
+    part = block // 8 * 3
+    shared = lax.dynamic_slice_in_dim(w_out, lax.axis_index("ctx") % 2 * part, part, 0)
+    mine = swapped(shared, "chip")
+    theirs = swapped(mine, "ctx")
+    sent, direct = mix(group_size, tokens, short_taps, weights, long_filter, w_out, block - 2 * part, n_ctx)
+    direct = swapped(direct, "chip")
     payload = lax.all_to_all(sent, "ctx", 0, 0, tiled=True)
 
-    ends, _ = lax.optimization_barrier((tokens[tok_len - RIM :], sent))
-    rim = passed_along(ends, "ctx", 1)
-    rim, conv_taps = lax.optimization_barrier((rim, short_taps))
+    near, far, ends = make_query(group_size, tokens, short_taps, weights, sent, n_chips)
+    far = swapped(far, "chip")
+    before = passed_along(ends, "ctx", 1)
 
     gain = lax.dynamic_slice_in_dim(skip_gain, fft_index() * block + lax.axis_index("ctx") * stretch, stretch, 0)
-    conv = convolve(group_size, span, stretch, payload, conv_taps, gain[:, None], n_chips)
-
-    rim, query_taps, _ = lax.optimization_barrier((rim, short_taps, conv))
-    near, far = make_query(group_size, rim, tokens, query_taps, weights, n_chips)
-    query = (near, swapped(far, "chip"))
+    conv = convolve(group_size, span, stretch, payload, short_taps, arrived(gain[:, None], mine, ends), n_chips)
+    fix = make_fix(group_size, before, arrived(ends, far, conv), short_taps)
     conv = lax.all_to_all(conv.reshape(n_chips * n_ctx, stretch, piece), ("chip", "ctx"), 0, 0, tiled=True)
     conv = conv.reshape(n_chips, block, piece)
 
-    out_weights = stage(w_out, across)
-    beside = swapped(output_part(1, jnp.bfloat16, query, conv, out_weights), "core")
-    total = output_part(0, jnp.float32, query, conv, out_weights)
-    return (total + beside.astype(jnp.float32)).astype(jnp.bfloat16)
+    fixes = (arrived(fix, theirs, direct), swapped(fix, "chip"))
+    other, staged, gated = other_part((near, far), fixes, conv, (w_out, mine, theirs, direct))
+    other = swapped(other, "core")
+    return (own_part(gated, staged) + other.astype(jnp.float32)).astype(jnp.bfloat16)
 
 
 def solution(mesh):

time: 66.4 us -> 62.8 us (0.946)
  waiting for transfers between devices: 21.5 us -> 14.8 us
  starting transfers between devices: 19 us -> 22.6 us
  local copies, waits for them, and re-layouts: 5.18 us -> 2.12 us
  Pallas kernels: 19.2 us -> 21.6 us
    all_to_all x1, waiting for transfers between devices: 8.83 us -> 1.6 us  [body(): payload = lax.all_to_all(sent, 'ctx', 0, 0, tiled=True)]
    all_to_all x1, waiting for transfers between devices: 0.01 us -> 4.08 us  [body(): lax.all_to_all(conv.reshape(n_chips * n_ctx, stretch, piece), ('chip', 'c...]
    pallas_call x4 -> x7, Pallas kernels: 9.25 us -> 12.7 us  [the longest x1 7.57 us: mix(): pl.pallas_call(functools.partial(mix_kernel, group_size), out_shape=[jax....]
    unnamed x14 -> x12, local copies, waits for them, and re-layouts: 4.16 us -> 0.74 us
    ppermute x3 -> x6, starting transfers between devices: 5.05 us -> 8 us  [swapped(): lax.ppermute(block, axis, [(i, i ^ 1) for i in range(lax.axis_size(axis))])]
    ppermute x1, waiting for transfers between devices: 1.84 us -> 0.01 us  [passed_along(): return lax.ppermute(block, axis, route)]
    ppermute x3 -> x6, waiting for transfers between devices: 10.8 us -> 9.15 us  [swapped(): lax.ppermute(block, axis, [(i, i ^ 1) for i in range(lax.axis_size(axis))])]
    dynamic_slice x0 -> x1, local copies, waits for them, and re-layouts: none -> 1.21 us  [body(): lax.dynamic_slice_in_dim(w_out, lax.axis_index('ctx') % 2 * part, part, 0)]
  transfers between devices with their start and end apart: 6 -> 9, of which waited for: 5 -> 4; matrix products, arithmetic and copies ran while one was open for 2% -> 0% of each run, Pallas kernels for 28% -> 29%
where the time goes in v3:
time: 62.8 us; the launch traced here: 62.1 us
  starting transfers between devices  22.6 us (36%)
  Pallas kernels  21.6 us (34%)
  waiting for transfers between devices  14.8 us (24%)
  local copies, waits for them, and re-layouts  2.12 us (3%)
  other arithmetic  0.9 us (1%)
    ppermute x6, waiting for transfers between devices, swapped(): lax.ppermute(block, axis, [(i, i ^ 1) for i in range(lax.axis_size(axis))])  9.15 us
    ppermute x6, starting transfers between devices, swapped(): lax.ppermute(block, axis, [(i, i ^ 1) for i in range(lax.axis_size(axis))])  8 us
    pallas_call x1, Pallas kernels, mix(): pl.pallas_call(functools.partial(mix_kernel, group_size), out_shape=[jax....  7.57 us
    all_to_all x1, starting transfers between devices, body(): payload = lax.all_to_all(sent, 'ctx', 0, 0, tiled=True)  5.82 us
    pallas_call x1, Pallas kernels, make_query(): pl.pallas_call(functools.partial(query_kernel, group_size), out_shape=[ja...  5.55 us
    ppermute x1, starting transfers between devices, passed_along(): return lax.ppermute(block, axis, route)  4.53 us
    all_to_all x1, starting transfers between devices, body(): lax.all_to_all(conv.reshape(n_chips * n_ctx, stretch, piece), ('chip', 'c...  4.23 us
    all_to_all x1, waiting for transfers between devices, body(): lax.all_to_all(conv.reshape(n_chips * n_ctx, stretch, piece), ('chip', 'c...  4.08 us
  transfers between devices with their start and end apart: 9, of which 4 were waited for; matrix products, arithmetic and copies ran while one was open for 0% of the time, Pallas kernels for 29%

profile of v3, /device:TPU:0, one launch (start us, length us, event | category | flops | bytes accessed | tf_op | source)
XLA Modules:
  0.0 62.1 jit_solution(7385361391744773264)
XLA Ops:
  0.0 0.0 copy-start
  0.0 1.2 %constant_dynamic-slice_fusion = bf16[192,2048]{1,0:T(8,128)(2,1)S(1)} fusion(bf16[512,2048]{1,0:T(8,128)(2,1)} %w_near.1, s32[]{:T(128)S(6)} %select_n.15), kind=kLoop, calls=%fused_computation.2 | loop fusion | bytes 1572868 | tf_op jit(solution)/shard_map/dynamic_slice | solution.py:498
  1.2 3.0 %collective-permute-start.2 = (bf16[192,2048]{1,0:T(8,128)(2,1)S(1)}, bf16[192,2048]{1,0:T(8,128)(2,1)}, u32[]{:S(2)}, u32[]{:S(2)}) collective-permute-start(bf16[192,2048]{1,0:T(8,128)(2,1)S(1)} %constant_dynamic-slice_fusion), channel_id=1, source_target_pairs={{0,2},{2,0},{1,3},{3,1},{4,6},{6,4},{5,7},{7,5},{8,10},{10,8},{9,1... | collective-permute-start | bytes 2359304 | tf_op jit(solution)/shard_map/ppermute | solution.py:31
  4.3 7.6 %mix.1 = (bf16[8,72,512]{2,1,0:T(8,128)(2,1)}, bf16[128,2048]{1,0:T(8,128)(2,1)}) custom-call(bf16[512,2048]{1,0:T(8,128)(2,1)} %tokens.3, f32[7,384]{1,0:T(8,128)} %taps.7, bf16[3,2048,512]{2,1,0:T(8,128)(2,1)} %bitcast.5, f32[512,128]{1,0:T(8,128)} %filt.1, bf16[512,2048]{1,0:T(8,128)(2,1)} %w_near.1), custom_call_target="tpu_custom_call" | custom-call | flops 2147483648 | bytes 6291456 | tf_op jit(solution)/shard_map/mix/pallas_call | solution.py:149
  11.8 5.8 %all-to-all-start = ((bf16[8,72,512]{2,1,0:T(8,128)(2,1)}), bf16[8,72,512]{2,1,0:T(8,128)(2,1)S(1)}, u32[]{:S(2)}, u32[]{:S(2)}) async-start(bf16[8,72,512]{2,1,0:T(8,128)(2,1)} %get-tuple-element.13.after), calls=%async_computation | async-start | bytes 1179648 | tf_op jit(solution)/shard_map/all_to_all | solution.py:503
  17.7 0.5 collective-permute-start.4
  18.2 5.5 %query.1 = (bf16[512,256]{1,0:T(8,128)(2,1)}, bf16[512,256]{1,0:T(8,128)(2,1)}, bf16[16,512]{1,0:T(8,128)(2,1)}) custom-call(bf16[512,2048]{1,0:T(8,128)(2,1)} %tokens.3, f32[7,384]{1,0:T(8,128)} %taps.7, bf16[3,2048,512]{2,1,0:T(8,128)(2,1)} %bitcast.6, bf16[8,72,512]{2,1,0:T(8,128)(2,1)} %get-tuple-element.13.after), custom_call_target="tpu_custom_call" | custom-call | flops 1073741824 | bytes 4194304 | tf_op jit(solution)/shard_map/query/pallas_call | solution.py:210
  23.7 4.5 %collective-permute-start.1 = (bf16[16,512]{1,0:T(8,128)(2,1)}, bf16[16,512]{1,0:T(8,128)(2,1)}, u32[]{:S(2)}, u32[]{:S(2)}) collective-permute-start(bf16[16,512]{1,0:T(8,128)(2,1)} %get-tuple-element.16.refs_1_.kept), channel_id=1, source_target_pairs={{0,4},{4,8},{8,12},{12,16},{16,20},{20,24},{24,28},{1,5},{5,9},{9,... | collective-permute-start | bytes 49160 | tf_op jit(solution)/shard_map/ppermute | solution.py:27
  28.2 1.5 %collective-permute-start = (bf16[512,256]{1,0:T(8,128)(2,1)}, bf16[512,256]{1,0:T(8,128)(2,1)S(1)}, u32[]{:S(2)}, u32[]{:S(2)}) collective-permute-start(bf16[512,256]{1,0:T(8,128)(2,1)} %get-tuple-element.15), channel_id=1, source_target_pairs={{0,2},{2,0},{1,3},{3,1},{4,6},{6,4},{5,7},{7,5},{8,10},{10,8},{9,1... | collective-permute-start | bytes 786440 | tf_op jit(solution)/shard_map/ppermute | solution.py:31
  29.8 0.0 copy-done
  29.8 0.1 dynamic-slice_bitcast_fusion
  29.9 0.1 copy.7.kept
  30.0 0.0 copy-start.3
  30.0 0.0 collective-permute-done.2.refs_0_.mine
  30.0 1.0 %collective-permute-start.3 = (bf16[192,2048]{1,0:T(8,128)(2,1)}, bf16[192,2048]{1,0:T(8,128)(2,1)}, u32[]{:S(2)}, u32[]{:S(2)}) collective-permute-start(bf16[192,2048]{1,0:T(8,128)(2,1)} %collective-permute-done.2.refs_0_.mine), channel_id=1, source_target_pairs={{0,4},{4,0},{8,12},{12,8},{16,20},{20,16},{24,28},{28,24},{1,5},{5... | collective-permute-start | bytes 2359304 | tf_op jit(solution)/shard_map/ppermute | solution.py:31
  31.0 0.0 copy-start.4
  31.0 0.7 %copy-done.4 = bf16[16,512]{1,0:T(8,128)(2,1)S(1)} copy-done((bf16[16,512]{1,0:T(8,128)(2,1)S(1)}, bf16[16,512]{1,0:T(8,128)(2,1)}, u32[]{:S(2)}) %copy-start.4) | copy-done | bytes 16408
  31.7 0.0 copy-start.5
  31.7 1.6 %all-to-all-done.payload = bf16[8,72,512]{2,1,0:T(8,128)(2,1)S(1)} async-done(((bf16[8,72,512]{2,1,0:T(8,128)(2,1)}), bf16[8,72,512]{2,1,0:T(8,128)(2,1)S(1)}, u32[]{:S(2)}, u32[]{:S(2)}) %all-to-all-start) | async-done | bytes 589856 | tf_op jit(solution)/shard_map/all_to_all | solution.py:503
  33.3 0.0 copy-done.3
  33.3 3.3 %convolve.1.refs_1_ = bf16[2,8,64,256]{3,2,1,0:T(8,128)(2,1)} custom-call(bf16[8,72,512]{2,1,0:T(8,128)(2,1)S(1)} %all-to-all-done.payload, f32[7,384]{1,0:T(8,128)S(1)} %copy-done.3, f32[64,1]{1,0:T(8,128)S(1)} %arrived.3.gain), custom_call_target="tpu_custom_call" | custom-call | flops 10000000000 | bytes 1179648 | tf_op jit(solution)/shard_map/convolve/pallas_call | solution.py:358
  36.6 4.2 %all-to-all-start.1 = ((bf16[16,64,256]{2,1,0:T(8,128)(2,1)}), bf16[16,64,256]{2,1,0:T(8,128)(2,1)}, u32[]{:S(2)}, u32[]{:S(2)}) async-start(bf16[16,64,256]{2,1,0:T(8,128)(2,1)} %bitcast.2), calls=%async_computation.1 | async-start | bytes 1048576 | tf_op jit(solution)/shard_map/all_to_all | solution.py:512
  40.9 0.0 collective-permute-done.refs_0_.q_far
  40.9 0.0 copy-done.5
  40.9 0.0 collective-permute-done.1.before
  40.9 1.0 %fix.1.kept = bf16[512,128]{1,0:T(8,128)(2,1)S(1)} custom-call(bf16[16,512]{1,0:T(8,128)(2,1)} %collective-permute-done.1.before, bf16[16,512]{1,0:T(8,128)(2,1)S(1)} %arrived.4.ends, f32[7,384]{1,0:T(8,128)S(1)} %copy-done.3), custom_call_target="tpu_custom_call" | custom-call | flops 1000000 | bytes 100000 | tf_op jit(solution)/shard_map/fix/pallas_call | solution.py:247
  41.9 0.0 copy-start.1
  41.9 0.0 copy-start.2
  41.9 1.9 %collective-permute-start.5 = (bf16[512,128]{1,0:T(8,128)(2,1)S(1)}, bf16[512,128]{1,0:T(8,128)(2,1)S(1)}, u32[]{:S(2)}, u32[]{:S(2)}) collective-permute-start(bf16[512,128]{1,0:T(8,128)(2,1)S(1)} %fix.1.kept), channel_id=1, source_target_pairs={{0,2},{2,0},{1,3},{3,1},{4,6},{6,4},{5,7},{7,5},{8,10},{10,8},{9,1... | collective-permute-start | bytes 393224 | tf_op jit(solution)/shard_map/ppermute | solution.py:31
  43.8 0.0 collective-permute-done.4.refs_1_.direct
  43.8 8.0 %collective-permute-done.3.refs_0_.theirs = bf16[192,2048]{1,0:T(8,128)(2,1)} collective-permute-done((bf16[192,2048]{1,0:T(8,128)(2,1)}, bf16[192,2048]{1,0:T(8,128)(2,1)}, u32[]{:S(2)}, u32[]{:S(2)}) %collective-permute-start.3) | collective-permute-done | bytes 786464 | tf_op jit(solution)/shard_map/ppermute | solution.py:31
  51.7 0.0 collective-permute-done.5.fix_far
  51.7 4.1 %all-to-all-done.1 = bf16[16,64,256]{2,1,0:T(8,128)(2,1)} async-done(((bf16[16,64,256]{2,1,0:T(8,128)(2,1)}), bf16[16,64,256]{2,1,0:T(8,128)(2,1)}, u32[]{:S(2)}, u32[]{:S(2)}) %all-to-all-start.1) | async-done | bytes 524320 | tf_op jit(solution)/shard_map/all_to_all | solution.py:512
  55.8 0.0 copy-done.1
  55.8 0.0 copy-done.2
  55.8 3.4 %other_part.1 = (bf16[128,2048]{1,0:T(8,128)(2,1)S(1)}, bf16[2,2,512,1024]{3,2,1,0:T(8,128)(2,1)S(1)}, bf16[2,128,512]{2,1,0:T(8,128)(2,1)S(1)}) custom-call(bf16[512,256]{1,0:T(8,128)(2,1)S(1)} %copy-done.2, bf16[512,256]{1,0:T(8,128)(2,1)S(1)} %collective-permute-done.refs_0_.q_far, bf16[512,128]{1,0:T(8,128)(2,1)S(1)} %arrived.5.fix_near, ...), custom_call_target="tpu_custom_call" | custom-call | flops 536870912 | bytes 4194304 | tf_op jit(solution)/shard_map/other_part/pallas_call | solution.py:448
  59.3 0.1 collective-permute-start.6
  59.3 0.7 %own_part.1 = f32[128,2048]{1,0:T(8,128)S(1)} custom-call(bf16[2,128,512]{2,1,0:T(8,128)(2,1)S(1)} %get-tuple-element.18.gated, bf16[2,2,512,1024]{3,2,1,0:T(8,128)(2,1)S(1)} %get-tuple-element.19.weights), custom_call_target="tpu_custom_call" | custom-call | flops 536870912 | bytes 4194304 | tf_op jit(solution)/shard_map/own_part/pallas_call | solution.py:474
  60.1 1.2 %collective-permute-done.6 = bf16[128,2048]{1,0:T(8,128)(2,1)S(1)} collective-permute-done((bf16[128,2048]{1,0:T(8,128)(2,1)S(1)}, bf16[128,2048]{1,0:T(8,128)(2,1)S(1)}, u32[]{:S(2)}, u32[]{:S(2)}) %collective-permute-start.6) | collective-permute-done | bytes 524320 | tf_op jit(solution)/shard_map/ppermute | solution.py:31
  61.2 0.9 %add_convert_fusion = bf16[128,2048]{1,0:T(8,128)(2,1)} fusion(f32[128,2048]{1,0:T(8,128)S(1)} %own_part.1, bf16[128,2048]{1,0:T(8,128)(2,1)S(1)} %collective-permute-done.6), kind=kLoop, calls=%fused_computation | loop fusion | flops 786432 | bytes 2097152 | tf_op jit(solution)/shard_map/convert_element_type | solution.py:518
  (3 shorter events, 0.0 us)
Async XLA Ops:
  0.0 29.8 %copy-start = (f32[2048]{0:T(1024)S(1)}, f32[2048]{0:T(1024)}, u32[]{:S(2)}) copy-start(f32[2048]{0:T(1024)} %param.10) | copy-start | bytes 24580
  1.2 28.7 %collective-permute-start.2 = (bf16[192,2048]{1,0:T(8,128)(2,1)S(1)}, bf16[192,2048]{1,0:T(8,128)(2,1)}, u32[]{:S(2)}, u32[]{:S(2)}) collective-permute-start(bf16[192,2048]{1,0:T(8,128)(2,1)S(1)} %constant_dynamic-slice_fusion), channel_id=1, source_target_pairs={{0,2},{2,0},{1,3},{3,1},{4,6},{6,4},{5,7},{7,5},{8,10},{10,8},{9,1... | collective-permute-start | bytes 2359304 | tf_op jit(solution)/shard_map/ppermute | solution.py:31
  11.8 21.5 %all-to-all-start = ((bf16[8,72,512]{2,1,0:T(8,128)(2,1)}), bf16[8,72,512]{2,1,0:T(8,128)(2,1)S(1)}, u32[]{:S(2)}, u32[]{:S(2)}) async-start(bf16[8,72,512]{2,1,0:T(8,128)(2,1)} %get-tuple-element.13.after), calls=%async_computation | async-start | bytes 1179648 | tf_op jit(solution)/shard_map/all_to_all | solution.py:503
  17.7 26.1 %collective-permute-start.4 = (bf16[128,2048]{1,0:T(8,128)(2,1)}, bf16[128,2048]{1,0:T(8,128)(2,1)}, u32[]{:S(2)}, u32[]{:S(2)}) collective-permute-start(bf16[128,2048]{1,0:T(8,128)(2,1)} %get-tuple-element.17), channel_id=1, source_target_pairs={{0,2},{2,0},{1,3},{3,1},{4,6},{6,4},{5,7},{7,5},{8,10},{10,8},{9,1... | collective-permute-start | bytes 1572872 | tf_op jit(solution)/shard_map/ppermute | solution.py:31
  23.7 17.2 %collective-permute-start.1 = (bf16[16,512]{1,0:T(8,128)(2,1)}, bf16[16,512]{1,0:T(8,128)(2,1)}, u32[]{:S(2)}, u32[]{:S(2)}) collective-permute-start(bf16[16,512]{1,0:T(8,128)(2,1)} %get-tuple-element.16.refs_1_.kept), channel_id=1, source_target_pairs={{0,4},{4,8},{8,12},{12,16},{16,20},{20,24},{24,28},{1,5},{5,9},{9,... | collective-permute-start | bytes 49160 | tf_op jit(solution)/shard_map/ppermute | solution.py:27
  28.2 12.6 %collective-permute-start = (bf16[512,256]{1,0:T(8,128)(2,1)}, bf16[512,256]{1,0:T(8,128)(2,1)S(1)}, u32[]{:S(2)}, u32[]{:S(2)}) collective-permute-start(bf16[512,256]{1,0:T(8,128)(2,1)} %get-tuple-element.15), channel_id=1, source_target_pairs={{0,2},{2,0},{1,3},{3,1},{4,6},{6,4},{5,7},{7,5},{8,10},{10,8},{9,1... | collective-permute-start | bytes 786440 | tf_op jit(solution)/shard_map/ppermute | solution.py:31
  30.0 3.3 %copy-start.3 = (f32[7,384]{1,0:T(8,128)S(1)}, f32[7,384]{1,0:T(8,128)}, u32[]{:S(2)}) copy-start(f32[7,384]{1,0:T(8,128)} %taps.7) | copy-start | bytes 32260
  30.0 21.8 %collective-permute-start.3 = (bf16[192,2048]{1,0:T(8,128)(2,1)}, bf16[192,2048]{1,0:T(8,128)(2,1)}, u32[]{:S(2)}, u32[]{:S(2)}) collective-permute-start(bf16[192,2048]{1,0:T(8,128)(2,1)} %collective-permute-done.2.refs_0_.mine), channel_id=1, source_target_pairs={{0,4},{4,0},{8,12},{12,8},{16,20},{20,16},{24,28},{28,24},{1,5},{5... | collective-permute-start | bytes 2359304 | tf_op jit(solution)/shard_map/ppermute | solution.py:31
  31.0 0.7 %copy-start.4 = (bf16[16,512]{1,0:T(8,128)(2,1)S(1)}, bf16[16,512]{1,0:T(8,128)(2,1)}, u32[]{:S(2)}) copy-start(bf16[16,512]{1,0:T(8,128)(2,1)} %get-tuple-element.16.refs_1_.kept) | copy-start | bytes 49156
  31.7 9.2 %copy-start.5 = (bf16[16,512]{1,0:T(8,128)(2,1)S(1)}, bf16[16,512]{1,0:T(8,128)(2,1)}, u32[]{:S(2)}) copy-start(bf16[16,512]{1,0:T(8,128)(2,1)} %get-tuple-element.16.refs_1_.kept) | copy-start | bytes 49156
  36.6 19.2 %all-to-all-start.1 = ((bf16[16,64,256]{2,1,0:T(8,128)(2,1)}), bf16[16,64,256]{2,1,0:T(8,128)(2,1)}, u32[]{:S(2)}, u32[]{:S(2)}) async-start(bf16[16,64,256]{2,1,0:T(8,128)(2,1)} %bitcast.2), calls=%async_computation.1 | async-start | bytes 1048576 | tf_op jit(solution)/shard_map/all_to_all | solution.py:512
  41.9 13.9 %copy-start.1 = (bf16[512,2048]{1,0:T(8,128)(2,1)S(1)}, bf16[512,2048]{1,0:T(8,128)(2,1)}, u32[]{:S(2)}) copy-start(bf16[512,2048]{1,0:T(8,128)(2,1)} %w_near.1) | copy-start | bytes 6291460
  41.9 13.9 %copy-start.2 = (bf16[512,256]{1,0:T(8,128)(2,1)S(1)}, bf16[512,256]{1,0:T(8,128)(2,1)}, u32[]{:S(2)}) copy-start(bf16[512,256]{1,0:T(8,128)(2,1)} %get-tuple-element.14.q_near) | copy-start | bytes 786436
  41.9 9.8 %collective-permute-start.5 = (bf16[512,128]{1,0:T(8,128)(2,1)S(1)}, bf16[512,128]{1,0:T(8,128)(2,1)S(1)}, u32[]{:S(2)}, u32[]{:S(2)}) collective-permute-start(bf16[512,128]{1,0:T(8,128)(2,1)S(1)} %fix.1.kept), channel_id=1, source_target_pairs={{0,2},{2,0},{1,3},{3,1},{4,6},{6,4},{5,7},{7,5},{8,10},{10,8},{9,1... | collective-permute-start | bytes 393224 | tf_op jit(solution)/shard_map/ppermute | solution.py:31
  59.3 2.0 %collective-permute-start.6 = (bf16[128,2048]{1,0:T(8,128)(2,1)S(1)}, bf16[128,2048]{1,0:T(8,128)(2,1)S(1)}, u32[]{:S(2)}, u32[]{:S(2)}) collective-permute-start(bf16[128,2048]{1,0:T(8,128)(2,1)S(1)} %get-tuple-element.20), channel_id=1, source_target_pairs={{0,1},{1,0},{2,3},{3,2},{4,5},{5,4},{6,7},{7,6},{8,9},{9,8},{10,11... | collective-permute-start | bytes 1572872 | tf_op jit(solution)/shard_map/ppermute | solution.py:31

commit v4 on v3

--- a/solution.py
+++ b/solution.py
@@ -298,53 +298,66 @@
                 lagrow[g : g + 1, at : at + 2 * LANES] = piece_rows[g * per_lag + h : g * per_lag + h + 1, :]
     zeros = jnp.zeros((1, LANES), jnp.float32)
 
-    def lag_block(d):
+    def lag_block(g, d):
         if static:
             at = d * LAG
-            return jnp.concatenate([lags[:, at + LANES : at + LANES + LAG], lags[:, at : at + LAG]], axis=0)
+            return jnp.concatenate([lags[g, :, at + LANES : at + LANES + LAG], lags[g, :, at : at + LAG]], axis=0)
         at = pl.multiple_of(d * LAG, LAG)
-        near = lags[:, pl.ds(pl.multiple_of(at + LANES, LANES), LAG)]
-        return jnp.concatenate([near, lags[:, pl.ds(at, LAG)]], axis=0)
-
-    for g in range(stretch // span):
+        near = lags[g, :, pl.ds(pl.multiple_of(at + LANES, LANES), LAG)]
+        return jnp.concatenate([near, lags[g, :, pl.ds(at, LAG)]], axis=0)
+
+    n_spans = stretch // span
+
+    def prepare(g):
         row = jnp.concatenate([zeros, lagrow[g : g + 1, :], zeros], axis=1)
         wide = jnp.broadcast_to(row, (LANES, length + 2 * LANES))
         turned = pltpu.roll(wide, 0, 1, stride=1, stride_axis=0)
-        lags[...] = turned[:, : length + LANES].astype(jnp.bfloat16)
+        lags[g] = turned[:, : length + LANES].astype(jnp.bfloat16)
         chans = slice(g * span, (g + 1) * span)
         if rows != span or lead:
-            held[...] = jnp.zeros_like(held)
+            held[g] = jnp.zeros(held.shape[1:], held.dtype)
         for i in range(n_blocks):
             s = i // per_src
             part = payload[s, chans, (i % per_src) * LAG : (i % per_src + 1) * LAG]
             at = lead + i * rows
-            held[at : at + span, :] = part
+            held[g, at : at + span, :] = part
             if i % per_src == 0:
                 patch = fixed[chans, s // 16 * LANES : (s // 16 + 1) * LANES]
                 if s % 16:
                     patch = pltpu.roll(patch, LANES - s % 16 * 8, 1)
                 patched = jnp.where(lane < 8, patch, part[:, :LANES].astype(jnp.float32))
-                held[at : at + span, :LANES] = patched.astype(jnp.bfloat16)
+                held[g, at : at + span, :LANES] = patched.astype(jnp.bfloat16)
+
+    def multiply(g):
         if static:
-            total[...] = jnp.dot(held[...], lag_block(0), preferred_element_type=jnp.float32)
+            total[g] = jnp.dot(held[g], lag_block(g, 0), preferred_element_type=jnp.float32)
             for d in range(1, n_blocks):
-                part = jnp.dot(held[: size - d * rows, :], lag_block(d), preferred_element_type=jnp.float32)
-                total[d * rows :, :] += part
+                part = jnp.dot(held[g, : size - d * rows, :], lag_block(g, d), preferred_element_type=jnp.float32)
+                total[g, d * rows :, :] += part
         else:
-            total[...] = jnp.zeros_like(total)
+            total[g] = jnp.zeros(total.shape[1:], total.dtype)
 
             @pl.loop(0, n_blocks)
             def _(d):
-                shifted = held[pl.ds(pl.multiple_of(size - d * rows, rows), size), :]
-                total[...] += jnp.dot(shifted, lag_block(d), preferred_element_type=jnp.float32)
-
+                shifted = held[g, pl.ds(pl.multiple_of(size - d * rows, rows), size), :]
+                total[g] += jnp.dot(shifted, lag_block(g, d), preferred_element_type=jnp.float32)
+
+    def store(g):
+        chans = slice(g * span, (g + 1) * span)
         for i in range(n_blocks):
             at = lead + i * rows
-            direct = gain[chans, :] * held[at : at + span, :].astype(jnp.float32)
-            both = (total[i * rows : i * rows + span, :] + direct).astype(jnp.bfloat16)
+            direct = gain[chans, :] * held[g, at : at + span, :].astype(jnp.float32)
+            both = (total[g, i * rows : i * rows + span, :] + direct).astype(jnp.bfloat16)
             for h in range(pieces):
                 at = i * pieces + h
                 out[at % n_chips, at // n_chips, chans, :] = both[:, h * piece : (h + 1) * piece]
+
+    prepare(0)
+    for g in range(n_spans):
+        if g + 1 < n_spans:
+            prepare(g + 1)
+        multiply(g)
+        store(g)
 
 
 def convolve(group_size, span, stretch, payload, taps, gain, n_chips):
@@ -353,6 +366,7 @@
     rows = max(span, 16)
     size = n_blocks * rows
     length = n_src * cols
+    spans = stretch // span
     held = size if n_blocks <= 16 else 2 * size
     vmem = pl.BlockSpec(memory_space=pltpu.VMEM)
     return pl.pallas_call(
@@ -361,11 +375,11 @@
         in_specs=[vmem, vmem, vmem],
         out_specs=vmem,
         scratch_shapes=[
-            pltpu.VMEM((LANES, length + LANES), jnp.bfloat16),
+            pltpu.VMEM((spans, LANES, length + LANES), jnp.bfloat16),
             pltpu.VMEM((LANES, -(-n_src // 16) * LANES), jnp.float32),
             pltpu.VMEM((8, length), jnp.float32),
-            pltpu.VMEM((held, LAG), jnp.bfloat16),
-            pltpu.VMEM((size, LAG), jnp.float32),
+            pltpu.VMEM((spans, held, LAG), jnp.bfloat16),
+            pltpu.VMEM((spans, size, LAG), jnp.float32),
         ],
         compiler_params=pltpu.CompilerParams(vmem_limit_bytes=48 * MIB),
         cost_estimate=pl.CostEstimate(

time: 62.8 us -> 62.5 us (level)
  no operation moved by 1% of the time
where the time goes in v4:
time: 62.5 us; the launch traced here: 61.9 us
  starting transfers between devices  22.6 us (36%)
  Pallas kernels  21.4 us (34%)
  waiting for transfers between devices  14.8 us (24%)
  local copies, waits for them, and re-layouts  2.12 us (3%)
  other arithmetic  0.9 us (1%)
    ppermute x6, waiting for transfers between devices, swapped(): lax.ppermute(block, axis, [(i, i ^ 1) for i in range(lax.axis_size(axis))])  9.39 us
    ppermute x6, starting transfers between devices, swapped(): lax.ppermute(block, axis, [(i, i ^ 1) for i in range(lax.axis_size(axis))])  8 us
    pallas_call x1, Pallas kernels, mix(): pl.pallas_call(functools.partial(mix_kernel, group_size), out_shape=[jax....  7.57 us
    all_to_all x1, starting transfers between devices, body(): payload = lax.all_to_all(sent, 'ctx', 0, 0, tiled=True)  5.82 us
    pallas_call x1, Pallas kernels, make_query(): pl.pallas_call(functools.partial(query_kernel, group_size), out_shape=[ja...  5.55 us
    ppermute x1, starting transfers between devices, passed_along(): return lax.ppermute(block, axis, route)  4.53 us
    all_to_all x1, starting transfers between devices, body(): lax.all_to_all(conv.reshape(n_chips * n_ctx, stretch, piece), ('chip', 'c...  4.23 us
    all_to_all x1, waiting for transfers between devices, body(): lax.all_to_all(conv.reshape(n_chips * n_ctx, stretch, piece), ('chip', 'c...  3.83 us
  transfers between devices with their start and end apart: 9, of which 4 were waited for; matrix products, arithmetic and copies ran while one was open for 0% of the time, Pallas kernels for 29%

profile of v4, /device:TPU:0, one launch (start us, length us, event | category | flops | bytes accessed | tf_op | source)
XLA Modules:
  0.0 61.9 jit_solution(11623342805896933778)
XLA Ops:
  0.0 0.0 copy-start
  0.0 1.2 %constant_dynamic-slice_fusion = bf16[192,2048]{1,0:T(8,128)(2,1)S(1)} fusion(bf16[512,2048]{1,0:T(8,128)(2,1)} %w_near.1, s32[]{:T(128)S(6)} %select_n.15), kind=kLoop, calls=%fused_computation.2 | loop fusion | bytes 1572868 | tf_op jit(solution)/shard_map/dynamic_slice | solution.py:512
  1.2 3.0 %collective-permute-start.2 = (bf16[192,2048]{1,0:T(8,128)(2,1)S(1)}, bf16[192,2048]{1,0:T(8,128)(2,1)}, u32[]{:S(2)}, u32[]{:S(2)}) collective-permute-start(bf16[192,2048]{1,0:T(8,128)(2,1)S(1)} %constant_dynamic-slice_fusion), channel_id=1, source_target_pairs={{0,2},{2,0},{1,3},{3,1},{4,6},{6,4},{5,7},{7,5},{8,10},{10,8},{9,1... | collective-permute-start | bytes 2359304 | tf_op jit(solution)/shard_map/ppermute | solution.py:31
  4.3 7.6 %mix.1 = (bf16[8,72,512]{2,1,0:T(8,128)(2,1)}, bf16[128,2048]{1,0:T(8,128)(2,1)}) custom-call(bf16[512,2048]{1,0:T(8,128)(2,1)} %tokens.3, f32[7,384]{1,0:T(8,128)} %taps.7, bf16[3,2048,512]{2,1,0:T(8,128)(2,1)} %bitcast.5, f32[512,128]{1,0:T(8,128)} %filt.1, bf16[512,2048]{1,0:T(8,128)(2,1)} %w_near.1), custom_call_target="tpu_custom_call" | custom-call | flops 2147483648 | bytes 6291456 | tf_op jit(solution)/shard_map/mix/pallas_call | solution.py:149
  11.8 5.8 %all-to-all-start = ((bf16[8,72,512]{2,1,0:T(8,128)(2,1)}), bf16[8,72,512]{2,1,0:T(8,128)(2,1)S(1)}, u32[]{:S(2)}, u32[]{:S(2)}) async-start(bf16[8,72,512]{2,1,0:T(8,128)(2,1)} %get-tuple-element.13.after), calls=%async_computation | async-start | bytes 1179648 | tf_op jit(solution)/shard_map/all_to_all | solution.py:517
  17.7 0.5 collective-permute-start.4
  18.2 5.5 %query.1 = (bf16[512,256]{1,0:T(8,128)(2,1)}, bf16[512,256]{1,0:T(8,128)(2,1)}, bf16[16,512]{1,0:T(8,128)(2,1)}) custom-call(bf16[512,2048]{1,0:T(8,128)(2,1)} %tokens.3, f32[7,384]{1,0:T(8,128)} %taps.7, bf16[3,2048,512]{2,1,0:T(8,128)(2,1)} %bitcast.6, bf16[8,72,512]{2,1,0:T(8,128)(2,1)} %get-tuple-element.13.after), custom_call_target="tpu_custom_call" | custom-call | flops 1073741824 | bytes 4194304 | tf_op jit(solution)/shard_map/query/pallas_call | solution.py:210
  23.7 4.5 %collective-permute-start.1 = (bf16[16,512]{1,0:T(8,128)(2,1)}, bf16[16,512]{1,0:T(8,128)(2,1)}, u32[]{:S(2)}, u32[]{:S(2)}) collective-permute-start(bf16[16,512]{1,0:T(8,128)(2,1)} %get-tuple-element.16.refs_1_.kept), channel_id=1, source_target_pairs={{0,4},{4,8},{8,12},{12,16},{16,20},{20,24},{24,28},{1,5},{5,9},{9,... | collective-permute-start | bytes 49160 | tf_op jit(solution)/shard_map/ppermute | solution.py:27
  28.2 1.5 %collective-permute-start = (bf16[512,256]{1,0:T(8,128)(2,1)}, bf16[512,256]{1,0:T(8,128)(2,1)S(1)}, u32[]{:S(2)}, u32[]{:S(2)}) collective-permute-start(bf16[512,256]{1,0:T(8,128)(2,1)} %get-tuple-element.15), channel_id=1, source_target_pairs={{0,2},{2,0},{1,3},{3,1},{4,6},{6,4},{5,7},{7,5},{8,10},{10,8},{9,1... | collective-permute-start | bytes 786440 | tf_op jit(solution)/shard_map/ppermute | solution.py:31
  29.8 0.0 copy-done
  29.8 0.1 dynamic-slice_bitcast_fusion
  29.9 0.1 copy.7.kept
  30.0 0.0 copy-start.3
  30.0 0.0 collective-permute-done.2.refs_0_.mine
  30.0 1.0 %collective-permute-start.3 = (bf16[192,2048]{1,0:T(8,128)(2,1)}, bf16[192,2048]{1,0:T(8,128)(2,1)}, u32[]{:S(2)}, u32[]{:S(2)}) collective-permute-start(bf16[192,2048]{1,0:T(8,128)(2,1)} %collective-permute-done.2.refs_0_.mine), channel_id=1, source_target_pairs={{0,4},{4,0},{8,12},{12,8},{16,20},{20,16},{24,28},{28,24},{1,5},{5... | collective-permute-start | bytes 2359304 | tf_op jit(solution)/shard_map/ppermute | solution.py:31
  31.0 0.0 copy-start.4
  31.0 0.7 %copy-done.4 = bf16[16,512]{1,0:T(8,128)(2,1)S(1)} copy-done((bf16[16,512]{1,0:T(8,128)(2,1)S(1)}, bf16[16,512]{1,0:T(8,128)(2,1)}, u32[]{:S(2)}) %copy-start.4) | copy-done | bytes 16408
  31.7 0.0 copy-start.5
  31.7 1.6 %all-to-all-done.payload = bf16[8,72,512]{2,1,0:T(8,128)(2,1)S(1)} async-done(((bf16[8,72,512]{2,1,0:T(8,128)(2,1)}), bf16[8,72,512]{2,1,0:T(8,128)(2,1)S(1)}, u32[]{:S(2)}, u32[]{:S(2)}) %all-to-all-start) | async-done | bytes 589856 | tf_op jit(solution)/shard_map/all_to_all | solution.py:517
  33.3 0.0 copy-done.3
  33.3 3.1 %convolve.1.refs_1_ = bf16[2,8,64,256]{3,2,1,0:T(8,128)(2,1)} custom-call(bf16[8,72,512]{2,1,0:T(8,128)(2,1)S(1)} %all-to-all-done.payload, f32[7,384]{1,0:T(8,128)S(1)} %copy-done.3, f32[64,1]{1,0:T(8,128)S(1)} %arrived.3.gain), custom_call_target="tpu_custom_call" | custom-call | flops 10000000000 | bytes 1179648 | tf_op jit(solution)/shard_map/convolve/pallas_call | solution.py:372
  36.4 4.2 %all-to-all-start.1 = ((bf16[16,64,256]{2,1,0:T(8,128)(2,1)}), bf16[16,64,256]{2,1,0:T(8,128)(2,1)}, u32[]{:S(2)}, u32[]{:S(2)}) async-start(bf16[16,64,256]{2,1,0:T(8,128)(2,1)} %bitcast.2), calls=%async_computation.1 | async-start | bytes 1048576 | tf_op jit(solution)/shard_map/all_to_all | solution.py:526
  40.6 0.0 collective-permute-done.refs_0_.q_far
  40.7 0.0 copy-done.5
  40.7 0.0 collective-permute-done.1.before
  40.7 1.0 %fix.1.kept = bf16[512,128]{1,0:T(8,128)(2,1)S(1)} custom-call(bf16[16,512]{1,0:T(8,128)(2,1)} %collective-permute-done.1.before, bf16[16,512]{1,0:T(8,128)(2,1)S(1)} %arrived.4.ends, f32[7,384]{1,0:T(8,128)S(1)} %copy-done.3), custom_call_target="tpu_custom_call" | custom-call | flops 1000000 | bytes 100000 | tf_op jit(solution)/shard_map/fix/pallas_call | solution.py:247
  41.7 0.0 copy-start.1
  41.7 0.0 copy-start.2
  41.7 1.9 %collective-permute-start.5 = (bf16[512,128]{1,0:T(8,128)(2,1)S(1)}, bf16[512,128]{1,0:T(8,128)(2,1)S(1)}, u32[]{:S(2)}, u32[]{:S(2)}) collective-permute-start(bf16[512,128]{1,0:T(8,128)(2,1)S(1)} %fix.1.kept), channel_id=1, source_target_pairs={{0,2},{2,0},{1,3},{3,1},{4,6},{6,4},{5,7},{7,5},{8,10},{10,8},{9,1... | collective-permute-start | bytes 393224 | tf_op jit(solution)/shard_map/ppermute | solution.py:31
  43.5 0.0 collective-permute-done.4.refs_1_.direct
  43.5 8.2 %collective-permute-done.3.refs_0_.theirs = bf16[192,2048]{1,0:T(8,128)(2,1)} collective-permute-done((bf16[192,2048]{1,0:T(8,128)(2,1)}, bf16[192,2048]{1,0:T(8,128)(2,1)}, u32[]{:S(2)}, u32[]{:S(2)}) %collective-permute-start.3) | collective-permute-done | bytes 786464 | tf_op jit(solution)/shard_map/ppermute | solution.py:31
  51.7 0.0 collective-permute-done.5.fix_far
  51.7 3.8 %all-to-all-done.1 = bf16[16,64,256]{2,1,0:T(8,128)(2,1)} async-done(((bf16[16,64,256]{2,1,0:T(8,128)(2,1)}), bf16[16,64,256]{2,1,0:T(8,128)(2,1)}, u32[]{:S(2)}, u32[]{:S(2)}) %all-to-all-start.1) | async-done | bytes 524320 | tf_op jit(solution)/shard_map/all_to_all | solution.py:526
  55.6 0.0 copy-done.1
  55.6 0.0 copy-done.2
  55.6 3.4 %other_part.1 = (bf16[128,2048]{1,0:T(8,128)(2,1)S(1)}, bf16[2,2,512,1024]{3,2,1,0:T(8,128)(2,1)S(1)}, bf16[2,128,512]{2,1,0:T(8,128)(2,1)S(1)}) custom-call(bf16[512,256]{1,0:T(8,128)(2,1)S(1)} %copy-done.2, bf16[512,256]{1,0:T(8,128)(2,1)S(1)} %collective-permute-done.refs_0_.q_far, bf16[512,128]{1,0:T(8,128)(2,1)S(1)} %arrived.5.fix_near, ...), custom_call_target="tpu_custom_call" | custom-call | flops 536870912 | bytes 4194304 | tf_op jit(solution)/shard_map/other_part/pallas_call | solution.py:462
  59.0 0.1 collective-permute-start.6
  59.1 0.7 %own_part.1 = f32[128,2048]{1,0:T(8,128)S(1)} custom-call(bf16[2,128,512]{2,1,0:T(8,128)(2,1)S(1)} %get-tuple-element.18.gated, bf16[2,2,512,1024]{3,2,1,0:T(8,128)(2,1)S(1)} %get-tuple-element.19.weights), custom_call_target="tpu_custom_call" | custom-call | flops 536870912 | bytes 4194304 | tf_op jit(solution)/shard_map/own_part/pallas_call | solution.py:488
  59.8 1.2 %collective-permute-done.6 = bf16[128,2048]{1,0:T(8,128)(2,1)S(1)} collective-permute-done((bf16[128,2048]{1,0:T(8,128)(2,1)S(1)}, bf16[128,2048]{1,0:T(8,128)(2,1)S(1)}, u32[]{:S(2)}, u32[]{:S(2)}) %collective-permute-start.6) | collective-permute-done | bytes 524320 | tf_op jit(solution)/shard_map/ppermute | solution.py:31
  61.0 0.9 %add_convert_fusion = bf16[128,2048]{1,0:T(8,128)(2,1)} fusion(f32[128,2048]{1,0:T(8,128)S(1)} %own_part.1, bf16[128,2048]{1,0:T(8,128)(2,1)S(1)} %collective-permute-done.6), kind=kLoop, calls=%fused_computation | loop fusion | flops 786432 | bytes 2097152 | tf_op jit(solution)/shard_map/convert_element_type | solution.py:532
  (3 shorter events, 0.0 us)
Async XLA Ops:
  0.0 29.8 %copy-start = (f32[2048]{0:T(1024)S(1)}, f32[2048]{0:T(1024)}, u32[]{:S(2)}) copy-start(f32[2048]{0:T(1024)} %param.10) | copy-start | bytes 24580
  1.2 28.7 %collective-permute-start.2 = (bf16[192,2048]{1,0:T(8,128)(2,1)S(1)}, bf16[192,2048]{1,0:T(8,128)(2,1)}, u32[]{:S(2)}, u32[]{:S(2)}) collective-permute-start(bf16[192,2048]{1,0:T(8,128)(2,1)S(1)} %constant_dynamic-slice_fusion), channel_id=1, source_target_pairs={{0,2},{2,0},{1,3},{3,1},{4,6},{6,4},{5,7},{7,5},{8,10},{10,8},{9,1... | collective-permute-start | bytes 2359304 | tf_op jit(solution)/shard_map/ppermute | solution.py:31
  11.8 21.5 %all-to-all-start = ((bf16[8,72,512]{2,1,0:T(8,128)(2,1)}), bf16[8,72,512]{2,1,0:T(8,128)(2,1)S(1)}, u32[]{:S(2)}, u32[]{:S(2)}) async-start(bf16[8,72,512]{2,1,0:T(8,128)(2,1)} %get-tuple-element.13.after), calls=%async_computation | async-start | bytes 1179648 | tf_op jit(solution)/shard_map/all_to_all | solution.py:517
  17.7 25.9 %collective-permute-start.4 = (bf16[128,2048]{1,0:T(8,128)(2,1)}, bf16[128,2048]{1,0:T(8,128)(2,1)}, u32[]{:S(2)}, u32[]{:S(2)}) collective-permute-start(bf16[128,2048]{1,0:T(8,128)(2,1)} %get-tuple-element.17), channel_id=1, source_target_pairs={{0,2},{2,0},{1,3},{3,1},{4,6},{6,4},{5,7},{7,5},{8,10},{10,8},{9,1... | collective-permute-start | bytes 1572872 | tf_op jit(solution)/shard_map/ppermute | solution.py:31
  23.7 17.0 %collective-permute-start.1 = (bf16[16,512]{1,0:T(8,128)(2,1)}, bf16[16,512]{1,0:T(8,128)(2,1)}, u32[]{:S(2)}, u32[]{:S(2)}) collective-permute-start(bf16[16,512]{1,0:T(8,128)(2,1)} %get-tuple-element.16.refs_1_.kept), channel_id=1, source_target_pairs={{0,4},{4,8},{8,12},{12,16},{16,20},{20,24},{24,28},{1,5},{5,9},{9,... | collective-permute-start | bytes 49160 | tf_op jit(solution)/shard_map/ppermute | solution.py:27
  28.2 12.4 %collective-permute-start = (bf16[512,256]{1,0:T(8,128)(2,1)}, bf16[512,256]{1,0:T(8,128)(2,1)S(1)}, u32[]{:S(2)}, u32[]{:S(2)}) collective-permute-start(bf16[512,256]{1,0:T(8,128)(2,1)} %get-tuple-element.15), channel_id=1, source_target_pairs={{0,2},{2,0},{1,3},{3,1},{4,6},{6,4},{5,7},{7,5},{8,10},{10,8},{9,1... | collective-permute-start | bytes 786440 | tf_op jit(solution)/shard_map/ppermute | solution.py:31
  30.0 3.3 %copy-start.3 = (f32[7,384]{1,0:T(8,128)S(1)}, f32[7,384]{1,0:T(8,128)}, u32[]{:S(2)}) copy-start(f32[7,384]{1,0:T(8,128)} %taps.7) | copy-start | bytes 32260
  30.0 21.8 %collective-permute-start.3 = (bf16[192,2048]{1,0:T(8,128)(2,1)}, bf16[192,2048]{1,0:T(8,128)(2,1)}, u32[]{:S(2)}, u32[]{:S(2)}) collective-permute-start(bf16[192,2048]{1,0:T(8,128)(2,1)} %collective-permute-done.2.refs_0_.mine), channel_id=1, source_target_pairs={{0,4},{4,0},{8,12},{12,8},{16,20},{20,16},{24,28},{28,24},{1,5},{5... | collective-permute-start | bytes 2359304 | tf_op jit(solution)/shard_map/ppermute | solution.py:31
  31.0 0.7 %copy-start.4 = (bf16[16,512]{1,0:T(8,128)(2,1)S(1)}, bf16[16,512]{1,0:T(8,128)(2,1)}, u32[]{:S(2)}) copy-start(bf16[16,512]{1,0:T(8,128)(2,1)} %get-tuple-element.16.refs_1_.kept) | copy-start | bytes 49156
  31.7 9.0 %copy-start.5 = (bf16[16,512]{1,0:T(8,128)(2,1)S(1)}, bf16[16,512]{1,0:T(8,128)(2,1)}, u32[]{:S(2)}) copy-start(bf16[16,512]{1,0:T(8,128)(2,1)} %get-tuple-element.16.refs_1_.kept) | copy-start | bytes 49156
  36.4 19.2 %all-to-all-start.1 = ((bf16[16,64,256]{2,1,0:T(8,128)(2,1)}), bf16[16,64,256]{2,1,0:T(8,128)(2,1)}, u32[]{:S(2)}, u32[]{:S(2)}) async-start(bf16[16,64,256]{2,1,0:T(8,128)(2,1)} %bitcast.2), calls=%async_computation.1 | async-start | bytes 1048576 | tf_op jit(solution)/shard_map/all_to_all | solution.py:526
  41.7 13.9 %copy-start.1 = (bf16[512,2048]{1,0:T(8,128)(2,1)S(1)}, bf16[512,2048]{1,0:T(8,128)(2,1)}, u32[]{:S(2)}) copy-start(bf16[512,2048]{1,0:T(8,128)(2,1)} %w_near.1) | copy-start | bytes 6291460
  41.7 13.9 %copy-start.2 = (bf16[512,256]{1,0:T(8,128)(2,1)S(1)}, bf16[512,256]{1,0:T(8,128)(2,1)}, u32[]{:S(2)}) copy-start(bf16[512,256]{1,0:T(8,128)(2,1)} %get-tuple-element.14.q_near) | copy-start | bytes 786436
  41.7 10.1 %collective-permute-start.5 = (bf16[512,128]{1,0:T(8,128)(2,1)S(1)}, bf16[512,128]{1,0:T(8,128)(2,1)S(1)}, u32[]{:S(2)}, u32[]{:S(2)}) collective-permute-start(bf16[512,128]{1,0:T(8,128)(2,1)S(1)} %fix.1.kept), channel_id=1, source_target_pairs={{0,2},{2,0},{1,3},{3,1},{4,6},{6,4},{5,7},{7,5},{8,10},{10,8},{9,1... | collective-permute-start | bytes 393224 | tf_op jit(solution)/shard_map/ppermute | solution.py:31
  59.0 2.0 %collective-permute-start.6 = (bf16[128,2048]{1,0:T(8,128)(2,1)S(1)}, bf16[128,2048]{1,0:T(8,128)(2,1)S(1)}, u32[]{:S(2)}, u32[]{:S(2)}) collective-permute-start(bf16[128,2048]{1,0:T(8,128)(2,1)S(1)} %get-tuple-element.20), channel_id=1, source_target_pairs={{0,1},{1,0},{2,3},{3,2},{4,5},{5,4},{6,7},{7,6},{8,9},{9,8},{10,11... | collective-permute-start | bytes 1572872 | tf_op jit(solution)/shard_map/ppermute | solution.py:31

commit v5 on v4

--- a/solution.py
+++ b/solution.py
@@ -46,7 +46,7 @@
     return feat.astype(jnp.bfloat16).astype(jnp.float32)
 
 
-def mix_kernel(group_size, tokens, taps, weights, filt, w_out, out, direct, ext, wbuf, proj, lag, turned_lag, cut, sems):
+def mix_kernel(group_size, tokens, taps, weights, filt, w_out, out, shared, direct, ext, wbuf, proj, lag, turned_lag, cut, sems):
     n_tok = tokens.shape[0]
     n_ctx = out.shape[0]
     stretch = out.shape[1] - 8
@@ -110,19 +110,32 @@
                 for c in range(0, LANES, stretch):
                     out[(tile * LANES + c) // stretch, 0:stretch, row : row + chunk] = flipped[c : c + stretch, :]
 
-    fetch = pltpu.make_async_copy(w_out.at[pl.ds(w_out.shape[0] - cut.shape[0], cut.shape[0])], cut, sems.at[2 + 2 * n_blocks])
-    store = pltpu.make_async_copy(cut, direct, sems.at[3 + 2 * n_blocks])
+    part, rest = shared.shape[0], direct.shape[0]
+    parity = lax.axis_index("ctx") % 2
+    base = 2 + 2 * n_blocks
+    fetches = [
+        pltpu.make_async_copy(
+            w_out.at[pl.ds(pl.multiple_of(parity * part, part), part)], cut.at[pl.ds(0, part)], sems.at[base]
+        ),
+        pltpu.make_async_copy(w_out.at[pl.ds(2 * part, rest)], cut.at[pl.ds(part, rest)], sems.at[base + 1]),
+    ]
+    stores = [
+        pltpu.make_async_copy(cut.at[pl.ds(0, part)], shared, sems.at[base + 2]),
+        pltpu.make_async_copy(cut.at[pl.ds(part, rest)], direct, sems.at[base + 3]),
+    ]
     main.wait()
     for blk in range(n_blocks):
         for load in loads[2 * blk : 2 * blk + 2]:
             load.wait()
         if blk == n_blocks - 1:
-            fetch.start()
+            for fetch in fetches:
+                fetch.start()
         multiply(blk)
         if blk:
             finish(blk - 1)
-    fetch.wait()
-    store.start()
+    for fetch, store in zip(fetches, stores):
+        fetch.wait()
+        store.start()
     finish(n_blocks - 1)
     low = lax.broadcasted_iota(jnp.int32, (8, LANES), 1) < LANES // 2
     for dest in range(n_ctx):
@@ -135,30 +148,32 @@
             if lane != LANES // 2:
                 tail = pltpu.roll(tail, (LANES // 2 - lane) % LANES, 1)
             out[dest, stretch:, k * LANES : (k + 1) * LANES] = jnp.where(low, head, tail).astype(jnp.bfloat16)
-    store.wait()
-
-
-def mix(group_size, tokens, taps, weights, filt, w_out, rest, n_ctx):
+    for store in stores:
+        store.wait()
+
+
+def mix(group_size, tokens, taps, weights, filt, w_out, part, n_ctx):
     n_tok, depth = tokens.shape
     block = weights.shape[2]
     width = min(256, block)
     stretch = block // n_ctx
-    direct = (rest, w_out.shape[1])
+    rest = block - 2 * part
+    parts = [(rows, w_out.shape[1]) for rows in (part, rest)]
     hbm = pl.BlockSpec(memory_space=pltpu.HBM)
     vmem = pl.BlockSpec(memory_space=pltpu.VMEM)
     return pl.pallas_call(
         functools.partial(mix_kernel, group_size),
-        out_shape=[jax.ShapeDtypeStruct(shape, jnp.bfloat16) for shape in ((n_ctx, stretch + 8, n_tok), direct)],
+        out_shape=[jax.ShapeDtypeStruct(shape, jnp.bfloat16) for shape in [(n_ctx, stretch + 8, n_tok)] + parts],
         in_specs=[hbm, vmem, hbm, hbm, hbm],
-        out_specs=[vmem, hbm],
+        out_specs=[vmem, hbm, hbm],
         scratch_shapes=[
             pltpu.VMEM((n_tok, depth), jnp.bfloat16),
             pltpu.VMEM((2, block // width, depth, width), jnp.bfloat16),
             pltpu.VMEM((2, block // LANES, RIM + n_tok, LANES), jnp.float32),
             pltpu.VMEM(filt.shape, jnp.float32),
             pltpu.VMEM(filt.shape[::-1], jnp.float32),
-            pltpu.VMEM(direct, jnp.bfloat16),
-            pltpu.SemaphoreType.DMA((4 + 2 * (block // width),)),
+            pltpu.VMEM((part + rest, w_out.shape[1]), jnp.bfloat16),
+            pltpu.SemaphoreType.DMA((6 + 2 * (block // width),)),
         ],
         compiler_params=pltpu.CompilerParams(vmem_limit_bytes=56 * MIB),
         cost_estimate=pl.CostEstimate(
@@ -229,7 +244,7 @@
 
 def fix_kernel(group_size, before, ends, taps, out):
     n_taps, n_groups = taps.shape[0], taps.shape[1] // 3
-    block = out.shape[0]
+    block = out.shape[1]
     group0 = fft_index() * (block // group_size)
     for tile in range(block // LANES):
         lanes = slice(tile * LANES, (tile + 1) * LANES)
@@ -238,15 +253,14 @@
             [before[:, lanes].astype(jnp.float32)[:8], ends[:, lanes].astype(jnp.float32)[8:]], axis=0
         )
         feat = filtered(coef, lambda j: both[8 - j : 16 - j, :], n_taps)
-        feat = jnp.concatenate([feat, jnp.zeros((LANES - 8, LANES), jnp.float32)], axis=0)
-        out[lanes, :] = feat.T.astype(jnp.bfloat16)
+        out[:, lanes] = jnp.concatenate([feat, jnp.zeros((8, LANES), jnp.float32)], axis=0).astype(jnp.bfloat16)
 
 
 def make_fix(group_size, before, ends, taps):
     vmem = pl.BlockSpec(memory_space=pltpu.VMEM)
     return pl.pallas_call(
         functools.partial(fix_kernel, group_size),
-        out_shape=jax.ShapeDtypeStruct((ends.shape[1], LANES), jnp.bfloat16),
+        out_shape=jax.ShapeDtypeStruct(ends.shape, jnp.bfloat16),
         in_specs=[vmem] * 3,
         out_specs=vmem,
         compiler_params=pltpu.CompilerParams(vmem_limit_bytes=16 * MIB),
@@ -427,15 +441,21 @@
             load.start()
     early = lax.broadcasted_iota(jnp.int32, (block, LANES), 1) < 8
 
+    def channels_first(fix):
+        rows = jnp.concatenate([fix[...].astype(jnp.float32), jnp.zeros((LANES - 16, block), jnp.float32)], axis=0)
+        return jnp.concatenate([rows[:, at : at + LANES].T for at in range(0, block, LANES)], axis=0)
+
+    fixes = [channels_first(fix) for fix in (fix_near, fix_far)]
+
     def gate(k, half):
-        query, fix = ((q_near, fix_near), (q_far, fix_far))[k]
+        query = (q_near, q_far)[k]
         pieces = []
         for t in range(0, n_tok, LANES):
             at = pl.ds(pl.multiple_of((core ^ half) * n_tok + t, LANES), LANES)
             values = query[:, at].astype(jnp.float32)
             if t == 0:
                 first = jnp.logical_and(early, jnp.logical_and(chip == 0, core == half))
-                values = jnp.where(first, fix[...].astype(jnp.float32), values)
+                values = jnp.where(first, fixes[k], values)
             product = values * conv[chip ^ k, :, at].astype(jnp.float32)
             pieces.append(product.T.astype(jnp.bfloat16))
         return pieces[0] if len(pieces) == 1 else jnp.concatenate(pieces, axis=0)
@@ -508,12 +528,11 @@
     piece = tok_len // n_chips
 
     weights = w_in.transpose(1, 0, 2)
-    part = block // 8 * 3
-    shared = lax.dynamic_slice_in_dim(w_out, lax.axis_index("ctx") % 2 * part, part, 0)
-    mine = swapped(shared, "chip")
+    sent, shared, direct = mix(
+        group_size, tokens, short_taps, weights, long_filter, w_out, block // 32 * 12, n_ctx
+    )
+    mine, direct = swapped(shared, "chip"), swapped(direct, "chip")
     theirs = swapped(mine, "ctx")
-    sent, direct = mix(group_size, tokens, short_taps, weights, long_filter, w_out, block - 2 * part, n_ctx)
-    direct = swapped(direct, "chip")
     payload = lax.all_to_all(sent, "ctx", 0, 0, tiled=True)
 
     near, far, ends = make_query(group_size, tokens, short_taps, weights, sent, n_chips)
@@ -522,11 +541,11 @@
 
     gain = lax.dynamic_slice_in_dim(skip_gain, fft_index() * block + lax.axis_index("ctx") * stretch, stretch, 0)
     conv = convolve(group_size, span, stretch, payload, short_taps, arrived(gain[:, None], mine, ends), n_chips)
-    fix = make_fix(group_size, before, arrived(ends, far, conv), short_taps)
+    fix = make_fix(group_size, before, arrived(ends, conv), short_taps)
     conv = lax.all_to_all(conv.reshape(n_chips * n_ctx, stretch, piece), ("chip", "ctx"), 0, 0, tiled=True)
     conv = conv.reshape(n_chips, block, piece)
 
-    fixes = (arrived(fix, theirs, direct), swapped(fix, "chip"))
+    fixes = (arrived(fix, theirs, direct, far), swapped(fix, "chip"))
     other, staged, gated = other_part((near, far), fixes, conv, (w_out, mine, theirs, direct))
     other = swapped(other, "core")
     return (own_part(gated, staged) + other.astype(jnp.float32)).astype(jnp.bfloat16)

time: 62.5 us -> 61.4 us (0.982)
  waiting for transfers between devices: 14.8 us -> 12 us
  starting transfers between devices: 22.6 us -> 25.4 us
  local copies, waits for them, and re-layouts: 2.12 us -> 0.91 us
    all_to_all x1, starting transfers between devices: 4.23 us -> 5.94 us  [body(): lax.all_to_all(conv.reshape(n_chips * n_ctx, stretch, piece), ('chip', 'c...]
    all_to_all x1, waiting for transfers between devices: 1.6 us -> 0.01 us  [body(): payload = lax.all_to_all(sent, 'ctx', 0, 0, tiled=True)]
    all_to_all x1, waiting for transfers between devices: 3.83 us -> 2.55 us  [body(): lax.all_to_all(conv.reshape(n_chips * n_ctx, stretch, piece), ('chip', 'c...]
    dynamic_slice x1 -> x0, local copies, waits for them, and re-layouts: 1.21 us -> none  [body(): lax.dynamic_slice_in_dim(w_out, lax.axis_index('ctx') % 2 * part, part, 0)]
    ppermute x6, starting transfers between devices: 8 us -> 9.16 us  [swapped(): lax.ppermute(block, axis, [(i, i ^ 1) for i in range(lax.axis_size(axis))])]
  transfers between devices with their start and end apart: 9 -> 9, of which waited for: 4 -> 5; matrix products, arithmetic and copies ran while one was open for 0% -> 0% of each run, Pallas kernels for 29% -> 17%
where the time goes in v5:
time: 61.4 us; the launch traced here: 60.8 us
  starting transfers between devices  25.4 us (41%)
  Pallas kernels  21.4 us (35%)
  waiting for transfers between devices  12 us (20%)
  local copies, waits for them, and re-layouts  0.91 us (1%)
  other arithmetic  0.9 us (1%)
    ppermute x6, waiting for transfers between devices, swapped(): lax.ppermute(block, axis, [(i, i ^ 1) for i in range(lax.axis_size(axis))])  9.46 us
    ppermute x6, starting transfers between devices, swapped(): lax.ppermute(block, axis, [(i, i ^ 1) for i in range(lax.axis_size(axis))])  9.16 us
    pallas_call x1, Pallas kernels, mix(): pl.pallas_call(functools.partial(mix_kernel, group_size), out_shape=[jax....  7.86 us
    all_to_all x1, starting transfers between devices, body(): lax.all_to_all(conv.reshape(n_chips * n_ctx, stretch, piece), ('chip', 'c...  5.94 us
    all_to_all x1, starting transfers between devices, body(): payload = lax.all_to_all(sent, 'ctx', 0, 0, tiled=True)  5.81 us
    pallas_call x1, Pallas kernels, make_query(): pl.pallas_call(functools.partial(query_kernel, group_size), out_shape=[ja...  5.54 us
    ppermute x1, starting transfers between devices, passed_along(): return lax.ppermute(block, axis, route)  4.53 us
    pallas_call x1, Pallas kernels, other_part(): pl.pallas_call(other_kernel, out_shape=[jax.ShapeDtypeStruct(shape, jnp.b...  3.32 us
  transfers between devices with their start and end apart: 9, of which 5 were waited for; matrix products, arithmetic and copies ran while one was open for 0% of the time, Pallas kernels for 17%

profile of v5, /device:TPU:0, one launch (start us, length us, event | category | flops | bytes accessed | tf_op | source)
XLA Modules:
  0.0 60.8 jit_solution(3642864892982167898)
XLA Ops:
  0.0 0.0 copy-start
  0.0 7.9 %mix.1 = (bf16[8,72,512]{2,1,0:T(8,128)(2,1)}, bf16[192,2048]{1,0:T(8,128)(2,1)}, bf16[128,2048]{1,0:T(8,128)(2,1)}) custom-call(bf16[512,2048]{1,0:T(8,128)(2,1)} %tokens.3, f32[7,384]{1,0:T(8,128)} %taps.7, bf16[3,2048,512]{2,1,0:T(8,128)(2,1)} %bitcast.6, f32[512,128]{1,0:T(8,128)} %filt.1, bf16[512,2048]{1,0:T(8,128)(2,1)} %w_near.1), custom_call_target="tpu_custom_call" | custom-call | flops 2147483648 | bytes 6291456 | tf_op jit(solution)/shard_map/mix/pallas_call | solution.py:164
  7.9 3.0 %collective-permute-start.2 = (bf16[192,2048]{1,0:T(8,128)(2,1)}, bf16[192,2048]{1,0:T(8,128)(2,1)}, u32[]{:S(2)}, u32[]{:S(2)}) collective-permute-start(bf16[192,2048]{1,0:T(8,128)(2,1)} %get-tuple-element.18), channel_id=1, source_target_pairs={{0,2},{2,0},{1,3},{3,1},{4,6},{6,4},{5,7},{7,5},{8,10},{10,8},{9,1... | collective-permute-start | bytes 2359304 | tf_op jit(solution)/shard_map/ppermute | solution.py:31
  10.9 5.8 %all-to-all-start = ((bf16[8,72,512]{2,1,0:T(8,128)(2,1)}), bf16[8,72,512]{2,1,0:T(8,128)(2,1)S(1)}, u32[]{:S(2)}, u32[]{:S(2)}) async-start(bf16[8,72,512]{2,1,0:T(8,128)(2,1)} %get-tuple-element.14.after), calls=%async_computation | async-start | bytes 1179648 | tf_op jit(solution)/shard_map/all_to_all | solution.py:536
  16.7 0.5 collective-permute-start.4
  17.2 5.5 %query.1 = (bf16[512,256]{1,0:T(8,128)(2,1)}, bf16[512,256]{1,0:T(8,128)(2,1)}, bf16[16,512]{1,0:T(8,128)(2,1)}) custom-call(bf16[512,2048]{1,0:T(8,128)(2,1)} %tokens.3, f32[7,384]{1,0:T(8,128)} %taps.7, bf16[3,2048,512]{2,1,0:T(8,128)(2,1)} %bitcast.7, bf16[8,72,512]{2,1,0:T(8,128)(2,1)} %get-tuple-element.14.after), custom_call_target="tpu_custom_call" | custom-call | flops 1073741824 | bytes 4194304 | tf_op jit(solution)/shard_map/query/pallas_call | solution.py:225
  22.8 4.5 %collective-permute-start.1 = (bf16[16,512]{1,0:T(8,128)(2,1)}, bf16[16,512]{1,0:T(8,128)(2,1)}, u32[]{:S(2)}, u32[]{:S(2)}) collective-permute-start(bf16[16,512]{1,0:T(8,128)(2,1)} %get-tuple-element.17.refs_1_.kept), channel_id=1, source_target_pairs={{0,4},{4,8},{8,12},{12,16},{16,20},{20,24},{24,28},{1,5},{5,9},{9,... | collective-permute-start | bytes 49160 | tf_op jit(solution)/shard_map/ppermute | solution.py:27
  27.3 1.5 %collective-permute-start = (bf16[512,256]{1,0:T(8,128)(2,1)}, bf16[512,256]{1,0:T(8,128)(2,1)}, u32[]{:S(2)}, u32[]{:S(2)}) collective-permute-start(bf16[512,256]{1,0:T(8,128)(2,1)} %get-tuple-element.16), channel_id=1, source_target_pairs={{0,2},{2,0},{1,3},{3,1},{4,6},{6,4},{5,7},{7,5},{8,10},{10,8},{9,1... | collective-permute-start | bytes 786440 | tf_op jit(solution)/shard_map/ppermute | solution.py:31
  28.8 0.0 copy-done
  28.8 0.1 dynamic-slice_bitcast_fusion
  28.9 0.1 copy.7.kept
  29.0 0.0 copy-start.3
  29.0 0.6 collective-permute-done.2.refs_0_.mine
  29.6 2.0 %collective-permute-start.3 = (bf16[192,2048]{1,0:T(8,128)(2,1)}, bf16[192,2048]{1,0:T(8,128)(2,1)}, u32[]{:S(2)}, u32[]{:S(2)}) collective-permute-start(bf16[192,2048]{1,0:T(8,128)(2,1)} %collective-permute-done.2.refs_0_.mine), channel_id=1, source_target_pairs={{0,4},{4,0},{8,12},{12,8},{16,20},{20,16},{24,28},{28,24},{1,5},{5... | collective-permute-start | bytes 2359304 | tf_op jit(solution)/shard_map/ppermute | solution.py:31
  31.6 0.0 copy-start.4
  31.6 0.7 %copy-done.4 = bf16[16,512]{1,0:T(8,128)(2,1)S(1)} copy-done((bf16[16,512]{1,0:T(8,128)(2,1)S(1)}, bf16[16,512]{1,0:T(8,128)(2,1)}, u32[]{:S(2)}) %copy-start.4) | copy-done | bytes 16408
  32.3 0.0 copy-start.5
  32.3 0.0 all-to-all-done.payload
  32.4 0.0 copy-done.3
  32.4 3.2 %convolve.1.refs_0_ = bf16[2,8,64,256]{3,2,1,0:T(8,128)(2,1)} custom-call(bf16[8,72,512]{2,1,0:T(8,128)(2,1)S(1)} %all-to-all-done.payload, f32[7,384]{1,0:T(8,128)S(1)} %copy-done.3, f32[64,1]{1,0:T(8,128)S(1)} %arrived.3.gain), custom_call_target="tpu_custom_call" | custom-call | flops 10000000000 | bytes 1179648 | tf_op jit(solution)/shard_map/convolve/pallas_call | solution.py:386
  35.5 0.0 copy-done.5
  35.5 5.9 %all-to-all-start.1 = ((bf16[16,64,256]{2,1,0:T(8,128)(2,1)}), bf16[16,64,256]{2,1,0:T(8,128)(2,1)S(1)}, u32[]{:S(2)}, u32[]{:S(2)}) async-start(bf16[16,64,256]{2,1,0:T(8,128)(2,1)} %bitcast.2), calls=%async_computation.1 | async-start | bytes 1048576 | tf_op jit(solution)/shard_map/all_to_all | solution.py:545
  41.5 0.0 collective-permute-done.1.before
  41.5 0.8 %fix.1.kept = bf16[16,512]{1,0:T(8,128)(2,1)S(1)} custom-call(bf16[16,512]{1,0:T(8,128)(2,1)} %collective-permute-done.1.before, bf16[16,512]{1,0:T(8,128)(2,1)S(1)} %arrived.4.ends, f32[7,384]{1,0:T(8,128)S(1)} %copy-done.3), custom_call_target="tpu_custom_call" | custom-call | flops 1000000 | bytes 100000 | tf_op jit(solution)/shard_map/fix/pallas_call | solution.py:261
  42.3 0.0 copy-start.1
  42.3 0.0 copy-start.2
  42.3 2.0 %collective-permute-start.5 = (bf16[16,512]{1,0:T(8,128)(2,1)S(1)}, bf16[16,512]{1,0:T(8,128)(2,1)S(1)}, u32[]{:S(2)}, u32[]{:S(2)}) collective-permute-start(bf16[16,512]{1,0:T(8,128)(2,1)S(1)} %fix.1.kept), channel_id=1, source_target_pairs={{0,2},{2,0},{1,3},{3,1},{4,6},{6,4},{5,7},{7,5},{8,10},{10,8},{9,1... | collective-permute-start | bytes 49160 | tf_op jit(solution)/shard_map/ppermute | solution.py:31
  44.3 5.3 %collective-permute-done.refs_2_.q_far = bf16[512,256]{1,0:T(8,128)(2,1)} collective-permute-done((bf16[512,256]{1,0:T(8,128)(2,1)}, bf16[512,256]{1,0:T(8,128)(2,1)}, u32[]{:S(2)}, u32[]{:S(2)}) %collective-permute-start) | collective-permute-done | bytes 262176 | tf_op jit(solution)/shard_map/ppermute | solution.py:31
  49.7 0.0 collective-permute-done.4.refs_1_.direct
  49.7 2.4 %collective-permute-done.3.refs_0_.theirs = bf16[192,2048]{1,0:T(8,128)(2,1)} collective-permute-done((bf16[192,2048]{1,0:T(8,128)(2,1)}, bf16[192,2048]{1,0:T(8,128)(2,1)}, u32[]{:S(2)}, u32[]{:S(2)}) %collective-permute-start.3) | collective-permute-done | bytes 786464 | tf_op jit(solution)/shard_map/ppermute | solution.py:31
  52.0 0.0 collective-permute-done.5.fix_far
  52.0 2.5 %all-to-all-done.1 = bf16[16,64,256]{2,1,0:T(8,128)(2,1)S(1)} async-done(((bf16[16,64,256]{2,1,0:T(8,128)(2,1)}), bf16[16,64,256]{2,1,0:T(8,128)(2,1)S(1)}, u32[]{:S(2)}, u32[]{:S(2)}) %all-to-all-start.1) | async-done | bytes 524320 | tf_op jit(solution)/shard_map/all_to_all | solution.py:545
  54.6 0.0 copy-done.1
  54.6 0.0 copy-done.2
  54.6 3.3 %other_part.1 = (bf16[128,2048]{1,0:T(8,128)(2,1)S(1)}, bf16[2,2,512,1024]{3,2,1,0:T(8,128)(2,1)S(1)}, bf16[2,128,512]{2,1,0:T(8,128)(2,1)S(1)}) custom-call(bf16[512,256]{1,0:T(8,128)(2,1)S(1)} %copy-done.2, bf16[512,256]{1,0:T(8,128)(2,1)} %collective-permute-done.refs_2_.q_far, bf16[16,512]{1,0:T(8,128)(2,1)S(1)} %arrived.5.fix_near, ...), custom_call_target="tpu_custom_call" | custom-call | flops 536870912 | bytes 4194304 | tf_op jit(solution)/shard_map/other_part/pallas_call | solution.py:482
  57.9 0.1 collective-permute-start.6
  58.0 0.7 %own_part.1 = f32[128,2048]{1,0:T(8,128)S(1)} custom-call(bf16[2,128,512]{2,1,0:T(8,128)(2,1)S(1)} %get-tuple-element.20.gated, bf16[2,2,512,1024]{3,2,1,0:T(8,128)(2,1)S(1)} %get-tuple-element.21.weights), custom_call_target="tpu_custom_call" | custom-call | flops 536870912 | bytes 4194304 | tf_op jit(solution)/shard_map/own_part/pallas_call | solution.py:508
  58.7 1.2 %collective-permute-done.6 = bf16[128,2048]{1,0:T(8,128)(2,1)S(1)} collective-permute-done((bf16[128,2048]{1,0:T(8,128)(2,1)S(1)}, bf16[128,2048]{1,0:T(8,128)(2,1)S(1)}, u32[]{:S(2)}, u32[]{:S(2)}) %collective-permute-start.6) | collective-permute-done | bytes 524320 | tf_op jit(solution)/shard_map/ppermute | solution.py:31
  59.9 0.9 %add_convert_fusion = bf16[128,2048]{1,0:T(8,128)(2,1)} fusion(f32[128,2048]{1,0:T(8,128)S(1)} %own_part.1, bf16[128,2048]{1,0:T(8,128)(2,1)S(1)} %collective-permute-done.6), kind=kLoop, calls=%fused_computation | loop fusion | flops 786432 | bytes 2097152 | tf_op jit(solution)/shard_map/convert_element_type | solution.py:551
  (3 shorter events, 0.0 us)
Async XLA Ops:
  0.0 28.8 %copy-start = (f32[2048]{0:T(1024)S(1)}, f32[2048]{0:T(1024)}, u32[]{:S(2)}) copy-start(f32[2048]{0:T(1024)} %param.10) | copy-start | bytes 24580
  7.9 21.7 %collective-permute-start.2 = (bf16[192,2048]{1,0:T(8,128)(2,1)}, bf16[192,2048]{1,0:T(8,128)(2,1)}, u32[]{:S(2)}, u32[]{:S(2)}) collective-permute-start(bf16[192,2048]{1,0:T(8,128)(2,1)} %get-tuple-element.18), channel_id=1, source_target_pairs={{0,2},{2,0},{1,3},{3,1},{4,6},{6,4},{5,7},{7,5},{8,10},{10,8},{9,1... | collective-permute-start | bytes 2359304 | tf_op jit(solution)/shard_map/ppermute | solution.py:31
  10.9 21.4 %all-to-all-start = ((bf16[8,72,512]{2,1,0:T(8,128)(2,1)}), bf16[8,72,512]{2,1,0:T(8,128)(2,1)S(1)}, u32[]{:S(2)}, u32[]{:S(2)}) async-start(bf16[8,72,512]{2,1,0:T(8,128)(2,1)} %get-tuple-element.14.after), calls=%async_computation | async-start | bytes 1179648 | tf_op jit(solution)/shard_map/all_to_all | solution.py:536
  16.7 32.9 %collective-permute-start.4 = (bf16[128,2048]{1,0:T(8,128)(2,1)}, bf16[128,2048]{1,0:T(8,128)(2,1)}, u32[]{:S(2)}, u32[]{:S(2)}) collective-permute-start(bf16[128,2048]{1,0:T(8,128)(2,1)} %get-tuple-element.19), channel_id=1, source_target_pairs={{0,2},{2,0},{1,3},{3,1},{4,6},{6,4},{5,7},{7,5},{8,10},{10,8},{9,1... | collective-permute-start | bytes 1572872 | tf_op jit(solution)/shard_map/ppermute | solution.py:31
  22.8 18.7 %collective-permute-start.1 = (bf16[16,512]{1,0:T(8,128)(2,1)}, bf16[16,512]{1,0:T(8,128)(2,1)}, u32[]{:S(2)}, u32[]{:S(2)}) collective-permute-start(bf16[16,512]{1,0:T(8,128)(2,1)} %get-tuple-element.17.refs_1_.kept), channel_id=1, source_target_pairs={{0,4},{4,8},{8,12},{12,16},{16,20},{20,24},{24,28},{1,5},{5,9},{9,... | collective-permute-start | bytes 49160 | tf_op jit(solution)/shard_map/ppermute | solution.py:27
  27.3 22.4 %collective-permute-start = (bf16[512,256]{1,0:T(8,128)(2,1)}, bf16[512,256]{1,0:T(8,128)(2,1)}, u32[]{:S(2)}, u32[]{:S(2)}) collective-permute-start(bf16[512,256]{1,0:T(8,128)(2,1)} %get-tuple-element.16), channel_id=1, source_target_pairs={{0,2},{2,0},{1,3},{3,1},{4,6},{6,4},{5,7},{7,5},{8,10},{10,8},{9,1... | collective-permute-start | bytes 786440 | tf_op jit(solution)/shard_map/ppermute | solution.py:31
  29.0 3.3 %copy-start.3 = (f32[7,384]{1,0:T(8,128)S(1)}, f32[7,384]{1,0:T(8,128)}, u32[]{:S(2)}) copy-start(f32[7,384]{1,0:T(8,128)} %taps.7) | copy-start | bytes 32260
  29.6 22.4 %collective-permute-start.3 = (bf16[192,2048]{1,0:T(8,128)(2,1)}, bf16[192,2048]{1,0:T(8,128)(2,1)}, u32[]{:S(2)}, u32[]{:S(2)}) collective-permute-start(bf16[192,2048]{1,0:T(8,128)(2,1)} %collective-permute-done.2.refs_0_.mine), channel_id=1, source_target_pairs={{0,4},{4,0},{8,12},{12,8},{16,20},{20,16},{24,28},{28,24},{1,5},{5... | collective-permute-start | bytes 2359304 | tf_op jit(solution)/shard_map/ppermute | solution.py:31
  31.6 0.7 %copy-start.4 = (bf16[16,512]{1,0:T(8,128)(2,1)S(1)}, bf16[16,512]{1,0:T(8,128)(2,1)}, u32[]{:S(2)}) copy-start(bf16[16,512]{1,0:T(8,128)(2,1)} %get-tuple-element.17.refs_1_.kept) | copy-start | bytes 49156
  32.3 3.2 %copy-start.5 = (bf16[16,512]{1,0:T(8,128)(2,1)S(1)}, bf16[16,512]{1,0:T(8,128)(2,1)}, u32[]{:S(2)}) copy-start(bf16[16,512]{1,0:T(8,128)(2,1)} %get-tuple-element.17.refs_1_.kept) | copy-start | bytes 49156
  35.5 19.1 %all-to-all-start.1 = ((bf16[16,64,256]{2,1,0:T(8,128)(2,1)}), bf16[16,64,256]{2,1,0:T(8,128)(2,1)S(1)}, u32[]{:S(2)}, u32[]{:S(2)}) async-start(bf16[16,64,256]{2,1,0:T(8,128)(2,1)} %bitcast.2), calls=%async_computation.1 | async-start | bytes 1048576 | tf_op jit(solution)/shard_map/all_to_all | solution.py:545
  42.3 12.3 %copy-start.1 = (bf16[512,2048]{1,0:T(8,128)(2,1)S(1)}, bf16[512,2048]{1,0:T(8,128)(2,1)}, u32[]{:S(2)}) copy-start(bf16[512,2048]{1,0:T(8,128)(2,1)} %w_near.1) | copy-start | bytes 6291460
  42.3 12.3 %copy-start.2 = (bf16[512,256]{1,0:T(8,128)(2,1)S(1)}, bf16[512,256]{1,0:T(8,128)(2,1)}, u32[]{:S(2)}) copy-start(bf16[512,256]{1,0:T(8,128)(2,1)} %get-tuple-element.15.q_near) | copy-start | bytes 786436
  42.3 9.7 %collective-permute-start.5 = (bf16[16,512]{1,0:T(8,128)(2,1)S(1)}, bf16[16,512]{1,0:T(8,128)(2,1)S(1)}, u32[]{:S(2)}, u32[]{:S(2)}) collective-permute-start(bf16[16,512]{1,0:T(8,128)(2,1)S(1)} %fix.1.kept), channel_id=1, source_target_pairs={{0,2},{2,0},{1,3},{3,1},{4,6},{6,4},{5,7},{7,5},{8,10},{10,8},{9,1... | collective-permute-start | bytes 49160 | tf_op jit(solution)/shard_map/ppermute | solution.py:31
  57.9 2.0 %collective-permute-start.6 = (bf16[128,2048]{1,0:T(8,128)(2,1)S(1)}, bf16[128,2048]{1,0:T(8,128)(2,1)S(1)}, u32[]{:S(2)}, u32[]{:S(2)}) collective-permute-start(bf16[128,2048]{1,0:T(8,128)(2,1)S(1)} %get-tuple-element.22), channel_id=1, source_target_pairs={{0,1},{1,0},{2,3},{3,2},{4,5},{5,4},{6,7},{7,6},{8,9},{9,8},{10,11... | collective-permute-start | bytes 1572872 | tf_op jit(solution)/shard_map/ppermute | solution.py:31

commit v6 on v4

--- a/solution.py
+++ b/solution.py
@@ -46,7 +46,7 @@
     return feat.astype(jnp.bfloat16).astype(jnp.float32)
 
 
-def mix_kernel(group_size, tokens, taps, weights, filt, w_out, out, direct, ext, wbuf, proj, lag, turned_lag, cut, sems):
+def mix_kernel(group_size, tokens, taps, weights, filt, w_out, out, shared, ext, wbuf, proj, lag, turned_lag, cut, sems):
     n_tok = tokens.shape[0]
     n_ctx = out.shape[0]
     stretch = out.shape[1] - 8
@@ -110,8 +110,12 @@
                 for c in range(0, LANES, stretch):
                     out[(tile * LANES + c) // stretch, 0:stretch, row : row + chunk] = flipped[c : c + stretch, :]
 
-    fetch = pltpu.make_async_copy(w_out.at[pl.ds(w_out.shape[0] - cut.shape[0], cut.shape[0])], cut, sems.at[2 + 2 * n_blocks])
-    store = pltpu.make_async_copy(cut, direct, sems.at[3 + 2 * n_blocks])
+    part = shared.shape[0]
+    parity = lax.axis_index("ctx") % 2
+    fetch = pltpu.make_async_copy(
+        w_out.at[pl.ds(pl.multiple_of(parity * part, part), part)], cut, sems.at[2 + 2 * n_blocks]
+    )
+    store = pltpu.make_async_copy(cut, shared, sems.at[3 + 2 * n_blocks])
     main.wait()
     for blk in range(n_blocks):
         for load in loads[2 * blk : 2 * blk + 2]:
@@ -138,17 +142,17 @@
     store.wait()
 
 
-def mix(group_size, tokens, taps, weights, filt, w_out, rest, n_ctx):
+def mix(group_size, tokens, taps, weights, filt, w_out, part, n_ctx):
     n_tok, depth = tokens.shape
     block = weights.shape[2]
     width = min(256, block)
     stretch = block // n_ctx
-    direct = (rest, w_out.shape[1])
+    shared = (part, w_out.shape[1])
     hbm = pl.BlockSpec(memory_space=pltpu.HBM)
     vmem = pl.BlockSpec(memory_space=pltpu.VMEM)
     return pl.pallas_call(
         functools.partial(mix_kernel, group_size),
-        out_shape=[jax.ShapeDtypeStruct(shape, jnp.bfloat16) for shape in ((n_ctx, stretch + 8, n_tok), direct)],
+        out_shape=[jax.ShapeDtypeStruct(shape, jnp.bfloat16) for shape in ((n_ctx, stretch + 8, n_tok), shared)],
         in_specs=[hbm, vmem, hbm, hbm, hbm],
         out_specs=[vmem, hbm],
         scratch_shapes=[
@@ -157,7 +161,7 @@
             pltpu.VMEM((2, block // LANES, RIM + n_tok, LANES), jnp.float32),
             pltpu.VMEM(filt.shape, jnp.float32),
             pltpu.VMEM(filt.shape[::-1], jnp.float32),
-            pltpu.VMEM(direct, jnp.bfloat16),
+            pltpu.VMEM(shared, jnp.bfloat16),
             pltpu.SemaphoreType.DMA((4 + 2 * (block // width),)),
         ],
         compiler_params=pltpu.CompilerParams(vmem_limit_bytes=56 * MIB),
@@ -168,7 +172,7 @@
     )(tokens, taps, weights, filt, w_out)
 
 
-def query_kernel(group_size, tokens, taps, weights, after, mine, other, ends, pieces, ext, wbuf, proj, sems):
+def query_kernel(group_size, tokens, taps, weights, w_out, after, mine, other, ends, direct, pieces, ext, wbuf, proj, cut, sems):
     n_tok = tokens.shape[0]
     block = wbuf.shape[1]
     n_taps, n_groups = taps.shape[0], taps.shape[1] // 3
@@ -176,13 +180,19 @@
     group0 = fft_index() * (block // group_size)
     main = pltpu.make_async_copy(tokens, ext, sems.at[0])
     load = pltpu.make_async_copy(weights.at[0], wbuf, sems.at[1])
+    rest = direct.shape[0]
+    fetch = pltpu.make_async_copy(w_out.at[pl.ds(w_out.shape[0] - rest, rest)], cut, sems.at[2])
+    store = pltpu.make_async_copy(cut, direct, sems.at[3])
     main.start()
     load.start()
+    fetch.start()
     tiles = block // LANES
     for tile in range(tiles):
         proj[tile, 0:RIM, :] = jnp.zeros((RIM, LANES), jnp.float32)
     main.wait()
     load.wait()
+    fetch.wait()
+    store.start()
     full = jnp.dot(ext[...], wbuf[...], preferred_element_type=jnp.float32)
     full = full.astype(jnp.bfloat16).astype(jnp.float32)
     for tile in range(tiles):
@@ -199,37 +209,40 @@
     chip = lax.axis_index("chip")
     mine[...] = pieces[chip]
     other[...] = pieces[chip ^ 1]
-
-
-def make_query(group_size, tokens, taps, weights, after, n_chips):
+    store.wait()
+
+
+def make_query(group_size, tokens, taps, weights, w_out, rest, after, n_chips):
     n_tok, depth = tokens.shape
     block = weights.shape[2]
     hbm = pl.BlockSpec(memory_space=pltpu.HBM)
     vmem = pl.BlockSpec(memory_space=pltpu.VMEM)
     piece = (block, n_tok // n_chips)
+    direct = (rest, w_out.shape[1])
     return pl.pallas_call(
         functools.partial(query_kernel, group_size),
-        out_shape=[jax.ShapeDtypeStruct(shape, jnp.bfloat16) for shape in (piece, piece, (16, block))],
-        in_specs=[hbm, vmem, hbm, hbm],
-        out_specs=[vmem] * 3,
+        out_shape=[jax.ShapeDtypeStruct(shape, jnp.bfloat16) for shape in (piece, piece, (16, block), direct)],
+        in_specs=[hbm, vmem, hbm, hbm, hbm],
+        out_specs=[vmem] * 3 + [hbm],
         scratch_shapes=[
             pltpu.VMEM((n_chips,) + piece, jnp.bfloat16),
             pltpu.VMEM((n_tok, depth), jnp.bfloat16),
             pltpu.VMEM((depth, block), jnp.bfloat16),
             pltpu.VMEM((block // LANES, RIM + n_tok, LANES), jnp.float32),
-            pltpu.SemaphoreType.DMA((2,)),
+            pltpu.VMEM(direct, jnp.bfloat16),
+            pltpu.SemaphoreType.DMA((4,)),
         ],
         compiler_params=pltpu.CompilerParams(vmem_limit_bytes=56 * MIB),
         cost_estimate=pl.CostEstimate(
             flops=2 * n_tok * depth * block, bytes_accessed=2 * (n_tok * depth + depth * block), transcendentals=0
         ),
         name="query",
-    )(tokens, taps, weights, after)
+    )(tokens, taps, weights, w_out, after)
 
 
 def fix_kernel(group_size, before, ends, taps, out):
     n_taps, n_groups = taps.shape[0], taps.shape[1] // 3
-    block = out.shape[0]
+    block = out.shape[1]
     group0 = fft_index() * (block // group_size)
     for tile in range(block // LANES):
         lanes = slice(tile * LANES, (tile + 1) * LANES)
@@ -238,15 +251,14 @@
             [before[:, lanes].astype(jnp.float32)[:8], ends[:, lanes].astype(jnp.float32)[8:]], axis=0
         )
         feat = filtered(coef, lambda j: both[8 - j : 16 - j, :], n_taps)
-        feat = jnp.concatenate([feat, jnp.zeros((LANES - 8, LANES), jnp.float32)], axis=0)
-        out[lanes, :] = feat.T.astype(jnp.bfloat16)
+        out[:, lanes] = jnp.concatenate([feat, jnp.zeros((8, LANES), jnp.float32)], axis=0).astype(jnp.bfloat16)
 
 
 def make_fix(group_size, before, ends, taps):
     vmem = pl.BlockSpec(memory_space=pltpu.VMEM)
     return pl.pallas_call(
         functools.partial(fix_kernel, group_size),
-        out_shape=jax.ShapeDtypeStruct((ends.shape[1], LANES), jnp.bfloat16),
+        out_shape=jax.ShapeDtypeStruct(ends.shape, jnp.bfloat16),
         in_specs=[vmem] * 3,
         out_specs=vmem,
         compiler_params=pltpu.CompilerParams(vmem_limit_bytes=16 * MIB),
@@ -427,15 +439,21 @@
             load.start()
     early = lax.broadcasted_iota(jnp.int32, (block, LANES), 1) < 8
 
+    def channels_first(fix):
+        rows = jnp.concatenate([fix[...].astype(jnp.float32), jnp.zeros((LANES - 16, block), jnp.float32)], axis=0)
+        return jnp.concatenate([rows[:, at : at + LANES].T for at in range(0, block, LANES)], axis=0)
+
+    fixes = [channels_first(fix) for fix in (fix_near, fix_far)]
+
     def gate(k, half):
-        query, fix = ((q_near, fix_near), (q_far, fix_far))[k]
+        query = (q_near, q_far)[k]
         pieces = []
         for t in range(0, n_tok, LANES):
             at = pl.ds(pl.multiple_of((core ^ half) * n_tok + t, LANES), LANES)
             values = query[:, at].astype(jnp.float32)
             if t == 0:
                 first = jnp.logical_and(early, jnp.logical_and(chip == 0, core == half))
-                values = jnp.where(first, fix[...].astype(jnp.float32), values)
+                values = jnp.where(first, fixes[k], values)
             product = values * conv[chip ^ k, :, at].astype(jnp.float32)
             pieces.append(product.T.astype(jnp.bfloat16))
         return pieces[0] if len(pieces) == 1 else jnp.concatenate(pieces, axis=0)
@@ -508,25 +526,25 @@
     piece = tok_len // n_chips
 
     weights = w_in.transpose(1, 0, 2)
-    part = block // 8 * 3
-    shared = lax.dynamic_slice_in_dim(w_out, lax.axis_index("ctx") % 2 * part, part, 0)
+    part = block // 32 * 11
+    sent, shared = mix(group_size, tokens, short_taps, weights, long_filter, w_out, part, n_ctx)
     mine = swapped(shared, "chip")
     theirs = swapped(mine, "ctx")
-    sent, direct = mix(group_size, tokens, short_taps, weights, long_filter, w_out, block - 2 * part, n_ctx)
-    direct = swapped(direct, "chip")
     payload = lax.all_to_all(sent, "ctx", 0, 0, tiled=True)
 
-    near, far, ends = make_query(group_size, tokens, short_taps, weights, sent, n_chips)
-    far = swapped(far, "chip")
+    near, far, ends, direct = make_query(
+        group_size, tokens, short_taps, weights, w_out, block - 2 * part, sent, n_chips
+    )
+    far, direct = swapped(far, "chip"), swapped(direct, "chip")
     before = passed_along(ends, "ctx", 1)
 
     gain = lax.dynamic_slice_in_dim(skip_gain, fft_index() * block + lax.axis_index("ctx") * stretch, stretch, 0)
     conv = convolve(group_size, span, stretch, payload, short_taps, arrived(gain[:, None], mine, ends), n_chips)
-    fix = make_fix(group_size, before, arrived(ends, far, conv), short_taps)
+    fix = make_fix(group_size, before, arrived(ends, conv), short_taps)
     conv = lax.all_to_all(conv.reshape(n_chips * n_ctx, stretch, piece), ("chip", "ctx"), 0, 0, tiled=True)
     conv = conv.reshape(n_chips, block, piece)
 
-    fixes = (arrived(fix, theirs, direct), swapped(fix, "chip"))
+    fixes = (arrived(fix, theirs, direct, far), swapped(fix, "chip"))
     other, staged, gated = other_part((near, far), fixes, conv, (w_out, mine, theirs, direct))
     other = swapped(other, "core")
     return (own_part(gated, staged) + other.astype(jnp.float32)).astype(jnp.bfloat16)

time: 62.5 us -> 61.1 us (0.978)
  local copies, waits for them, and re-layouts: 2.12 us -> 0.91 us
    all_to_all x1, waiting for transfers between devices: 3.83 us -> 0.73 us  [body(): lax.all_to_all(conv.reshape(n_chips * n_ctx, stretch, piece), ('chip', 'c...]
    ppermute x6, waiting for transfers between devices: 9.39 us -> 12 us  [swapped(): lax.ppermute(block, axis, [(i, i ^ 1) for i in range(lax.axis_size(axis))])]
    dynamic_slice x1 -> x0, local copies, waits for them, and re-layouts: 1.21 us -> none  [body(): lax.dynamic_slice_in_dim(w_out, lax.axis_index('ctx') % 2 * part, part, 0)]
  transfers between devices with their start and end apart: 9 -> 9, of which waited for: 4 -> 5; matrix products, arithmetic and copies ran while one was open for 0% -> 0% of each run, Pallas kernels for 29% -> 17%
where the time goes in v6:
time: 61.1 us; the launch traced here: 60.5 us
  starting transfers between devices  23 us (38%)
  Pallas kernels  21.4 us (35%)
  waiting for transfers between devices  14.2 us (23%)
  local copies, waits for them, and re-layouts  0.91 us (1%)
  other arithmetic  0.9 us (1%)
    ppermute x6, waiting for transfers between devices, swapped(): lax.ppermute(block, axis, [(i, i ^ 1) for i in range(lax.axis_size(axis))])  12 us
    ppermute x6, starting transfers between devices, swapped(): lax.ppermute(block, axis, [(i, i ^ 1) for i in range(lax.axis_size(axis))])  8.13 us
    pallas_call x1, Pallas kernels, mix(): pl.pallas_call(functools.partial(mix_kernel, group_size), out_shape=[jax....  7.67 us
    all_to_all x1, starting transfers between devices, body(): payload = lax.all_to_all(sent, 'ctx', 0, 0, tiled=True)  5.81 us
    pallas_call x1, Pallas kernels, make_query(): pl.pallas_call(functools.partial(query_kernel, group_size), out_shape=[ja...  5.72 us
    all_to_all x1, starting transfers between devices, body(): lax.all_to_all(conv.reshape(n_chips * n_ctx, stretch, piece), ('chip', 'c...  4.55 us
    ppermute x1, starting transfers between devices, passed_along(): return lax.ppermute(block, axis, route)  4.52 us
    pallas_call x1, Pallas kernels, other_part(): pl.pallas_call(other_kernel, out_shape=[jax.ShapeDtypeStruct(shape, jnp.b...  3.32 us
  transfers between devices with their start and end apart: 9, of which 5 were waited for; matrix products, arithmetic and copies ran while one was open for 0% of the time, Pallas kernels for 17%

profile of v6, /device:TPU:0, one launch (start us, length us, event | category | flops | bytes accessed | tf_op | source)
XLA Modules:
  0.0 60.5 jit_solution(4603100215564172512)
XLA Ops:
  0.0 0.0 copy-start
  0.0 7.7 %mix.1 = (bf16[8,72,512]{2,1,0:T(8,128)(2,1)}, bf16[176,2048]{1,0:T(8,128)(2,1)}) custom-call(bf16[512,2048]{1,0:T(8,128)(2,1)} %tokens.3, f32[7,384]{1,0:T(8,128)} %taps.7, bf16[3,2048,512]{2,1,0:T(8,128)(2,1)} %bitcast.6, f32[512,128]{1,0:T(8,128)} %filt.1, bf16[512,2048]{1,0:T(8,128)(2,1)} %w_near.1), custom_call_target="tpu_custom_call" | custom-call | flops 2147483648 | bytes 6291456 | tf_op jit(solution)/shard_map/mix/pallas_call | solution.py:153
  7.7 3.0 %collective-permute-start.2 = (bf16[176,2048]{1,0:T(8,128)(2,1)}, bf16[176,2048]{1,0:T(8,128)(2,1)}, u32[]{:S(2)}, u32[]{:S(2)}) collective-permute-start(bf16[176,2048]{1,0:T(8,128)(2,1)} %get-tuple-element.18), channel_id=1, source_target_pairs={{0,2},{2,0},{1,3},{3,1},{4,6},{6,4},{5,7},{7,5},{8,10},{10,8},{9,1... | collective-permute-start | bytes 2162696 | tf_op jit(solution)/shard_map/ppermute | solution.py:31
  10.7 5.8 %all-to-all-start = ((bf16[8,72,512]{2,1,0:T(8,128)(2,1)}), bf16[8,72,512]{2,1,0:T(8,128)(2,1)S(1)}, u32[]{:S(2)}, u32[]{:S(2)}) async-start(bf16[8,72,512]{2,1,0:T(8,128)(2,1)} %get-tuple-element.14.after), calls=%async_computation | async-start | bytes 1179648 | tf_op jit(solution)/shard_map/all_to_all | solution.py:533
  16.5 5.7 %query.1 = (bf16[512,256]{1,0:T(8,128)(2,1)}, bf16[512,256]{1,0:T(8,128)(2,1)}, bf16[16,512]{1,0:T(8,128)(2,1)}, bf16[160,2048]{1,0:T(8,128)(2,1)}) custom-call(bf16[512,2048]{1,0:T(8,128)(2,1)} %tokens.3, f32[7,384]{1,0:T(8,128)} %taps.7, bf16[3,2048,512]{2,1,0:T(8,128)(2,1)} %bitcast.7, bf16[512,2048]{1,0:T(8,128)(2,1)} %w_near.1, ...), custom_call_target="tpu_custom_call" | custom-call | flops 1073741824 | bytes 4194304 | tf_op jit(solution)/shard_map/query/pallas_call | solution.py:222
  22.2 4.5 %collective-permute-start.1 = (bf16[16,512]{1,0:T(8,128)(2,1)}, bf16[16,512]{1,0:T(8,128)(2,1)}, u32[]{:S(2)}, u32[]{:S(2)}) collective-permute-start(bf16[16,512]{1,0:T(8,128)(2,1)} %get-tuple-element.17.refs_1_.kept), channel_id=1, source_target_pairs={{0,4},{4,8},{8,12},{12,16},{16,20},{20,24},{24,28},{1,5},{5,9},{9,... | collective-permute-start | bytes 49160 | tf_op jit(solution)/shard_map/ppermute | solution.py:27
  26.8 0.5 collective-permute-start
  27.3 1.5 %collective-permute-start.4 = (bf16[160,2048]{1,0:T(8,128)(2,1)}, bf16[160,2048]{1,0:T(8,128)(2,1)}, u32[]{:S(2)}, u32[]{:S(2)}) collective-permute-start(bf16[160,2048]{1,0:T(8,128)(2,1)} %get-tuple-element.19), channel_id=1, source_target_pairs={{0,2},{2,0},{1,3},{3,1},{4,6},{6,4},{5,7},{7,5},{8,10},{10,8},{9,1... | collective-permute-start | bytes 1966088 | tf_op jit(solution)/shard_map/ppermute | solution.py:31
  28.8 0.0 copy-done
  28.8 0.1 dynamic-slice_bitcast_fusion
  28.9 0.1 copy.7.kept
  29.0 0.0 copy-start.3
  29.0 0.0 collective-permute-done.2.refs_0_.mine
  29.0 1.0 %collective-permute-start.3 = (bf16[176,2048]{1,0:T(8,128)(2,1)}, bf16[176,2048]{1,0:T(8,128)(2,1)}, u32[]{:S(2)}, u32[]{:S(2)}) collective-permute-start(bf16[176,2048]{1,0:T(8,128)(2,1)} %collective-permute-done.2.refs_0_.mine), channel_id=1, source_target_pairs={{0,4},{4,0},{8,12},{12,8},{16,20},{20,16},{24,28},{28,24},{1,5},{5... | collective-permute-start | bytes 2162696 | tf_op jit(solution)/shard_map/ppermute | solution.py:31
  30.0 0.0 copy-start.4
  30.0 0.7 %copy-done.4 = bf16[16,512]{1,0:T(8,128)(2,1)S(1)} copy-done((bf16[16,512]{1,0:T(8,128)(2,1)S(1)}, bf16[16,512]{1,0:T(8,128)(2,1)}, u32[]{:S(2)}) %copy-start.4) | copy-done | bytes 16408
  30.7 0.0 copy-start.5
  30.7 1.4 %all-to-all-done.payload = bf16[8,72,512]{2,1,0:T(8,128)(2,1)S(1)} async-done(((bf16[8,72,512]{2,1,0:T(8,128)(2,1)}), bf16[8,72,512]{2,1,0:T(8,128)(2,1)S(1)}, u32[]{:S(2)}, u32[]{:S(2)}) %all-to-all-start) | async-done | bytes 589856 | tf_op jit(solution)/shard_map/all_to_all | solution.py:533
  32.2 0.0 copy-done.3
  32.2 3.1 %convolve.1.refs_0_ = bf16[2,8,64,256]{3,2,1,0:T(8,128)(2,1)} custom-call(bf16[8,72,512]{2,1,0:T(8,128)(2,1)S(1)} %all-to-all-done.payload, f32[7,384]{1,0:T(8,128)S(1)} %copy-done.3, f32[64,1]{1,0:T(8,128)S(1)} %arrived.3.gain), custom_call_target="tpu_custom_call" | custom-call | flops 10000000000 | bytes 1179648 | tf_op jit(solution)/shard_map/convolve/pallas_call | solution.py:384
  35.3 0.0 copy-done.5
  35.3 4.6 %all-to-all-start.1 = ((bf16[16,64,256]{2,1,0:T(8,128)(2,1)}), bf16[16,64,256]{2,1,0:T(8,128)(2,1)S(1)}, u32[]{:S(2)}, u32[]{:S(2)}) async-start(bf16[16,64,256]{2,1,0:T(8,128)(2,1)} %bitcast.2), calls=%async_computation.1 | async-start | bytes 1048576 | tf_op jit(solution)/shard_map/all_to_all | solution.py:544
  39.8 0.0 collective-permute-done.1.before
  39.9 0.8 %fix.1.kept = bf16[16,512]{1,0:T(8,128)(2,1)S(1)} custom-call(bf16[16,512]{1,0:T(8,128)(2,1)} %collective-permute-done.1.before, bf16[16,512]{1,0:T(8,128)(2,1)S(1)} %arrived.4.ends, f32[7,384]{1,0:T(8,128)S(1)} %copy-done.3), custom_call_target="tpu_custom_call" | custom-call | flops 1000000 | bytes 100000 | tf_op jit(solution)/shard_map/fix/pallas_call | solution.py:259
  40.7 0.0 copy-start.1
  40.7 0.0 copy-start.2
  40.7 2.0 %collective-permute-start.5 = (bf16[16,512]{1,0:T(8,128)(2,1)S(1)}, bf16[16,512]{1,0:T(8,128)(2,1)S(1)}, u32[]{:S(2)}, u32[]{:S(2)}) collective-permute-start(bf16[16,512]{1,0:T(8,128)(2,1)S(1)} %fix.1.kept), channel_id=1, source_target_pairs={{0,2},{2,0},{1,3},{3,1},{4,6},{6,4},{5,7},{7,5},{8,10},{10,8},{9,1... | collective-permute-start | bytes 49160 | tf_op jit(solution)/shard_map/ppermute | solution.py:31
  42.7 0.0 collective-permute-done.refs_2_.q_far
  42.7 10.5 %collective-permute-done.4.refs_1_.direct = bf16[160,2048]{1,0:T(8,128)(2,1)} collective-permute-done((bf16[160,2048]{1,0:T(8,128)(2,1)}, bf16[160,2048]{1,0:T(8,128)(2,1)}, u32[]{:S(2)}, u32[]{:S(2)}) %collective-permute-start.4) | collective-permute-done | bytes 655392 | tf_op jit(solution)/shard_map/ppermute | solution.py:31
  53.1 0.0 collective-permute-done.3.refs_0_.theirs
  53.2 0.4 collective-permute-done.5.fix_far
  53.6 0.7 %all-to-all-done.1 = bf16[16,64,256]{2,1,0:T(8,128)(2,1)S(1)} async-done(((bf16[16,64,256]{2,1,0:T(8,128)(2,1)}), bf16[16,64,256]{2,1,0:T(8,128)(2,1)S(1)}, u32[]{:S(2)}, u32[]{:S(2)}) %all-to-all-start.1) | async-done | bytes 524320 | tf_op jit(solution)/shard_map/all_to_all | solution.py:544
  54.3 0.0 copy-done.1
  54.3 0.0 copy-done.2
  54.3 3.3 %other_part.1 = (bf16[128,2048]{1,0:T(8,128)(2,1)S(1)}, bf16[2,2,512,1024]{3,2,1,0:T(8,128)(2,1)S(1)}, bf16[2,128,512]{2,1,0:T(8,128)(2,1)S(1)}) custom-call(bf16[512,256]{1,0:T(8,128)(2,1)S(1)} %copy-done.2, bf16[512,256]{1,0:T(8,128)(2,1)} %collective-permute-done.refs_2_.q_far, bf16[16,512]{1,0:T(8,128)(2,1)S(1)} %arrived.5.fix_near, ...), custom_call_target="tpu_custom_call" | custom-call | flops 536870912 | bytes 4194304 | tf_op jit(solution)/shard_map/other_part/pallas_call | solution.py:480
  57.6 0.1 collective-permute-start.6
  57.7 0.7 %own_part.1 = f32[128,2048]{1,0:T(8,128)S(1)} custom-call(bf16[2,128,512]{2,1,0:T(8,128)(2,1)S(1)} %get-tuple-element.20.gated, bf16[2,2,512,1024]{3,2,1,0:T(8,128)(2,1)S(1)} %get-tuple-element.21.weights), custom_call_target="tpu_custom_call" | custom-call | flops 536870912 | bytes 4194304 | tf_op jit(solution)/shard_map/own_part/pallas_call | solution.py:506
  58.4 1.2 %collective-permute-done.6 = bf16[128,2048]{1,0:T(8,128)(2,1)S(1)} collective-permute-done((bf16[128,2048]{1,0:T(8,128)(2,1)S(1)}, bf16[128,2048]{1,0:T(8,128)(2,1)S(1)}, u32[]{:S(2)}, u32[]{:S(2)}) %collective-permute-start.6) | collective-permute-done | bytes 524320 | tf_op jit(solution)/shard_map/ppermute | solution.py:31
  59.6 0.9 %add_convert_fusion = bf16[128,2048]{1,0:T(8,128)(2,1)} fusion(f32[128,2048]{1,0:T(8,128)S(1)} %own_part.1, bf16[128,2048]{1,0:T(8,128)(2,1)S(1)} %collective-permute-done.6), kind=kLoop, calls=%fused_computation | loop fusion | flops 786432 | bytes 2097152 | tf_op jit(solution)/shard_map/convert_element_type | solution.py:550
  (3 shorter events, 0.0 us)
Async XLA Ops:
  0.0 28.8 %copy-start = (f32[2048]{0:T(1024)S(1)}, f32[2048]{0:T(1024)}, u32[]{:S(2)}) copy-start(f32[2048]{0:T(1024)} %param.10) | copy-start | bytes 24580
  7.7 21.3 %collective-permute-start.2 = (bf16[176,2048]{1,0:T(8,128)(2,1)}, bf16[176,2048]{1,0:T(8,128)(2,1)}, u32[]{:S(2)}, u32[]{:S(2)}) collective-permute-start(bf16[176,2048]{1,0:T(8,128)(2,1)} %get-tuple-element.18), channel_id=1, source_target_pairs={{0,2},{2,0},{1,3},{3,1},{4,6},{6,4},{5,7},{7,5},{8,10},{10,8},{9,1... | collective-permute-start | bytes 2162696 | tf_op jit(solution)/shard_map/ppermute | solution.py:31
  10.7 21.4 %all-to-all-start = ((bf16[8,72,512]{2,1,0:T(8,128)(2,1)}), bf16[8,72,512]{2,1,0:T(8,128)(2,1)S(1)}, u32[]{:S(2)}, u32[]{:S(2)}) async-start(bf16[8,72,512]{2,1,0:T(8,128)(2,1)} %get-tuple-element.14.after), calls=%async_computation | async-start | bytes 1179648 | tf_op jit(solution)/shard_map/all_to_all | solution.py:533
  22.2 17.6 %collective-permute-start.1 = (bf16[16,512]{1,0:T(8,128)(2,1)}, bf16[16,512]{1,0:T(8,128)(2,1)}, u32[]{:S(2)}, u32[]{:S(2)}) collective-permute-start(bf16[16,512]{1,0:T(8,128)(2,1)} %get-tuple-element.17.refs_1_.kept), channel_id=1, source_target_pairs={{0,4},{4,8},{8,12},{12,16},{16,20},{20,24},{24,28},{1,5},{5,9},{9,... | collective-permute-start | bytes 49160 | tf_op jit(solution)/shard_map/ppermute | solution.py:27
  26.8 15.9 %collective-permute-start = (bf16[512,256]{1,0:T(8,128)(2,1)}, bf16[512,256]{1,0:T(8,128)(2,1)}, u32[]{:S(2)}, u32[]{:S(2)}) collective-permute-start(bf16[512,256]{1,0:T(8,128)(2,1)} %get-tuple-element.16), channel_id=1, source_target_pairs={{0,2},{2,0},{1,3},{3,1},{4,6},{6,4},{5,7},{7,5},{8,10},{10,8},{9,1... | collective-permute-start | bytes 786440 | tf_op jit(solution)/shard_map/ppermute | solution.py:31
  27.3 25.8 %collective-permute-start.4 = (bf16[160,2048]{1,0:T(8,128)(2,1)}, bf16[160,2048]{1,0:T(8,128)(2,1)}, u32[]{:S(2)}, u32[]{:S(2)}) collective-permute-start(bf16[160,2048]{1,0:T(8,128)(2,1)} %get-tuple-element.19), channel_id=1, source_target_pairs={{0,2},{2,0},{1,3},{3,1},{4,6},{6,4},{5,7},{7,5},{8,10},{10,8},{9,1... | collective-permute-start | bytes 1966088 | tf_op jit(solution)/shard_map/ppermute | solution.py:31
  29.0 3.2 %copy-start.3 = (f32[7,384]{1,0:T(8,128)S(1)}, f32[7,384]{1,0:T(8,128)}, u32[]{:S(2)}) copy-start(f32[7,384]{1,0:T(8,128)} %taps.7) | copy-start | bytes 32260
  29.0 24.2 %collective-permute-start.3 = (bf16[176,2048]{1,0:T(8,128)(2,1)}, bf16[176,2048]{1,0:T(8,128)(2,1)}, u32[]{:S(2)}, u32[]{:S(2)}) collective-permute-start(bf16[176,2048]{1,0:T(8,128)(2,1)} %collective-permute-done.2.refs_0_.mine), channel_id=1, source_target_pairs={{0,4},{4,0},{8,12},{12,8},{16,20},{20,16},{24,28},{28,24},{1,5},{5... | collective-permute-start | bytes 2162696 | tf_op jit(solution)/shard_map/ppermute | solution.py:31
  30.0 0.7 %copy-start.4 = (bf16[16,512]{1,0:T(8,128)(2,1)S(1)}, bf16[16,512]{1,0:T(8,128)(2,1)}, u32[]{:S(2)}) copy-start(bf16[16,512]{1,0:T(8,128)(2,1)} %get-tuple-element.17.refs_1_.kept) | copy-start | bytes 49156
  30.7 4.6 %copy-start.5 = (bf16[16,512]{1,0:T(8,128)(2,1)S(1)}, bf16[16,512]{1,0:T(8,128)(2,1)}, u32[]{:S(2)}) copy-start(bf16[16,512]{1,0:T(8,128)(2,1)} %get-tuple-element.17.refs_1_.kept) | copy-start | bytes 49156
  35.3 19.0 %all-to-all-start.1 = ((bf16[16,64,256]{2,1,0:T(8,128)(2,1)}), bf16[16,64,256]{2,1,0:T(8,128)(2,1)S(1)}, u32[]{:S(2)}, u32[]{:S(2)}) async-start(bf16[16,64,256]{2,1,0:T(8,128)(2,1)} %bitcast.2), calls=%async_computation.1 | async-start | bytes 1048576 | tf_op jit(solution)/shard_map/all_to_all | solution.py:544
  40.7 13.6 %copy-start.1 = (bf16[512,2048]{1,0:T(8,128)(2,1)S(1)}, bf16[512,2048]{1,0:T(8,128)(2,1)}, u32[]{:S(2)}) copy-start(bf16[512,2048]{1,0:T(8,128)(2,1)} %w_near.1) | copy-start | bytes 6291460
  40.7 13.6 %copy-start.2 = (bf16[512,256]{1,0:T(8,128)(2,1)S(1)}, bf16[512,256]{1,0:T(8,128)(2,1)}, u32[]{:S(2)}) copy-start(bf16[512,256]{1,0:T(8,128)(2,1)} %get-tuple-element.15.q_near) | copy-start | bytes 786436
  40.7 12.9 %collective-permute-start.5 = (bf16[16,512]{1,0:T(8,128)(2,1)S(1)}, bf16[16,512]{1,0:T(8,128)(2,1)S(1)}, u32[]{:S(2)}, u32[]{:S(2)}) collective-permute-start(bf16[16,512]{1,0:T(8,128)(2,1)S(1)} %fix.1.kept), channel_id=1, source_target_pairs={{0,2},{2,0},{1,3},{3,1},{4,6},{6,4},{5,7},{7,5},{8,10},{10,8},{9,1... | collective-permute-start | bytes 49160 | tf_op jit(solution)/shard_map/ppermute | solution.py:31
  57.6 2.0 %collective-permute-start.6 = (bf16[128,2048]{1,0:T(8,128)(2,1)S(1)}, bf16[128,2048]{1,0:T(8,128)(2,1)S(1)}, u32[]{:S(2)}, u32[]{:S(2)}) collective-permute-start(bf16[128,2048]{1,0:T(8,128)(2,1)S(1)} %get-tuple-element.22), channel_id=1, source_target_pairs={{0,1},{1,0},{2,3},{3,2},{4,5},{5,4},{6,7},{7,6},{8,9},{9,8},{10,11... | collective-permute-start | bytes 1572872 | tf_op jit(solution)/shard_map/ppermute | solution.py:31

commit v7 on v6

--- a/solution.py
+++ b/solution.py
@@ -270,7 +270,7 @@
 def convolve_kernel(group_size, sizes, payload, taps, gain, out, lags, fixed, lagrow, held, total):
     stretch, span, rows = sizes
     n_src, _, cols = payload.shape
-    n_chips, n_ctx, _, piece = out.shape
+    n_ctx, n_chips, _, piece = out.shape
     n_taps, n_groups = taps.shape[0], taps.shape[1] // 3
     n_blocks = n_src * cols // LAG
     per_src = cols // LAG
@@ -362,7 +362,7 @@
             both = (total[g, i * rows : i * rows + span, :] + direct).astype(jnp.bfloat16)
             for h in range(pieces):
                 at = i * pieces + h
-                out[at % n_chips, at // n_chips, chans, :] = both[:, h * piece : (h + 1) * piece]
+                out[at // n_chips, at % n_chips, chans, :] = both[:, h * piece : (h + 1) * piece]
 
     prepare(0)
     for g in range(n_spans):
@@ -383,7 +383,7 @@
     vmem = pl.BlockSpec(memory_space=pltpu.VMEM)
     return pl.pallas_call(
         functools.partial(convolve_kernel, group_size, (stretch, span, rows)),
-        out_shape=jax.ShapeDtypeStruct((n_chips, n_src, stretch, cols // n_chips), jnp.bfloat16),
+        out_shape=jax.ShapeDtypeStruct((n_src, n_chips, stretch, cols // n_chips), jnp.bfloat16),
         in_specs=[vmem, vmem, vmem],
         out_specs=vmem,
         scratch_shapes=[
@@ -454,7 +454,8 @@
             if t == 0:
                 first = jnp.logical_and(early, jnp.logical_and(chip == 0, core == half))
                 values = jnp.where(first, fixes[k], values)
-            product = values * conv[chip ^ k, :, at].astype(jnp.float32)
+            source = jnp.concatenate([conv[s, chip ^ k, :, at] for s in range(conv.shape[0])], axis=0)
+            product = values * source.astype(jnp.float32)
             pieces.append(product.T.astype(jnp.bfloat16))
         return pieces[0] if len(pieces) == 1 else jnp.concatenate(pieces, axis=0)
 
@@ -470,7 +471,7 @@
 
 
 def other_part(query, fixes, conv, weights):
-    _, block, n_tok = conv.shape
+    block, n_tok = query[0].shape
     n_tok //= 2
     width = weights[0].shape[1]
     step = width // 2
@@ -541,8 +542,8 @@
     gain = lax.dynamic_slice_in_dim(skip_gain, fft_index() * block + lax.axis_index("ctx") * stretch, stretch, 0)
     conv = convolve(group_size, span, stretch, payload, short_taps, arrived(gain[:, None], mine, ends), n_chips)
     fix = make_fix(group_size, before, arrived(ends, conv), short_taps)
-    conv = lax.all_to_all(conv.reshape(n_chips * n_ctx, stretch, piece), ("chip", "ctx"), 0, 0, tiled=True)
-    conv = conv.reshape(n_chips, block, piece)
+    conv = lax.all_to_all(conv.reshape(n_ctx * n_chips, stretch, piece), ("ctx", "chip"), 0, 0, tiled=True)
+    conv = conv.reshape(n_ctx, n_chips, stretch, piece)
 
     fixes = (arrived(fix, theirs, direct, far), swapped(fix, "chip"))
     other, staged, gated = other_part((near, far), fixes, conv, (w_out, mine, theirs, direct))

time: 61.1 us -> 61.1 us (level)
  no operation moved by 1% of the time
where the time goes in v7:
time: 61.1 us; the launch traced here: 60.5 us
  starting transfers between devices  23 us (38%)
  Pallas kernels  21.3 us (35%)
  waiting for transfers between devices  14.2 us (23%)
  local copies, waits for them, and re-layouts  0.91 us (1%)
  other arithmetic  0.9 us (1%)
    ppermute x6, waiting for transfers between devices, swapped(): lax.ppermute(block, axis, [(i, i ^ 1) for i in range(lax.axis_size(axis))])  12.1 us
    ppermute x6, starting transfers between devices, swapped(): lax.ppermute(block, axis, [(i, i ^ 1) for i in range(lax.axis_size(axis))])  8.13 us
    pallas_call x1, Pallas kernels, mix(): pl.pallas_call(functools.partial(mix_kernel, group_size), out_shape=[jax....  7.67 us
    all_to_all x1, starting transfers between devices, body(): payload = lax.all_to_all(sent, 'ctx', 0, 0, tiled=True)  5.81 us
    pallas_call x1, Pallas kernels, make_query(): pl.pallas_call(functools.partial(query_kernel, group_size), out_shape=[ja...  5.72 us
    all_to_all x1, starting transfers between devices, body(): lax.all_to_all(conv.reshape(n_ctx * n_chips, stretch, piece), ('ctx', 'ch...  4.55 us
    ppermute x1, starting transfers between devices, passed_along(): return lax.ppermute(block, axis, route)  4.52 us
    pallas_call x1, Pallas kernels, other_part(): pl.pallas_call(other_kernel, out_shape=[jax.ShapeDtypeStruct(shape, jnp.b...  3.3 us
  transfers between devices with their start and end apart: 9, of which 5 were waited for; matrix products, arithmetic and copies ran while one was open for 0% of the time, Pallas kernels for 17%

profile of v7, /device:TPU:0, one launch (start us, length us, event | category | flops | bytes accessed | tf_op | source)
XLA Modules:
  0.0 60.5 jit_solution(623794396701690961)
XLA Ops:
  0.0 0.0 copy-start
  0.0 7.7 %mix.1 = (bf16[8,72,512]{2,1,0:T(8,128)(2,1)}, bf16[176,2048]{1,0:T(8,128)(2,1)}) custom-call(bf16[512,2048]{1,0:T(8,128)(2,1)} %tokens.3, f32[7,384]{1,0:T(8,128)} %taps.7, bf16[3,2048,512]{2,1,0:T(8,128)(2,1)} %bitcast.6, f32[512,128]{1,0:T(8,128)} %filt.1, bf16[512,2048]{1,0:T(8,128)(2,1)} %w_near.1), custom_call_target="tpu_custom_call" | custom-call | flops 2147483648 | bytes 6291456 | tf_op jit(solution)/shard_map/mix/pallas_call | solution.py:153
  7.7 3.0 %collective-permute-start.2 = (bf16[176,2048]{1,0:T(8,128)(2,1)}, bf16[176,2048]{1,0:T(8,128)(2,1)}, u32[]{:S(2)}, u32[]{:S(2)}) collective-permute-start(bf16[176,2048]{1,0:T(8,128)(2,1)} %get-tuple-element.18), channel_id=1, source_target_pairs={{0,2},{2,0},{1,3},{3,1},{4,6},{6,4},{5,7},{7,5},{8,10},{10,8},{9,1... | collective-permute-start | bytes 2162696 | tf_op jit(solution)/shard_map/ppermute | solution.py:31
  10.7 5.8 %all-to-all-start = ((bf16[8,72,512]{2,1,0:T(8,128)(2,1)}), bf16[8,72,512]{2,1,0:T(8,128)(2,1)S(1)}, u32[]{:S(2)}, u32[]{:S(2)}) async-start(bf16[8,72,512]{2,1,0:T(8,128)(2,1)} %get-tuple-element.14.after), calls=%async_computation | async-start | bytes 1179648 | tf_op jit(solution)/shard_map/all_to_all | solution.py:534
  16.5 5.7 %query.1 = (bf16[512,256]{1,0:T(8,128)(2,1)}, bf16[512,256]{1,0:T(8,128)(2,1)}, bf16[16,512]{1,0:T(8,128)(2,1)}, bf16[160,2048]{1,0:T(8,128)(2,1)}) custom-call(bf16[512,2048]{1,0:T(8,128)(2,1)} %tokens.3, f32[7,384]{1,0:T(8,128)} %taps.7, bf16[3,2048,512]{2,1,0:T(8,128)(2,1)} %bitcast.7, bf16[512,2048]{1,0:T(8,128)(2,1)} %w_near.1, ...), custom_call_target="tpu_custom_call" | custom-call | flops 1073741824 | bytes 4194304 | tf_op jit(solution)/shard_map/query/pallas_call | solution.py:222
  22.2 4.5 %collective-permute-start.1 = (bf16[16,512]{1,0:T(8,128)(2,1)}, bf16[16,512]{1,0:T(8,128)(2,1)}, u32[]{:S(2)}, u32[]{:S(2)}) collective-permute-start(bf16[16,512]{1,0:T(8,128)(2,1)} %get-tuple-element.17.refs_1_.kept), channel_id=1, source_target_pairs={{0,4},{4,8},{8,12},{12,16},{16,20},{20,24},{24,28},{1,5},{5,9},{9,... | collective-permute-start | bytes 49160 | tf_op jit(solution)/shard_map/ppermute | solution.py:27
  26.8 0.5 collective-permute-start
  27.3 1.5 %collective-permute-start.4 = (bf16[160,2048]{1,0:T(8,128)(2,1)}, bf16[160,2048]{1,0:T(8,128)(2,1)}, u32[]{:S(2)}, u32[]{:S(2)}) collective-permute-start(bf16[160,2048]{1,0:T(8,128)(2,1)} %get-tuple-element.19), channel_id=1, source_target_pairs={{0,2},{2,0},{1,3},{3,1},{4,6},{6,4},{5,7},{7,5},{8,10},{10,8},{9,1... | collective-permute-start | bytes 1966088 | tf_op jit(solution)/shard_map/ppermute | solution.py:31
  28.8 0.0 copy-done
  28.8 0.1 dynamic-slice_bitcast_fusion
  28.9 0.1 copy.7.kept
  29.0 0.0 copy-start.3
  29.0 0.0 collective-permute-done.2.refs_0_.mine
  29.0 1.0 %collective-permute-start.3 = (bf16[176,2048]{1,0:T(8,128)(2,1)}, bf16[176,2048]{1,0:T(8,128)(2,1)}, u32[]{:S(2)}, u32[]{:S(2)}) collective-permute-start(bf16[176,2048]{1,0:T(8,128)(2,1)} %collective-permute-done.2.refs_0_.mine), channel_id=1, source_target_pairs={{0,4},{4,0},{8,12},{12,8},{16,20},{20,16},{24,28},{28,24},{1,5},{5... | collective-permute-start | bytes 2162696 | tf_op jit(solution)/shard_map/ppermute | solution.py:31
  30.0 0.0 copy-start.4
  30.0 0.7 %copy-done.4 = bf16[16,512]{1,0:T(8,128)(2,1)S(1)} copy-done((bf16[16,512]{1,0:T(8,128)(2,1)S(1)}, bf16[16,512]{1,0:T(8,128)(2,1)}, u32[]{:S(2)}) %copy-start.4) | copy-done | bytes 16408
  30.7 0.0 copy-start.5
  30.7 1.4 %all-to-all-done.payload = bf16[8,72,512]{2,1,0:T(8,128)(2,1)S(1)} async-done(((bf16[8,72,512]{2,1,0:T(8,128)(2,1)}), bf16[8,72,512]{2,1,0:T(8,128)(2,1)S(1)}, u32[]{:S(2)}, u32[]{:S(2)}) %all-to-all-start) | async-done | bytes 589856 | tf_op jit(solution)/shard_map/all_to_all | solution.py:534
  32.2 0.0 copy-done.3
  32.2 3.1 %convolve.1.refs_0_ = bf16[8,2,64,256]{3,2,1,0:T(8,128)(2,1)} custom-call(bf16[8,72,512]{2,1,0:T(8,128)(2,1)S(1)} %all-to-all-done.payload, f32[7,384]{1,0:T(8,128)S(1)} %copy-done.3, f32[64,1]{1,0:T(8,128)S(1)} %arrived.3.gain), custom_call_target="tpu_custom_call" | custom-call | flops 10000000000 | bytes 1179648 | tf_op jit(solution)/shard_map/convolve/pallas_call | solution.py:384
  35.3 0.0 copy-done.5
  35.3 4.6 %all-to-all-start.1 = ((bf16[16,64,256]{2,1,0:T(8,128)(2,1)}), bf16[16,64,256]{2,1,0:T(8,128)(2,1)S(1)}, u32[]{:S(2)}, u32[]{:S(2)}) async-start(bf16[16,64,256]{2,1,0:T(8,128)(2,1)} %bitcast.2), calls=%async_computation.1 | async-start | bytes 1048576 | tf_op jit(solution)/shard_map/all_to_all | solution.py:545
  39.8 0.0 collective-permute-done.1.before
  39.9 0.8 %fix.1.kept = bf16[16,512]{1,0:T(8,128)(2,1)S(1)} custom-call(bf16[16,512]{1,0:T(8,128)(2,1)} %collective-permute-done.1.before, bf16[16,512]{1,0:T(8,128)(2,1)S(1)} %arrived.4.ends, f32[7,384]{1,0:T(8,128)S(1)} %copy-done.3), custom_call_target="tpu_custom_call" | custom-call | flops 1000000 | bytes 100000 | tf_op jit(solution)/shard_map/fix/pallas_call | solution.py:259
  40.7 0.0 copy-start.1
  40.7 0.0 copy-start.2
  40.7 2.0 %collective-permute-start.5 = (bf16[16,512]{1,0:T(8,128)(2,1)S(1)}, bf16[16,512]{1,0:T(8,128)(2,1)S(1)}, u32[]{:S(2)}, u32[]{:S(2)}) collective-permute-start(bf16[16,512]{1,0:T(8,128)(2,1)S(1)} %fix.1.kept), channel_id=1, source_target_pairs={{0,2},{2,0},{1,3},{3,1},{4,6},{6,4},{5,7},{7,5},{8,10},{10,8},{9,1... | collective-permute-start | bytes 49160 | tf_op jit(solution)/shard_map/ppermute | solution.py:31
  42.7 0.0 collective-permute-done.refs_2_.q_far
  42.7 10.1 %collective-permute-done.4.refs_1_.direct = bf16[160,2048]{1,0:T(8,128)(2,1)} collective-permute-done((bf16[160,2048]{1,0:T(8,128)(2,1)}, bf16[160,2048]{1,0:T(8,128)(2,1)}, u32[]{:S(2)}, u32[]{:S(2)}) %collective-permute-start.4) | collective-permute-done | bytes 655392 | tf_op jit(solution)/shard_map/ppermute | solution.py:31
  52.8 0.0 collective-permute-done.3.refs_0_.theirs
  52.8 0.8 %collective-permute-done.5.fix_far = bf16[16,512]{1,0:T(8,128)(2,1)S(1)} collective-permute-done((bf16[16,512]{1,0:T(8,128)(2,1)S(1)}, bf16[16,512]{1,0:T(8,128)(2,1)S(1)}, u32[]{:S(2)}, u32[]{:S(2)}) %collective-permute-start.5) | collective-permute-done | bytes 16416 | tf_op jit(solution)/shard_map/ppermute | solution.py:31
  53.6 0.7 %all-to-all-done.1 = bf16[16,64,256]{2,1,0:T(8,128)(2,1)S(1)} async-done(((bf16[16,64,256]{2,1,0:T(8,128)(2,1)}), bf16[16,64,256]{2,1,0:T(8,128)(2,1)S(1)}, u32[]{:S(2)}, u32[]{:S(2)}) %all-to-all-start.1) | async-done | bytes 524320 | tf_op jit(solution)/shard_map/all_to_all | solution.py:545
  54.3 0.0 copy-done.1
  54.3 0.0 copy-done.2
  54.3 3.3 %other_part.1 = (bf16[128,2048]{1,0:T(8,128)(2,1)S(1)}, bf16[2,2,512,1024]{3,2,1,0:T(8,128)(2,1)S(1)}, bf16[2,128,512]{2,1,0:T(8,128)(2,1)S(1)}) custom-call(bf16[512,256]{1,0:T(8,128)(2,1)S(1)} %copy-done.2, bf16[512,256]{1,0:T(8,128)(2,1)} %collective-permute-done.refs_2_.q_far, bf16[16,512]{1,0:T(8,128)(2,1)S(1)} %arrived.5.fix_near, ...), custom_call_target="tpu_custom_call" | custom-call | flops 536870912 | bytes 4194304 | tf_op jit(solution)/shard_map/other_part/pallas_call | solution.py:481
  57.6 0.1 collective-permute-start.6
  57.7 0.7 %own_part.1 = f32[128,2048]{1,0:T(8,128)S(1)} custom-call(bf16[2,128,512]{2,1,0:T(8,128)(2,1)S(1)} %get-tuple-element.20.gated, bf16[2,2,512,1024]{3,2,1,0:T(8,128)(2,1)S(1)} %get-tuple-element.21.weights), custom_call_target="tpu_custom_call" | custom-call | flops 536870912 | bytes 4194304 | tf_op jit(solution)/shard_map/own_part/pallas_call | solution.py:507
  58.4 1.2 %collective-permute-done.6 = bf16[128,2048]{1,0:T(8,128)(2,1)S(1)} collective-permute-done((bf16[128,2048]{1,0:T(8,128)(2,1)S(1)}, bf16[128,2048]{1,0:T(8,128)(2,1)S(1)}, u32[]{:S(2)}, u32[]{:S(2)}) %collective-permute-start.6) | collective-permute-done | bytes 524320 | tf_op jit(solution)/shard_map/ppermute | solution.py:31
  59.6 0.9 %add_convert_fusion = bf16[128,2048]{1,0:T(8,128)(2,1)} fusion(f32[128,2048]{1,0:T(8,128)S(1)} %own_part.1, bf16[128,2048]{1,0:T(8,128)(2,1)S(1)} %collective-permute-done.6), kind=kLoop, calls=%fused_computation | loop fusion | flops 786432 | bytes 2097152 | tf_op jit(solution)/shard_map/convert_element_type | solution.py:551
  (3 shorter events, 0.0 us)
Async XLA Ops:
  0.0 28.8 %copy-start = (f32[2048]{0:T(1024)S(1)}, f32[2048]{0:T(1024)}, u32[]{:S(2)}) copy-start(f32[2048]{0:T(1024)} %param.10) | copy-start | bytes 24580
  7.7 21.3 %collective-permute-start.2 = (bf16[176,2048]{1,0:T(8,128)(2,1)}, bf16[176,2048]{1,0:T(8,128)(2,1)}, u32[]{:S(2)}, u32[]{:S(2)}) collective-permute-start(bf16[176,2048]{1,0:T(8,128)(2,1)} %get-tuple-element.18), channel_id=1, source_target_pairs={{0,2},{2,0},{1,3},{3,1},{4,6},{6,4},{5,7},{7,5},{8,10},{10,8},{9,1... | collective-permute-start | bytes 2162696 | tf_op jit(solution)/shard_map/ppermute | solution.py:31
  10.7 21.4 %all-to-all-start = ((bf16[8,72,512]{2,1,0:T(8,128)(2,1)}), bf16[8,72,512]{2,1,0:T(8,128)(2,1)S(1)}, u32[]{:S(2)}, u32[]{:S(2)}) async-start(bf16[8,72,512]{2,1,0:T(8,128)(2,1)} %get-tuple-element.14.after), calls=%async_computation | async-start | bytes 1179648 | tf_op jit(solution)/shard_map/all_to_all | solution.py:534
  22.2 17.6 %collective-permute-start.1 = (bf16[16,512]{1,0:T(8,128)(2,1)}, bf16[16,512]{1,0:T(8,128)(2,1)}, u32[]{:S(2)}, u32[]{:S(2)}) collective-permute-start(bf16[16,512]{1,0:T(8,128)(2,1)} %get-tuple-element.17.refs_1_.kept), channel_id=1, source_target_pairs={{0,4},{4,8},{8,12},{12,16},{16,20},{20,24},{24,28},{1,5},{5,9},{9,... | collective-permute-start | bytes 49160 | tf_op jit(solution)/shard_map/ppermute | solution.py:27
  26.8 15.9 %collective-permute-start = (bf16[512,256]{1,0:T(8,128)(2,1)}, bf16[512,256]{1,0:T(8,128)(2,1)}, u32[]{:S(2)}, u32[]{:S(2)}) collective-permute-start(bf16[512,256]{1,0:T(8,128)(2,1)} %get-tuple-element.16), channel_id=1, source_target_pairs={{0,2},{2,0},{1,3},{3,1},{4,6},{6,4},{5,7},{7,5},{8,10},{10,8},{9,1... | collective-permute-start | bytes 786440 | tf_op jit(solution)/shard_map/ppermute | solution.py:31
  27.3 25.5 %collective-permute-start.4 = (bf16[160,2048]{1,0:T(8,128)(2,1)}, bf16[160,2048]{1,0:T(8,128)(2,1)}, u32[]{:S(2)}, u32[]{:S(2)}) collective-permute-start(bf16[160,2048]{1,0:T(8,128)(2,1)} %get-tuple-element.19), channel_id=1, source_target_pairs={{0,2},{2,0},{1,3},{3,1},{4,6},{6,4},{5,7},{7,5},{8,10},{10,8},{9,1... | collective-permute-start | bytes 1966088 | tf_op jit(solution)/shard_map/ppermute | solution.py:31
  29.0 3.2 %copy-start.3 = (f32[7,384]{1,0:T(8,128)S(1)}, f32[7,384]{1,0:T(8,128)}, u32[]{:S(2)}) copy-start(f32[7,384]{1,0:T(8,128)} %taps.7) | copy-start | bytes 32260
  29.0 23.8 %collective-permute-start.3 = (bf16[176,2048]{1,0:T(8,128)(2,1)}, bf16[176,2048]{1,0:T(8,128)(2,1)}, u32[]{:S(2)}, u32[]{:S(2)}) collective-permute-start(bf16[176,2048]{1,0:T(8,128)(2,1)} %collective-permute-done.2.refs_0_.mine), channel_id=1, source_target_pairs={{0,4},{4,0},{8,12},{12,8},{16,20},{20,16},{24,28},{28,24},{1,5},{5... | collective-permute-start | bytes 2162696 | tf_op jit(solution)/shard_map/ppermute | solution.py:31
  30.0 0.7 %copy-start.4 = (bf16[16,512]{1,0:T(8,128)(2,1)S(1)}, bf16[16,512]{1,0:T(8,128)(2,1)}, u32[]{:S(2)}) copy-start(bf16[16,512]{1,0:T(8,128)(2,1)} %get-tuple-element.17.refs_1_.kept) | copy-start | bytes 49156
  30.7 4.6 %copy-start.5 = (bf16[16,512]{1,0:T(8,128)(2,1)S(1)}, bf16[16,512]{1,0:T(8,128)(2,1)}, u32[]{:S(2)}) copy-start(bf16[16,512]{1,0:T(8,128)(2,1)} %get-tuple-element.17.refs_1_.kept) | copy-start | bytes 49156
  35.3 19.0 %all-to-all-start.1 = ((bf16[16,64,256]{2,1,0:T(8,128)(2,1)}), bf16[16,64,256]{2,1,0:T(8,128)(2,1)S(1)}, u32[]{:S(2)}, u32[]{:S(2)}) async-start(bf16[16,64,256]{2,1,0:T(8,128)(2,1)} %bitcast.2), calls=%async_computation.1 | async-start | bytes 1048576 | tf_op jit(solution)/shard_map/all_to_all | solution.py:545
  40.7 13.6 %copy-start.1 = (bf16[512,2048]{1,0:T(8,128)(2,1)S(1)}, bf16[512,2048]{1,0:T(8,128)(2,1)}, u32[]{:S(2)}) copy-start(bf16[512,2048]{1,0:T(8,128)(2,1)} %w_near.1) | copy-start | bytes 6291460
  40.7 13.6 %copy-start.2 = (bf16[512,256]{1,0:T(8,128)(2,1)S(1)}, bf16[512,256]{1,0:T(8,128)(2,1)}, u32[]{:S(2)}) copy-start(bf16[512,256]{1,0:T(8,128)(2,1)} %get-tuple-element.15.q_near) | copy-start | bytes 786436
  40.7 12.9 %collective-permute-start.5 = (bf16[16,512]{1,0:T(8,128)(2,1)S(1)}, bf16[16,512]{1,0:T(8,128)(2,1)S(1)}, u32[]{:S(2)}, u32[]{:S(2)}) collective-permute-start(bf16[16,512]{1,0:T(8,128)(2,1)S(1)} %fix.1.kept), channel_id=1, source_target_pairs={{0,2},{2,0},{1,3},{3,1},{4,6},{6,4},{5,7},{7,5},{8,10},{10,8},{9,1... | collective-permute-start | bytes 49160 | tf_op jit(solution)/shard_map/ppermute | solution.py:31
  57.6 2.0 %collective-permute-start.6 = (bf16[128,2048]{1,0:T(8,128)(2,1)S(1)}, bf16[128,2048]{1,0:T(8,128)(2,1)S(1)}, u32[]{:S(2)}, u32[]{:S(2)}) collective-permute-start(bf16[128,2048]{1,0:T(8,128)(2,1)S(1)} %get-tuple-element.22), channel_id=1, source_target_pairs={{0,1},{1,0},{2,3},{3,2},{4,5},{5,4},{6,7},{7,6},{8,9},{9,8},{10,11... | collective-permute-start | bytes 1572872 | tf_op jit(solution)/shard_map/ppermute | solution.py:31
